TPU v7x, 128 devices: a whole 4x4x4 slice. The times are simulated.
128 devices in a mesh: dp: 16 (over y_lo, x, core), tensor: 8 (over y_hi, z).
Axes of the slice: x: 4, y: 4 (y_hi: 2, y_lo: 2; y = y_hi * 2 + y_lo), z: 4, core: 2. Of those that a mesh axis runs over, the one named last changes fastest.
Arguments:
- tokens: bfloat16 [32768, 1536], P(('dp', 'tensor')), may hold values from -6 to 6
- norm_gain: float32 [1536], replicated, may hold values from 0.5 to 1.5
- w_gate: bfloat16 [1536, 3072], P('dp', 'tensor'), may hold values from -0.15625 to 0.15625
- w_inner: bfloat16 [1536, 3072], P('dp', 'tensor'), may hold values from -0.15625 to 0.15625
- w_bc: bfloat16 [1536, 256], P('dp'), may hold values from -0.15625 to 0.15625
- w_step: bfloat16 [1536, 48], P('dp', 'tensor'), may hold values from -0.15625 to 0.15625
- conv_inner: float32 [4, 3072], P(None, 'tensor'), may hold values from -3 to 3
- bias_inner: float32 [3072], P('tensor'), may hold values from -3 to 3
- conv_bc: float32 [4, 256], replicated, may hold values from -3 to 3
- bias_bc: float32 [256], replicated, may hold values from -3 to 3
- step_bias: float32 [48], P('tensor'), may hold values from -5 to -1
- decay_log: float32 [48], P('tensor'), may hold values from -2 to 2.5
- skip_gain: float32 [48], P('tensor'), may hold values from 0.5 to 1.5
- gate_gain: float32 [3072], P('tensor'), may hold values from 0.5 to 1.5
- w_out: bfloat16 [1536, 3072], P('dp', 'tensor'), may hold values from -0.109375 to 0.109375
- cotangent: bfloat16 [32768, 1536], P(('dp', 'tensor')), may hold values from -6 to 6
Outputs:
- output: bfloat16 [32768, 1536], P(('dp', 'tensor'))
- tokens_grad: float32 [32768, 1536], P(('dp', 'tensor'))
- norm_gain_grad: float32 [1536], replicated
- w_gate_grad: float32 [1536, 3072], P('dp', 'tensor')
- w_inner_grad: float32 [1536, 3072], P('dp', 'tensor')
- w_bc_grad: float32 [1536, 256], P('dp')
- w_step_grad: float32 [1536, 48], P('dp', 'tensor')
- conv_inner_grad: float32 [4, 3072], P(None, 'tensor')
- bias_inner_grad: float32 [3072], P('tensor')
- conv_bc_grad: float32 [4, 256], replicated
- bias_bc_grad: float32 [256], replicated
- step_bias_grad: float32 [48], P('tensor')
- decay_log_grad: float32 [48], P('tensor')
- skip_gain_grad: float32 [48], P('tensor')
- gate_gain_grad: float32 [3072], P('tensor')
- w_out_grad: float32 [1536, 3072], P('dp', 'tensor')
All inputs are finite; a program needn't handle non-finite values.
Results may differ from a plain program's by a relative error of at most 0.012.
Values may be sent and summed in bfloat16 or wider, within the bound.
A program may use at most 192 MiB of HBM per device.

v0:
```python
import jax
import jax.numpy as jnp
from jax import lax
from jax.sharding import PartitionSpec as P

HEAD_DIM = 64
STATE = 128
BLOCK = 256
LEN = 1024
INNER = 3072


epsilon = 1e-05
highest = lax.Precision.HIGHEST


def causal_conv(values, weight, shift_bias):
    kernel_taps = weight.shape[0]
    padded = jnp.pad(values, ((0, 0), (kernel_taps - 1, 0), (0, 0)))
    summed = jnp.zeros_like(values) + shift_bias
    for offset in range(kernel_taps):
        summed = summed + weight[offset] * padded[:, offset : offset + values.shape[1], :]
    return jax.nn.silu(summed)


def block_scan(inputs, b_proj, c_proj, step_sizes, decay_rate, skip_gain):
    length, head_count, head_width = inputs.shape
    blocks = length // BLOCK
    step_logs = (step_sizes * decay_rate).reshape(blocks, BLOCK, head_count).transpose(0, 2, 1)
    running = jnp.cumsum(step_logs, axis=2)
    weighted = (inputs * step_sizes[:, :, None]).reshape(blocks, BLOCK, head_count, head_width)
    b_block = b_proj.reshape(blocks, BLOCK, -1)
    c_block = c_proj.reshape(blocks, BLOCK, -1)
    scores = jnp.einsum("ktn,ksn->kts", c_block, b_block, precision=highest)
    causal = jnp.arange(BLOCK)[:, None] >= jnp.arange(BLOCK)[None, :]
    log_gaps = running[:, :, :, None] - running[:, :, None, :]
    decays = jnp.where(causal, jnp.exp(jnp.where(causal, log_gaps, 0.0)), 0.0)
    mixing = decays * scores[:, None, :, :]
    within = jnp.einsum("khts,kshp->kthp", mixing, weighted, precision=highest)
    to_end = jnp.exp(running[:, :, -1:] - running)
    states = jnp.einsum("khs,kshp,ksn->khpn", to_end, weighted, b_block, precision=highest)
    factors = jnp.exp(running[:, :, -1])

    def carry_step(carried, block_in):
        block_state, factor = block_in
        return (carried * factor[:, None, None] + block_state, carried)

    start_state = jnp.zeros((head_count, head_width, b_proj.shape[1]), jnp.float32)
    _, entering = lax.scan(carry_step, start_state, (states, factors))
    across = jnp.einsum(
        "ktn,khpn,kht->kthp", c_block, entering, jnp.exp(running), precision=highest
    )
    result = (
        within
        + across
        + skip_gain[None, None, :, None] * inputs.reshape(blocks, BLOCK, head_count, head_width)
    )
    return result.reshape(length, head_count, head_width)


def local_mixer(
    inner_in, step_in, conv_inner, bias_inner, step_bias, decay_log, skip_gain, b_proj, c_proj
):
    sequences = inner_in.shape[0] // LEN
    head_count = step_in.shape[1]
    inner_conv = causal_conv(inner_in.reshape(sequences, LEN, -1), conv_inner, bias_inner)
    step_sizes = jax.nn.softplus(step_in.reshape(sequences, LEN, head_count) + step_bias)
    decay_rate = -jnp.exp(decay_log)
    scanned = jax.vmap(block_scan, in_axes=(0, 0, 0, 0, None, None))(
        inner_conv.reshape(sequences, LEN, head_count, HEAD_DIM),
        b_proj,
        c_proj,
        step_sizes,
        decay_rate,
        skip_gain,
    )
    return scanned.reshape(inner_in.shape[0], -1)


def bc_branch(bc_in, conv_bc, bias_bc):
    sequences = bc_in.shape[0] // LEN
    bc_conv = causal_conv(bc_in.reshape(sequences, LEN, -1), conv_bc, bias_bc)
    return (bc_conv[:, :, :STATE], bc_conv[:, :, STATE:])


def shards(
    tokens,
    norm_gain,
    w_gate,
    w_inner,
    w_bc,
    w_step,
    conv_inner,
    bias_inner,
    conv_bc,
    bias_bc,
    step_bias,
    decay_log,
    skip_gain,
    gate_gain,
    w_out,
    cotangent,
):
    local_rows = tokens.shape[0]
    residual = tokens.astype(jnp.float32)
    inv_root = lax.rsqrt(jnp.mean(residual * residual, axis=1, keepdims=True) + epsilon)
    normed = (residual * inv_root * norm_gain).astype(jnp.bfloat16)
    fwd_gate, fwd_inner, fwd_bc, fwd_step, fwd_out = (
        lax.all_gather(w_gate, "dp", axis=0, tiled=True),
        lax.all_gather(w_inner, "dp", axis=0, tiled=True),
        lax.all_gather(w_bc, "dp", axis=0, tiled=True),
        lax.all_gather(w_step, "dp", axis=0, tiled=True),
        lax.all_gather(w_out, "dp", axis=0, tiled=True),
    )
    inner_cols = fwd_gate.shape[1]
    head_cols = 2 * inner_cols + fwd_step.shape[1]
    fwd_cat = jnp.concatenate([fwd_gate, fwd_inner, fwd_step, fwd_bc], axis=1)
    normed_all = lax.all_gather(normed, "tensor", axis=0, tiled=True)
    projected = jnp.dot(normed_all, fwd_cat, preferred_element_type=jnp.float32)
    gate_in = projected[:, :inner_cols]
    inner_in = projected[:, inner_cols : 2 * inner_cols]
    step_in = projected[:, 2 * inner_cols : head_cols]
    bc_in = projected[:, head_cols:]
    (b_proj, c_proj), bc_back = jax.vjp(bc_branch, bc_in, conv_bc, bias_bc)
    scanned, mixer_back = jax.vjp(
        local_mixer,
        inner_in,
        step_in,
        conv_inner,
        bias_inner,
        step_bias,
        decay_log,
        skip_gain,
        b_proj,
        c_proj,
    )
    gate_sig = jax.nn.sigmoid(gate_in)
    gate_act = gate_in * gate_sig
    gate_prod = scanned * gate_act
    square_sum = lax.psum(jnp.sum(gate_prod * gate_prod, axis=1), "tensor")
    inner_root = lax.rsqrt(square_sum / INNER + epsilon)[:, None]
    mixed_out = (gate_prod * inner_root * gate_gain).astype(jnp.bfloat16)
    row_block = mixed_out
    branch_sum = lax.psum_scatter(
        jnp.einsum("ri,di->rd", row_block, fwd_out, preferred_element_type=jnp.float32).astype(
            jnp.bfloat16
        ),
        "tensor",
        scatter_dimension=0,
        tiled=True,
    ).astype(jnp.float32)
    output = (residual + branch_sum).astype(jnp.bfloat16)
    back_gate, back_inner, back_bc, back_step, back_out = (
        lax.all_gather(w_gate, "dp", axis=0, tiled=True),
        lax.all_gather(w_inner, "dp", axis=0, tiled=True),
        lax.all_gather(w_bc, "dp", axis=0, tiled=True),
        lax.all_gather(w_step, "dp", axis=0, tiled=True),
        lax.all_gather(w_out, "dp", axis=0, tiled=True),
    )
    back_heads = jnp.concatenate([back_gate, back_inner, back_step], axis=1)
    cot_all = lax.all_gather(cotangent, "tensor", axis=0, tiled=True)
    grad_out = jnp.einsum("rd,ri->di", cot_all, mixed_out, preferred_element_type=jnp.float32)
    grad_mixed = jnp.dot(cot_all, back_out, preferred_element_type=jnp.float32)
    scaled_grad = grad_mixed * gate_gain
    cross_sum = lax.psum(jnp.sum(scaled_grad * gate_prod, axis=1), "tensor")
    grad_gate_gain = jnp.sum(grad_mixed * gate_prod * inner_root, axis=0)
    grad_gated = (
        inner_root * scaled_grad
        - gate_prod * (inner_root * inner_root * inner_root) * (cross_sum / INNER)[:, None]
    )
    grad_scanned = grad_gated * gate_act
    grad_gate_in = grad_gated * scanned * gate_sig * (1.0 + gate_in * (1.0 - gate_sig))
    (
        grad_inner_in,
        grad_step_in,
        grad_conv_inner,
        grad_bias_inner,
        grad_step_bias,
        grad_decay_log,
        grad_skip,
        grad_b_part,
        grad_c_part,
    ) = mixer_back(grad_scanned)
    grad_b_proj, grad_c_proj = lax.psum((grad_b_part, grad_c_part), "tensor")
    grad_bc_in, grad_conv_bc, grad_bias_bc = bc_back((grad_b_proj, grad_c_proj))
    grad_heads = jnp.concatenate([grad_gate_in, grad_inner_in, grad_step_in], axis=1).astype(
        jnp.bfloat16
    )
    grad_bc_low = grad_bc_in.astype(jnp.bfloat16)
    grad_heads_w = jnp.einsum(
        "rd,rc->dc", normed_all, grad_heads, preferred_element_type=jnp.float32
    )
    grad_bc_w = jnp.einsum("rd,rc->dc", normed_all, grad_bc_low, preferred_element_type=jnp.float32)
    row_block = grad_heads
    grad_normed = lax.psum_scatter(
        jnp.einsum("rc,dc->rd", row_block, back_heads, preferred_element_type=jnp.float32).astype(
            jnp.bfloat16
        ),
        "tensor",
        scatter_dimension=0,
        tiled=True,
    ).astype(jnp.float32)
    own_bc = lax.dynamic_slice_in_dim(
        grad_bc_low, lax.axis_index("tensor") * local_rows, local_rows, 0
    )
    grad_normed = grad_normed + jnp.einsum(
        "rc,dc->rd", own_bc, back_bc, preferred_element_type=jnp.float32
    )
    scaled_input = grad_normed * norm_gain
    grad_norm_part = jnp.sum(grad_normed * residual * inv_root, axis=0)
    tokens_grad = (
        cotangent.astype(jnp.float32)
        + inv_root * scaled_input
        - residual
        * (inv_root * inv_root * inv_root)
        * jnp.mean(scaled_input * residual, axis=1, keepdims=True)
    )
    gate_sum, inner_sum, bc_sum, step_sum, out_sum = (
        lax.psum_scatter(grad_heads_w[:, :inner_cols], "dp", scatter_dimension=0, tiled=True),
        lax.psum_scatter(
            grad_heads_w[:, inner_cols : 2 * inner_cols], "dp", scatter_dimension=0, tiled=True
        ),
        lax.psum_scatter(grad_bc_w, "dp", scatter_dimension=0, tiled=True),
        lax.psum_scatter(grad_heads_w[:, 2 * inner_cols :], "dp", scatter_dimension=0, tiled=True),
        lax.psum_scatter(grad_out, "dp", scatter_dimension=0, tiled=True),
    )
    (
        conv_inner_sum,
        bias_inner_sum,
        conv_bc_sum,
        bias_bc_sum,
        step_bias_sum,
        decay_sum,
        skip_sum,
        gate_gain_sum,
    ) = lax.psum(
        (
            grad_conv_inner,
            grad_bias_inner,
            grad_conv_bc,
            grad_bias_bc,
            grad_step_bias,
            grad_decay_log,
            grad_skip,
            grad_gate_gain,
        ),
        "dp",
    )
    norm_gain_sum = lax.psum(grad_norm_part, ("dp", "tensor"))
    return (
        output,
        tokens_grad,
        norm_gain_sum,
        gate_sum,
        inner_sum,
        bc_sum,
        step_sum,
        conv_inner_sum,
        bias_inner_sum,
        conv_bc_sum,
        bias_bc_sum,
        step_bias_sum,
        decay_sum,
        skip_sum,
        gate_gain_sum,
        out_sum,
    )


def solution(mesh):
    placed = (
        P(("dp", "tensor"), None),
        P(),
        P("dp", "tensor"),
        P("dp", "tensor"),
        P("dp", None),
        P("dp", "tensor"),
        P(None, "tensor"),
        P("tensor"),
        P(),
        P(),
        P("tensor"),
        P("tensor"),
        P("tensor"),
        P("tensor"),
        P("dp", "tensor"),
        P(("dp", "tensor"), None),
    )
    return jax.shard_map(
        shards,
        mesh=mesh,
        in_specs=placed,
        out_specs=(
            P(("dp", "tensor"), None),
            P(("dp", "tensor"), None),
            P(),
            P("dp", "tensor"),
            P("dp", "tensor"),
            P("dp", None),
            P("dp", "tensor"),
            P(None, "tensor"),
            P("tensor"),
            P(),
            P(),
            P("tensor"),
            P("tensor"),
            P("tensor"),
            P("tensor"),
            P("dp", "tensor"),
        ),
        check_vma=False,
    )
```

profile of v0, /device:TPU:0, one launch (start us, length us, event | category | flops | bytes accessed | tf_op | source)
XLA Modules:
  0.0 1136.1 jit_solution(18441711831389464051)
XLA Ops:
  15.5 22.0 %all_gather.30 = bf16[1536,256]{1,0:T(8,128)(2,1)S(1)} all-gather(bf16[96,256]{1,0:T(8,128)(2,1)S(1)} %copy-done.51), channel_id=1, replica_groups=mesh['dp'=16,'tensor'=8] {'dp'}, dimensions={0}, use_global_device_ids=true | all-gather | bytes 835584 | tf_op jit(solution)/shard_map/all_gather | solution.py:111
  37.4 16.3 %all-gather = bf16[16,96,6]{1,2,0:T(8,128)(2,1)S(1)} all-gather(bf16[1,96,6]{1,2,0:T(8,128)(2,1)S(1)} %bitcast.278), channel_id=1, replica_groups=mesh['dp'=16,'tensor'=8] {'dp'}, dimensions={0}, use_global_device_ids=true | all-gather | bytes 19584 | tf_op jit(solution)/shard_map/all_gather | solution.py:112
  56.0 24.6 %all-gather.11.cloned.1.call-done = bf16[1536,384]{1,0:T(8,128)(2,1)} async-done(((bf16[96,384]{1,0:T(8,128)(2,1)}), bf16[1536,384]{1,0:T(8,128)(2,1)}) %all-gather.11.cloned.1.call-update) | async-done | bytes 1179664 | tf_op jit(solution)/shard_map/all_gather | solution.py:110
  80.6 6.2 concatenate.10
  86.8 85.8 %all-gather.7.cloned.1.call-done = bf16[2048,1536]{1,0:T(8,128)(2,1)} async-done(((bf16[256,1536]{1,0:T(8,128)(2,1)}), bf16[2048,1536]{1,0:T(8,128)(2,1)}) %all-gather.7.cloned.1.call-update) | async-done | bytes 6291472 | tf_op jit(solution)/shard_map/all_gather | solution.py:118
  172.7 10.0 fusion.137
  187.2 4.5 reshape.285
  192.4 4.4 fusion.129
  198.4 2.5 fusion.33
  200.9 3.5 reshape.281
  210.3 25.5 %reduce-window.14 = f32[2,4,6,2,128]{4,3,2,1,0:T(2,128)} reduce-window(f32[2,4,6,2,128]{4,3,2,1,0:T(2,128)} %copy.297, f32[]{:T(128)} %constant.103.clone.1), window={size=1x1x1x1x128 pad=0_0x0_0x0_0x0_0x127_0}, to_apply=%region_1.2 | reduce-window | flops 1560576 | bytes 98308 | tf_op jit(solution)/shard_map/reduce-window
  245.8 12.3 %fusion.128 = (f32[2,1024,256]{1,0,2:T(2,128)S(1)}, f32[2,1024,256]{1,0,2:T(2,128)}) fusion(f32[2,1024,256]{1,0,2:T(2,128)} %reshape.285, f32[256]{0:T(256)} %bitcast.270, f32[256]{0:T(256)} %bitcast.272, f32[256]{0:T(256)S(1)} %bitcast.268, f32[256]{0:T(256)S(1)} %bitcast.266, f32[256]{0:T(256)} %param.29), kind=kLoop, calls=%fused_computation.215 | loop fusion | flops 6291456 | bytes 6296576 | tf_op jit(solution)/shard_map/jvp(jit(silu))/mul | solution.py:23
  260.2 2.6 copy.303
  262.8 4.1 copy.442
  270.7 4.7 fusion.138
  275.4 4.3 fusion.77
  281.2 16.3 %while.34 = (s32[]{:T(128)}, f32[2,6,64,128]{3,2,1,0:T(8,128)}, f32[4,2,6,64,128]{4,3,2,1,0:T(8,128)}, f32[4,2,6,1,1]{2,1,4,3,0:T(2,128)}, f32[4,2,6]{2,0,1:T(4,...) while((s32[]{:T(128)}, f32[2,6,64,128]{3,2,1,0:T(8,128)}, ...), condition=%wide.region_4.5_spmd.clone, body=%wide.region_3.4_spmd.clone.sunk | while | flops 393219 | bytes 1967416 | solution.py:49
  297.5 4.7 fusion.87
  302.3 14.8 %fusion.31 = f32[2,4,256,6,64]{2,4,3,1,0:T(8,128)S(1)} fusion(f32[2,4,6,64,256]{4,3,2,1,0:T(8,128)S(1)} %fusion.87, f32[2,4,256,6,64]{2,1,4,3,0:T(4,128)S(1)} %reshape.281, f32[2,4,256,256]{3,2,1,0:T(8,128)S(1)} %copy-done.24, f32[2,4,6,256]{3,2,1,0:T(8,128)S(1)} %copy-done.47, pred[256,256]{1,0:T(8,128)(4,1)S(1)} %copy-done.44, f32[6]{0:T(128)S(1)} %copy-done.87, ...), kind=kOutput, calls=%fused_computation.61 | convolution fusion | flops 2432434176 | bytes 11747352 | tf_op jit(solution)/shard_map/jvp(vmap(khts,kshp->kthp))/dot_general | solution.py:39
  317.1 3.7 copy.312
  320.8 5.2 reshape.288
  326.0 5.6 multiply_reduce_fusion.11
  331.6 20.5 %psum.91 = f32[2048]{0:T(1024)} all-reduce(f32[2048]{0:T(1024)S(1)} %get-tuple-element.477), channel_id=1, replica_groups=mesh['dp'=16,'tensor'=8] {'tensor'}, use_global_device_ids=true, to_apply=%region_6.7 | all-reduce | flops 2048 | bytes 16384 | tf_op jit(solution)/shard_map/psum | solution.py:140
  353.4 9.4 multiply_reduce_fusion.3
  362.7 21.6 %psum.92 = f32[2048]{0:T(1024)} all-reduce(f32[2048]{0:T(1024)} %get-tuple-element.418), channel_id=1, replica_groups=mesh['dp'=16,'tensor'=8] {'tensor'}, use_global_device_ids=true, to_apply=%region_9.10 | all-reduce | flops 2048 | bytes 16384 | tf_op jit(solution)/shard_map/psum | solution.py:165
  385.0 9.3 multiply_reduce_fusion.4
  394.3 5.3 reshape.290
  399.6 7.1 fusion.80
  406.7 19.6 %fusion.8 = (f32[2,4,6,256]{3,2,1,0:T(8,128)}, f32[2,4,6,256]{3,2,1,0:T(8,128)}, f32[2,4,256,256]{3,2,1,0:T(8,128)}) fusion(f32[2,4,256,256]{3,2,1,0:T(8,128)S(1)} %copy-done.25, f32[2,4,6,256]{3,2,1,0:T(8,128)S(1)} %copy-done.48, pred[256,256]{1,0:T(8,128)(4,1)S(1)} %copy-done.45, f32[2,4,256,6,64]{2,1,4,3,0:T(4,128)S(1)} %reshape.281, ...), kind=kOutput, calls=%fused_computation.19 | convolution fusion | flops 2450759680 | bytes 10747904 | tf_op jit(solution)/shard_map/transpose(jvp(vmap(khts,kshp->kthp)))/dot_general | solution.py:39
  426.3 6.8 fusion.94
  435.0 16.4 %while.35 = (s32[]{:T(128)}, f32[2,6,64,128]{3,2,1,0:T(8,128)S(1)}, f32[4,2,6,64,128]{4,3,2,1,0:T(8,128)}, f32[4,2,6]{2,0,1:T(4,128)}, f32[4,2,6,64,128]{4,3,2,0...) while((s32[]{:T(128)}, f32[2,6,64,128]{3,2,1,0:T(8,128)S(1)}, ...), condition=%wide.region_12.13_spmd.clone, body=%wide.region_10.12_spmd.clone.sunk | while | flops 589816 | bytes 2359732 | solution.py:49
  451.4 8.0 fusion.89
  459.4 5.5 multiply_reduce_fusion.1
  465.0 7.2 convolution_add_fusion.1
  474.5 4.2 convolution_add_fusion.2
  480.9 3.7 pad_add_fusion.6
  484.8 13.0 %bitcast_add_fusion.2 = f32[2,4,256,6,64]{2,4,3,1,0:T(8,128)S(1)} fusion(f32[2,4,256,6,64]{2,4,3,1,0:T(8,128)} %get-tuple-element.513, f32[2,4,256,256]{3,2,1,0:T(8,128)} %fusion.138, f32[2,4,6,256]{3,2,1,0:T(8,128)S(1)} %copy-done.49, pred[256,256]{1,0:T(8,128)(4,1)S(1)} %copy-done.46, f32[2,4,256,6,64]{2,1,0,4,3:T(4,128)S(1)} %copy-done.1, ...), kind=kOutput, calls=%fused_computation.51 | convolution fusion | flops 2430074880 | bytes 11698176 | tf_op jit(solution)/shard_map/transpose(jvp(vmap(khts,kshp->kthp)))/dot_general | solution.py:39
  497.8 3.7 copy.319
  508.4 60.4 %reduce-window.16 = f32[2,4,6,2,128]{4,3,2,1,0:T(2,128)S(1)} reduce-window(f32[2,4,6,2,128]{4,3,2,1,0:T(2,128)S(1)} %reshape.315, f32[]{:T(128)} %constant.103.clone.1), window={size=1x1x1x1x128 pad=0_0x0_0x0_0x0_0x0_127}, to_apply=%region_17.18 | reduce-window | flops 1560576 | bytes 98308 | tf_op jit(solution)/shard_map/reduce-window.2
  570.0 5.4 reshape.291
  575.7 10.0 multiply_reduce_fusion.7
  586.6 2.5 fusion.58
  592.9 7.4 fusion.99
  605.3 10.4 convolution_convert_fusion
  617.5 6.9 convolution_convert_fusion.1
  624.5 4.9 fusion.134
  629.3 3.1 copy.371
  632.5 3.1 copy.373
  635.6 6.8 convolution_bitcast_fusion
  642.5 3.3 copy.377
  645.9 14.8 %multiply_reduce_fusion.15 = (f32[256]{0:T(256)}, f32[256]{0:T(256)}, f32[256]{0:T(256)}, f32[256]{0:T(256)}, f32[256]{0:T(256)}, /*index=5*/f32[2,1024,256]{1,0,2:T(2,128)S(1)}) fusion(f32[2,1024,256]{1,0,2:T(2,128)S(1)} %copy-done.11, f32[2,1024,256]{1,0,2:T(2,128)} %get-tuple-element.482, f32[2,1024,256]{1,0,2:T(2,128)} %all-reduce.25.cloned.1.call-done), kind=kLoop, calls=%fused_computation.109 | loop fusion | flops 9435904 | bytes 8393728 | tf_op jit(solution)/shard_map/transpose(jvp())/reduce_sum | solution.py:22
  660.8 2.5 broadcast_multiply_fusion.4
  663.3 6.7 fusion.51
  670.4 3.0 fusion.139
  679.6 53.8 %all-reduce.22 = (f32[4,384]{1,0:T(4,128)}, f32[384]{0:T(512)}, f32[4,256]{1,0:T(4,128)}, f32[256]{0:T(256)}, f32[6]{0:T(128)}, /*index=5*/f32[6]{0:T(128)}, f32[6]{0:T(128)}, f32[384]{0:T(512)}) all-reduce(f32[4,384]{1,0:T(4,128)S(1)} %pad_add_fusion.7, f32[384]{0:T(512)S(1)} %copy-done.75, ...), channel_id=1, replica_groups=mesh['dp'=16,'tensor'=8] {'dp'}, use_global_device_ids=true, to_apply=%region_34.35 | all-reduce | flops 3602 | bytes 28816 | tf_op jit(solution)/shard_map/psum | solution.py:236
  733.4 34.0 %reduce-scatter.18.cloned.1.call-done = bf16[256,1536]{1,0:T(8,128)(2,1)} async-done(((bf16[2048,1536]{1,0:T(8,128)(2,1)}), bf16[256,1536]{1,0:T(8,128)(2,1)}) %reduce-scatter.18.cloned.1.call-update) | async-done | bytes 786448 | tf_op jit(solution)/shard_map/reduce_scatter | solution.py:195
  767.4 3.0 fusion.67
  770.5 74.0 %psum.95 = f32[1536]{0:T(1024)} all-reduce(f32[1536]{0:T(1024)S(1)} %get-tuple-element.428), channel_id=1, replica_groups=mesh['dp'=16,'tensor'=8] {'dp','tensor'}, use_global_device_ids=true, to_apply=%region_25.26 | all-reduce | flops 1536 | bytes 12288 | tf_op jit(solution)/shard_map/psum | solution.py:249
  844.4 24.9 %reduce-scatter.16.cloned.1.call-done = bf16[256,1536]{1,0:T(8,128)(2,1)} async-done(((bf16[2048,1536]{1,0:T(8,128)(2,1)}), bf16[256,1536]{1,0:T(8,128)(2,1)}) %reduce-scatter.16.cloned.1.call-update) | async-done | bytes 786448 | tf_op jit(solution)/shard_map/reduce_scatter | solution.py:144
  869.3 3.6 fusion.64
  873.0 61.4 %reduce-scatter.22.cloned.1.call-done = f32[96,384]{1,0:T(8,128)} async-done(((f32[1536,384]{1,0:T(8,128)}), f32[96,384]{1,0:T(8,128)}) %reduce-scatter.22.cloned.1.call-update) | async-done | bytes 147472
  934.3 65.5 %reduce-scatter.24.cloned.1.call-done = f32[96,384]{1,0:T(8,128)} async-done(((f32[1536,384]{1,0:T(8,128)}), f32[96,384]{1,0:T(8,128)}) %reduce-scatter.24.cloned.1.call-update) | async-done | bytes 147472
  999.8 65.2 %reduce-scatter.28.cloned.1.call-done = f32[96,384]{1,0:T(8,128)} async-done(((f32[1536,384]{1,0:T(8,128)}), f32[96,384]{1,0:T(8,128)}) %reduce-scatter.28.cloned.1.call-update) | async-done | bytes 147472
  1065.1 64.1 %reduce-scatter.20.cloned.1.call-done = f32[96,256]{1,0:T(8,128)} async-done(((f32[1536,256]{1,0:T(8,128)}), f32[96,256]{1,0:T(8,128)}) %reduce-scatter.20.cloned.1.call-update) | async-done | bytes 98320 | tf_op jit(solution)/shard_map/reduce_scatter | solution.py:223
  (330 shorter events, 108.2 us)
Async XLA Ops:
  7.2 8.3 copy-start.51
  7.2 30.2 %copy-start.85 = (bf16[96,6]{0,1:T(8,128)(2,1)S(1)}, bf16[96,6]{0,1:T(8,128)(2,1)}, u32[]{:S(2)}) copy-start(bf16[96,6]{0,1:T(8,128)(2,1)} %param.25) | copy-start | bytes 3460
  7.2 46.8 %copy-start.81 = (f32[4,256]{1,0:T(4,128)S(1)}, f32[4,256]{1,0:T(4,128)}, u32[]{:S(2)}) copy-start(f32[4,256]{1,0:T(4,128)} %param.28) | copy-start | bytes 12292
  7.2 47.5 %copy-start.78 = (f32[4,384]{1,0:T(4,128)S(1)}, f32[4,384]{1,0:T(4,128)}, u32[]{:S(2)}) copy-start(f32[4,384]{1,0:T(4,128)} %param.26) | copy-start | bytes 18436
  7.2 47.5 %copy-start.88 = (f32[6]{0:T(128)S(1)}, f32[6]{0:T(128)}, u32[]{:S(2)}) copy-start(f32[6]{0:T(128)} %param.31) | copy-start | bytes 76
  7.2 48.0 %copy-start.86 = (f32[6]{0:T(128)S(1)}, f32[6]{0:T(128)}, u32[]{:S(2)}) copy-start(f32[6]{0:T(128)} %param.32) | copy-start | bytes 76
  7.2 48.8 %all-gather.9.cloned.1.call-start = ((), (), s32[]{:S(2)}) async-start(), calls=%async_computation.8 | async-start | bytes 1253376 | tf_op jit(solution)/shard_map/all_gather | solution.py:109
  8.0 72.6 %all-gather.11.cloned.1.call-start = ((), (), s32[]{:S(2)}) async-start(), calls=%async_computation.9 | async-start | bytes 1253376 | tf_op jit(solution)/shard_map/all_gather | solution.py:110
  8.7 163.9 %all-gather.7.cloned.1.call-start = ((), (), s32[]{:S(2)}) async-start(), calls=%async_computation.7 | async-start | bytes 7077888 | tf_op jit(solution)/shard_map/all_gather | solution.py:118
  13.6 339.8 %all-gather.13.cloned.1.call-start = ((), (), s32[]{:S(2)}) async-start(), calls=%async_computation.10 | async-start | bytes 1253376 | tf_op jit(solution)/shard_map/all_gather | solution.py:113
  14.1 339.2 %all-gather.15.cloned.1.call-start = ((), (), s32[]{:S(2)}) async-start(), calls=%async_computation.12 | async-start | bytes 7077888 | tf_op jit(solution)/shard_map/all_gather | solution.py:161
  14.7 631.1 %all-reduce.25.cloned.1.call-start = ((), (), s32[]{:S(2)}) async-start(), calls=%async_computation.15 | async-start | bytes 4194304 | tf_op jit(solution)/shard_map/psum | solution.py:184
  37.4 49.4 %copy-start.22 = (bf16[1536,256]{1,0:T(8,128)(2,1)}, bf16[1536,256]{1,0:T(8,128)(2,1)S(1)}, u32[]{:S(2)}) copy-start(bf16[1536,256]{1,0:T(8,128)(2,1)S(1)} %all_gather.30) | copy-start | bytes 2359300
  54.0 32.8 %copy-start.27 = (bf16[16,96,6]{2,1,0:T(8,128)(2,1)}, bf16[16,96,6]{2,1,0:T(8,128)(2,1)S(1)}, u32[]{:S(2)}) copy-start(bf16[16,96,6]{2,1,0:T(8,128)(2,1)S(1)} %copy.379) | copy-start | bytes 55300
  54.7 137.4 %copy-start.54 = (f32[384]{0:T(512)}, f32[384]{0:T(512)S(1)}, u32[]{:S(2)}) copy-start(f32[384]{0:T(512)S(1)} %get-tuple-element.433) | copy-start | bytes 4612
  54.7 137.4 %copy-start.56 = (f32[384]{0:T(512)}, f32[384]{0:T(512)S(1)}, u32[]{:S(2)}) copy-start(f32[384]{0:T(512)S(1)} %get-tuple-element.434) | copy-start | bytes 4612
  54.7 137.4 %copy-start.58 = (f32[384]{0:T(512)}, f32[384]{0:T(512)S(1)}, u32[]{:S(2)}) copy-start(f32[384]{0:T(512)S(1)} %get-tuple-element.435) | copy-start | bytes 4612
  54.8 137.4 %copy-start.60 = (f32[384]{0:T(512)}, f32[384]{0:T(512)S(1)}, u32[]{:S(2)}) copy-start(f32[384]{0:T(512)S(1)} %get-tuple-element.436) | copy-start | bytes 4612
  200.9 44.9 %copy-start.63 = (f32[1,256]{1,0:T(1,128)S(1)}, f32[1,256]{1,0:T(1,128)}, u32[]{:S(2)}) copy-start(f32[1,256]{1,0:T(1,128)} %get-tuple-element.505) | copy-start | bytes 3076
  200.9 44.9 %copy-start.65 = (f32[1,256]{1,0:T(1,128)S(1)}, f32[1,256]{1,0:T(1,128)}, u32[]{:S(2)}) copy-start(f32[1,256]{1,0:T(1,128)} %get-tuple-element.506) | copy-start | bytes 3076
  269.2 6.3 copy-start.8
  269.2 6.3 copy-start.29
  270.7 9.0 copy-start.34
  302.2 14.9 %copy-start.15 = (f32[2,4,6,64,256]{4,3,2,1,0:T(8,128)}, f32[2,4,6,64,256]{4,3,2,1,0:T(8,128)S(1)}, u32[]{:S(2)}) copy-start(f32[2,4,6,64,256]{4,3,2,1,0:T(8,128)S(1)} %fusion.87) | copy-start | bytes 9437188
  353.4 31.7 %copy-start.83 = (f32[384]{0:T(512)S(1)}, f32[384]{0:T(512)}, u32[]{:S(2)}) copy-start(f32[384]{0:T(512)} %param.33) | copy-start | bytes 4612
  399.5 7.2 copy-start
  399.5 7.2 copy-start.25
  399.5 7.2 copy-start.31
  399.5 7.2 copy-start.45
  399.5 7.2 copy-start.48
  406.7 19.6 %copy-start.2 = (f32[4,2,6,64,128]{4,3,2,1,0:T(8,128)S(1)}, f32[4,2,6,64,128]{4,3,2,1,0:T(8,128)}, u32[]{:S(2)}) copy-start(f32[4,2,6,64,128]{4,3,2,1,0:T(8,128)} %get-tuple-element.629) | copy-start | bytes 4718596
  406.7 19.6 %copy-start.37 = (f32[2,4,256,6]{2,3,1,0:T(8,128)S(1)}, f32[2,4,256,6]{2,3,1,0:T(8,128)}, u32[]{:S(2)}) copy-start(f32[2,4,256,6]{2,3,1,0:T(8,128)} %get-tuple-element.500) | copy-start | bytes 147460
  451.4 8.0 copy-start.9
  451.4 8.0 copy-start.13
  451.4 8.0 copy-start.32
  464.9 9.5 copy-start.10
  465.0 9.5 copy-start.18
  484.7 192.7 %reduce-scatter.26.cloned.1.call-start = ((), (), s32[]{:S(2)}) async-start(), calls=%async_computation.18 | async-start | bytes 835584
  570.0 5.6 copy-start.5
  570.0 5.6 copy-start.74
  575.6 10.1 copy-start.55
  575.7 10.0 copy-start.57
  575.7 10.0 copy-start.59
  575.7 10.0 copy-start.61
  592.9 7.5 copy-start.53
  592.9 12.3 %copy-start.28 = (bf16[16,96,6]{2,1,0:T(8,128)(2,1)S(1)}, bf16[16,96,6]{2,1,0:T(8,128)(2,1)}, u32[]{:S(2)}) copy-start(bf16[16,96,6]{2,1,0:T(8,128)(2,1)} %copy-done.27) | copy-start | bytes 55300
  605.2 162.2 %reduce-scatter.18.cloned.1.call-start = ((), (), s32[]{:S(2)}) async-start(), calls=%async_computation.13 | async-start | bytes 7077888 | tf_op jit(solution)/shard_map/reduce_scatter | solution.py:195
  615.7 253.7 %reduce-scatter.16.cloned.1.call-start = ((), (), s32[]{:S(2)}) async-start(), calls=%async_computation.11 | async-start | bytes 7077888 | tf_op jit(solution)/shard_map/reduce_scatter | solution.py:144
  624.4 309.9 %reduce-scatter.22.cloned.1.call-start = ((), (), s32[]{:S(2)}) async-start(), calls=%async_computation.16 | async-start | bytes 2506752
  632.4 367.4 %reduce-scatter.24.cloned.1.call-start = ((), (), s32[]{:S(2)}) async-start(), calls=%async_computation.17 | async-start | bytes 2506752
  635.6 429.5 %reduce-scatter.28.cloned.1.call-start = ((), (), s32[]{:S(2)}) async-start(), calls=%async_computation.19 | async-start | bytes 2506752
  645.8 483.4 %reduce-scatter.20.cloned.1.call-start = ((), (), s32[]{:S(2)}) async-start(), calls=%async_computation.14 | async-start | bytes 1671168 | tf_op jit(solution)/shard_map/reduce_scatter | solution.py:223
  645.9 14.9 %copy-start.64 = (f32[1,256]{1,0:T(1,128)S(1)}, f32[1,256]{1,0:T(1,128)}, u32[]{:S(2)}) copy-start(f32[1,256]{1,0:T(1,128)} %get-tuple-element.505) | copy-start | bytes 3076
  645.9 14.8 %copy-start.66 = (f32[1,256]{1,0:T(1,128)S(1)}, f32[1,256]{1,0:T(1,128)}, u32[]{:S(2)}) copy-start(f32[1,256]{1,0:T(1,128)} %get-tuple-element.506) | copy-start | bytes 3076
  645.9 14.8 %copy-start.67 = (f32[1,256]{1,0:T(1,128)S(1)}, f32[1,256]{1,0:T(1,128)}, u32[]{:S(2)}) copy-start(f32[1,256]{1,0:T(1,128)} %get-tuple-element.507) | copy-start | bytes 3076
  645.9 14.8 %copy-start.68 = (f32[1,256]{1,0:T(1,128)S(1)}, f32[1,256]{1,0:T(1,128)}, u32[]{:S(2)}) copy-start(f32[1,256]{1,0:T(1,128)} %get-tuple-element.508) | copy-start | bytes 3076
  660.7 9.5 slice-start
  663.3 7.0 slice-start.1
  670.3 9.3 copy-start.75
  670.3 97.1 %copy-start.19 = (bf16[256,1536]{1,0:T(8,128)(2,1)S(1)}, bf16[256,1536]{1,0:T(8,128)(2,1)}, u32[]{:S(2)}) copy-start(bf16[256,1536]{1,0:T(8,128)(2,1)} %param.20) | copy-start | bytes 2359300
  670.3 97.1 %copy-start.23 = (bf16[1536,256]{1,0:T(8,128)(2,1)S(1)}, bf16[1536,256]{1,0:T(8,128)(2,1)}, u32[]{:S(2)}) copy-start(bf16[1536,256]{1,0:T(8,128)(2,1)} %copy-done.22) | copy-start | bytes 2359300
  670.4 97.1 %copy-start.52 = (f32[1536]{0:T(1024)S(1)}, f32[1536]{0:T(1024)}, u32[]{:S(2)}) copy-start(f32[1536]{0:T(1024)} %param.21) | copy-start | bytes 18436
  670.4 97.1 %copy-start.70 = (f32[256]{0:T(256)S(1)}, f32[256]{0:T(256)}, u32[]{:S(2)}) copy-start(f32[256]{0:T(256)} %copy-done.69) | copy-start | bytes 3076
  673.4 196.0 %copy-start.21 = (bf16[256,1536]{1,0:T(8,128)(2,1)S(1)}, bf16[256,1536]{1,0:T(8,128)(2,1)}, u32[]{:S(2)}) copy-start(bf16[256,1536]{1,0:T(8,128)(2,1)} %param.35) | copy-start | bytes 2359300
  (40 other events, 137.1 us)
Sparse Core Ops, SparseCore 0:
  9.8 35.5 all-gather.8
  47.1 33.4 all-gather.10
  83.5 89.1 all-gather.6
  174.2 30.3 all-gather.12
  206.8 89.1 all-gather.14
  484.8 91.7 all-reduce.24
  605.3 59.8 reduce-scatter.25
  669.6 97.7 reduce-scatter.17
  771.8 97.5 reduce-scatter.15
  872.3 61.9 reduce-scatter.21
  937.4 62.3 reduce-scatter.23
  1002.8 62.2 reduce-scatter.27
  1068.2 60.9 reduce-scatter.19
where the time goes:
time: 1150 us; the launch traced here: 1140 us
  waiting for transfers between devices  428 us (37%)
  blocking collectives  208 us (18%)
  other arithmetic  206 us (18%)
  matrix products  157 us (14%)
  local copies, waits for them, and re-layouts  121 us (11%)
  between operations  15.4 us (1%)
    unnamed x17, waiting for transfers between devices  195 us
    another operation x8, other arithmetic  94.5 us
    all_gather x1, waiting for transfers between devices, shards(): normed_all = lax.all_gather(normed, 'tensor', axis=0, tiled=True)  85.8 us
    psum x1, blocking collectives, shards(): norm_gain_sum = lax.psum(grad_norm_part, ('dp', 'tensor'))  74 us
    reduce_scatter x1, waiting for transfers between devices, shards(): lax.psum_scatter(grad_bc_w, 'dp', scatter_dimension=0, tiled=True)  64.1 us
    psum x1, blocking collectives, shards(): lax.psum((grad_conv_inner, grad_bias_inner, grad_conv_bc, grad_bias_bc, g...  53.8 us
    dot_general x3, matrix products, block_scan(): within = jnp.einsum('khts,kshp->kthp', mixing, weighted, precision=highest)  47.4 us
    reduce_scatter x1, waiting for transfers between devices, shards(): lax.psum_scatter(jnp.einsum('rc,dc->rd', row_block, back_heads, preferred...  34 us
  transfers between devices with their start and end apart: 13, of which 8 were waited for; matrix products, arithmetic and copies ran while one was open for 32% of the time, Pallas kernels for 0%

commit v1 on v0

v1 whole, which is shorter than its diff:
```python
import functools

import jax
import jax.numpy as jnp
from jax import lax
from jax.experimental import pallas as pl
from jax.experimental.pallas import tpu as pltpu
from jax.sharding import Mesh
from jax.sharding import PartitionSpec as P

D = 1536
LEN = 1024
INNER = 3072
STATE = 128
BLOCK = 256
BLOCKS = LEN // BLOCK
GROUPS = 2
HEADS = 6
COLS = HEADS * 64
LOG2E = 1.4426950408889634
EPS = 1e-05
F32 = jnp.float32
BF16 = jnp.bfloat16
MESH = pl.DeviceIdType.MESH
AXES = ("yl", "x", "c", "yh", "z")
ANY = pl.BlockSpec(memory_space=pl.ANY)


def dot(a, b):
    return jnp.dot(a, b, preferred_element_type=F32)


def dot_nt(a, b):
    return lax.dot_general(a, b, (((1,), (1,)), ((), ())), preferred_element_type=F32)


def dot_tn(a, b):
    return lax.dot_general(a, b, (((0,), (0,)), ((), ())), preferred_element_type=F32)


def pieces(v, n):
    out = []
    for _ in range(n):
        hi = v.astype(BF16)
        out.append(hi)
        v = v - hi.astype(F32)
    return out


def dot_left(v, ones, n):
    return sum(dot(p, ones) for p in pieces(v, n))


def dot_right(ones, v, n):
    return sum(dot(ones, p) for p in pieces(v, n))


def iota(shape, axis):
    return lax.broadcasted_iota(jnp.int32, shape, axis)


def expander():
    row, col = iota((128, COLS), 0), iota((128, COLS), 1)
    return (row == lax.shift_right_logical(col, 6)).astype(BF16)


def reducer():
    row, col = iota((COLS, 128), 0), iota((COLS, 128), 1)
    return (col == lax.shift_right_logical(row, 6)).astype(BF16)


def sigmoid(v):
    return 1.0 / (1.0 + jnp.exp(-v))


def causal(shape=(BLOCK, BLOCK)):
    return iota(shape, 0) >= iota(shape, 1)


def lower(strict=False):
    row, col = iota((BLOCK, BLOCK), 0), iota((BLOCK, BLOCK), 1)
    return ((row > col) if strict else (row >= col)).astype(BF16)


def upper():
    return (iota((BLOCK, BLOCK), 0) <= iota((BLOCK, BLOCK), 1)).astype(BF16)


def maps_kernel(normed, wsm, prm, conv_bc, bias_bc, bc_in_out, z_out, bc_out, s_out, st_out, dt_out, r_out, rt_out, u_out, ext):
    k = pl.program_id(0)
    x = normed[...]
    proj = dot(x, wsm[...])
    bc_in = jnp.concatenate([proj[:, 0:128], proj[:, 256:384]], axis=1)
    bc_in_out[...] = bc_in

    @pl.when(k == 0)
    def _():
        ext[0:8, :] = jnp.zeros((8, 256), F32)

    @pl.when(k > 0)
    def _():
        ext[0:8, :] = ext[BLOCK : BLOCK + 8, :]

    ext[8 : BLOCK + 8, :] = bc_in
    z = bias_bc[...] + sum(conv_bc[j : j + 1, :] * ext[5 + j : 5 + j + BLOCK, :] for j in range(4))
    z_out[...] = z
    bc = (z * sigmoid(z)).astype(BF16)
    bc_out[...] = bc
    b, c = bc[:, :STATE], bc[:, STATE:]
    s_out[0] = jnp.where(causal(), dot_nt(c, b), 0.0)
    st_out[0] = jnp.where(iota((BLOCK, BLOCK), 1) >= iota((BLOCK, BLOCK), 0), dot_nt(b, c), 0.0)
    tri = lower()
    for g in range(GROUPS):
        u = proj[:, 128 + 256 * g : 256 + 256 * g] + prm[g, 6:7, 0:128]
        dt = jnp.maximum(u, 0.0) + jnp.log(1.0 + jnp.exp(-jnp.abs(u)))
        rate = -jnp.exp(prm[g, 7:8, 0:128]) * LOG2E
        r = dot_right(tri, dt * rate, 3)
        u_out[g] = u
        dt_out[g] = dt
        r_out[g] = r
        rt_out[g] = jnp.transpose(r)[0:8, :]


def run_maps(normed_all, wsm, prm, conv_bc, bias_bc):
    full = lambda *s: pl.BlockSpec(s, lambda k: (0,) * len(s))
    small = lambda: pl.BlockSpec((GROUPS, BLOCK, 128), lambda k: (0, k, 0))
    rows = lambda n: pl.BlockSpec((BLOCK, n), lambda k: (k, 0))
    sq = lambda: pl.BlockSpec((1, BLOCK, BLOCK), lambda k: (k, 0, 0))
    shape = jax.ShapeDtypeStruct
    return pl.pallas_call(
        maps_kernel,
        grid=(BLOCKS,),
        out_shape=[
            shape((LEN, 256), F32),
            shape((LEN, 256), F32),
            shape((LEN, 256), BF16),
            shape((BLOCKS, BLOCK, BLOCK), F32),
            shape((BLOCKS, BLOCK, BLOCK), F32),
            shape((GROUPS, LEN, 128), F32),
            shape((GROUPS, LEN, 128), F32),
            shape((GROUPS, 8, LEN), F32),
            shape((GROUPS, LEN, 128), F32),
        ],
        in_specs=[rows(D), full(D, 512), full(GROUPS, 16, COLS), full(4, 256), full(1, 256)],
        out_specs=[rows(256), rows(256), rows(256), sq(), sq(), small(), small(), pl.BlockSpec((GROUPS, 8, BLOCK), lambda k: (0, 0, k)), small()],
        scratch_shapes=[pltpu.VMEM((BLOCK + 8, 256), F32)],
        compiler_params=pltpu.CompilerParams(vmem_limit_bytes=40 * 2**20),
        name="state_maps",
    )(normed_all, wsm, prm, conv_bc, bias_bc)


def fwd_kernel(normed, wcat, prm, bc, s, dt, r, rt, gate_out, inner_out, z_out, y_out, gp_out, h_out, ss_out, ext, state):
    k, g = pl.program_id(0), pl.program_id(1)
    proj = dot(normed[...], wcat[...])
    gate = proj[:, :COLS]
    inner = proj[:, COLS:]
    gate_out[...] = gate
    inner_out[...] = inner

    @pl.when(k == 0)
    def _():
        ext[g, 0:8, :] = jnp.zeros((8, COLS), F32)
        state[g] = jnp.zeros((STATE, COLS), F32)

    @pl.when(k > 0)
    def _():
        ext[g, 0:8, :] = ext[g, BLOCK : BLOCK + 8, :]

    ext[g, 8 : BLOCK + 8, :] = inner
    z = prm[0, 4:5, :] + sum(prm[0, j : j + 1, :] * ext[g, 5 + j : 5 + j + BLOCK, :] for j in range(4))
    z_out[...] = z
    x = z * sigmoid(z)
    spread = expander()
    rv = r[0]
    last = rv[BLOCK - 1 : BLOCK, :]
    w = x * dot_left(dt[0], spread, 2)
    grow = dot_left(jnp.exp2(rv), spread, 2)
    tail = dot_left(jnp.exp2(last - rv), spread, 2)
    wl = w.astype(BF16)
    b, c = bc[:, :STATE], bc[:, STATE:]
    h = state[g]
    h_out[0, 0] = h
    scores = s[0]
    left = iota((BLOCK, 128), 1) < 64
    parts = []
    for p in range(HEADS // 2):
        halves = []
        for q in (2 * p, 2 * p + 1):
            gap = jnp.minimum(rv[:, q : q + 1] - rt[0, q : q + 1, :], 0.0)
            halves.append(dot((scores * jnp.exp2(gap)).astype(BF16), wl[:, 128 * p : 128 * (p + 1)]))
        parts.append(jnp.where(left, halves[0], halves[1]))
    y = jnp.concatenate(parts, axis=1) + grow * dot(c, h.astype(BF16)) + prm[0, 9:10, :] * x
    y_out[...] = y
    state[g] = grow[BLOCK - 1 : BLOCK, :] * h + dot_tn(b, (tail * w).astype(BF16))
    gp = y * (gate * sigmoid(gate))
    gp_out[...] = gp
    sq = gp * gp
    ss = sq[:, 0:128] + sq[:, 128:256] + sq[:, 256:384]

    @pl.when(g == 0)
    def _():
        ss_out[...] = ss

    @pl.when(g > 0)
    def _():
        ss_out[...] += ss


def run_fwd(normed_all, wcat, prm, bc, s, dt, r, rt):
    shape = jax.ShapeDtypeStruct
    cols = lambda: pl.BlockSpec((BLOCK, COLS), lambda k, g: (k, g))
    small = lambda: pl.BlockSpec((1, BLOCK, 128), lambda k, g: (g, k, 0))
    wide = shape((LEN, GROUPS * COLS), F32)
    return pl.pallas_call(
        fwd_kernel,
        grid=(BLOCKS, GROUPS),
        out_shape=[wide, wide, wide, wide, wide, shape((BLOCKS, GROUPS, STATE, COLS), F32), shape((LEN, 128), F32)],
        in_specs=[
            pl.BlockSpec((BLOCK, D), lambda k, g: (k, 0)),
            pl.BlockSpec((D, 2 * COLS), lambda k, g: (0, g)),
            pl.BlockSpec((1, 16, COLS), lambda k, g: (g, 0, 0)),
            pl.BlockSpec((BLOCK, 256), lambda k, g: (k, 0)),
            pl.BlockSpec((1, BLOCK, BLOCK), lambda k, g: (k, 0, 0)),
            small(),
            small(),
            pl.BlockSpec((1, 8, BLOCK), lambda k, g: (g, 0, k)),
        ],
        out_specs=[
            cols(),
            cols(),
            cols(),
            cols(),
            cols(),
            pl.BlockSpec((1, 1, STATE, COLS), lambda k, g: (k, g, 0, 0)),
            pl.BlockSpec((BLOCK, 128), lambda k, g: (k, 0)),
        ],
        scratch_shapes=[pltpu.VMEM((GROUPS, BLOCK + 8, COLS), F32), pltpu.VMEM((GROUPS, STATE, COLS), F32)],
        compiler_params=pltpu.CompilerParams(vmem_limit_bytes=48 * 2**20),
        cost_estimate=pl.CostEstimate(flops=16 * 2**30, bytes_accessed=40 * 2**20, transcendentals=2**23),
        name="scan_forward",
    )(normed_all, wcat, prm, bc, s, dt, r, rt)


def bwd_kernel(gm, gate, inner, zin, yin, hin, prm, bc, st, dt, r, rt, u, root, cross, cat_out, gstep_out, dbc_out, acc, ext, dstate, dst, dbc):
    k, g = pl.program_id(0), pl.program_id(1)

    @pl.when((k == 0) & (g == 0))
    def _():
        acc[...] = jnp.zeros_like(acc)

    @pl.when(k == 0)
    def _():
        ext[g, BLOCK : BLOCK + 8, :] = jnp.zeros((8, COLS), F32)
        dstate[g] = jnp.zeros((STATE, COLS), F32)

    @pl.when(k > 0)
    def _():
        ext[g, BLOCK : BLOCK + 8, :] = ext[g, 0:8, :]

    @pl.when(g == 0)
    def _():
        dst[...] = jnp.zeros_like(dst)
        dbc[...] = jnp.zeros_like(dbc)

    y = yin[...]
    gv = gate[...]
    sig = sigmoid(gv)
    act = gv * sig
    ir = root[...]
    gain = prm[0, 5:6, :]
    gp = y * act
    gmix = gm[...]
    gain_grad = gmix * gp * ir
    gated = ir * (gmix * gain) - gp * cross[...]
    gs = gated * act
    cat_out[:, :COLS] = (gated * y * sig * (1.0 + gv * (1.0 - sig))).astype(BF16)
    z = zin[...]
    zs = sigmoid(z)
    x = z * zs
    spread, fold = expander(), reducer()
    rv = r[0]
    last = rv[BLOCK - 1 : BLOCK, :]
    dte = dot_left(dt[0], spread, 2)
    grow = dot_left(jnp.exp2(rv), spread, 2)
    tail = dot_left(jnp.exp2(last - rv), spread, 2)
    w = x * dte
    wl = w.astype(BF16)
    gl = gs.astype(BF16)
    b, c = bc[:, :STATE], bc[:, STATE:]
    h = hin[0, 0]
    dh = dstate[g]
    dhl = dh.astype(BF16)
    scores = st[0]
    left = iota((BLOCK, 128), 1) < 64
    parts = []
    for p in range(HEADS // 2):
        halves = []
        cut = slice(128 * p, 128 * (p + 1))
        wp, gpair = wl[:, cut], gl[:, cut]
        zero = jnp.zeros_like(wp)
        for q in (2 * p, 2 * p + 1):
            decay = jnp.exp2(jnp.minimum(rt[0, q : q + 1, :] - rv[:, q : q + 1], 0.0))
            halves.append(dot((scores * decay).astype(BF16), gpair))
            mine = jnp.where(left, wp, zero) if q % 2 == 0 else jnp.where(left, zero, wp)
            dst[...] += dot_nt(mine, gpair) * decay
        parts.append(jnp.where(left, halves[0], halves[1]))
    dwi = jnp.concatenate(parts, axis=1)
    dws = tail * dot(b, dhl)
    dw = dwi + dws
    skip = prm[0, 9:10, :]
    skipgrad = gs * x
    glf = gl.astype(F32)
    diff = dot_left(glf * (y - skip * x) - wl.astype(F32) * dwi, fold, 3)
    zsum = dot_left(w * dws, fold, 3)
    const = dot_left(jnp.sum(h * dh, axis=0, keepdims=True) * grow[BLOCK - 1 : BLOCK, :] + jnp.zeros((8, COLS), F32), fold, 3)
    da = dot_right(upper(), diff, 3) + dot_right(lower(strict=True), zsum, 3) + const[0:1, :]
    rate = -jnp.exp(prm[0, 7:8, 0:128])
    ddt = dot_left(x * dw, fold, 3) + rate * da
    uu = u[0]
    dstep = ddt * sigmoid(uu)
    gstep_out[0] = dstep.astype(BF16)
    gx = grow * gs
    gxl = gx.astype(BF16)
    dbc[:, STATE:] += dot_nt(gxl, h.astype(BF16))
    dbc[:, :STATE] += dot_nt((tail * w).astype(BF16), dhl)
    dstate[g] = grow[BLOCK - 1 : BLOCK, :] * dh + dot_tn(c, gxl)
    dx = dte * dw + skip * gs
    dz = dx * (zs * (1.0 + z * (1.0 - zs)))
    ext[g, 0:BLOCK, :] = dz
    xi = inner[...]
    gi = jnp.zeros((BLOCK, COLS), F32)
    for j in range(4):
        moved = ext[g, 3 - j : 3 - j + BLOCK, :]
        gi = gi + prm[0, j : j + 1, :] * moved
        acc[g, j : j + 1, :] += jnp.sum(xi * moved, axis=0, keepdims=True)
    cat_out[:, COLS:] = gi.astype(BF16)
    acc[g, 4:5, :] += jnp.sum(dz, axis=0, keepdims=True)
    acc[g, 5:6, :] += jnp.sum(gain_grad, axis=0, keepdims=True)
    acc[g, 6:7, 0:128] += jnp.sum(dstep, axis=0, keepdims=True)
    acc[g, 7:8, 0:128] += jnp.sum(da * dt[0], axis=0, keepdims=True) * rate
    acc[g, 9:10, :] += jnp.sum(skipgrad, axis=0, keepdims=True)

    @pl.when(g == GROUPS - 1)
    def _():
        ds = jnp.where(iota((BLOCK, BLOCK), 1) >= iota((BLOCK, BLOCK), 0), dst[...], 0.0).astype(BF16)
        dbc_out[:, STATE:] = (dbc[:, STATE:] + dot_tn(ds, b)).astype(BF16)
        dbc_out[:, :STATE] = (dbc[:, :STATE] + dot(ds, c)).astype(BF16)


def run_bwd(gm, gate, inner, z, y, hin, prm, bc, st, dt, r, rt, u, root, cross):
    shape = jax.ShapeDtypeStruct
    rev = lambda k: BLOCKS - 1 - k
    cols = lambda: pl.BlockSpec((BLOCK, COLS), lambda k, g: (rev(k), g))
    small = lambda: pl.BlockSpec((1, BLOCK, 128), lambda k, g: (g, rev(k), 0))
    column = lambda: pl.BlockSpec((BLOCK, 1), lambda k, g: (rev(k), 0))
    return pl.pallas_call(
        bwd_kernel,
        grid=(BLOCKS, GROUPS),
        out_shape=[
            shape((LEN, GROUPS * 2 * COLS), BF16),
            shape((GROUPS, LEN, 128), BF16),
            shape((LEN, 256), BF16),
            shape((GROUPS, 16, COLS), F32),
        ],
        in_specs=[
            cols(),
            cols(),
            cols(),
            cols(),
            cols(),
            pl.BlockSpec((1, 1, STATE, COLS), lambda k, g: (rev(k), g, 0, 0)),
            pl.BlockSpec((1, 16, COLS), lambda k, g: (g, 0, 0)),
            pl.BlockSpec((BLOCK, 256), lambda k, g: (rev(k), 0)),
            pl.BlockSpec((1, BLOCK, BLOCK), lambda k, g: (rev(k), 0, 0)),
            small(),
            small(),
            pl.BlockSpec((1, 8, BLOCK), lambda k, g: (g, 0, rev(k))),
            small(),
            column(),
            column(),
        ],
        out_specs=[
            pl.BlockSpec((BLOCK, 2 * COLS), lambda k, g: (rev(k), g)),
            small(),
            pl.BlockSpec((BLOCK, 256), lambda k, g: (rev(k), 0)),
            pl.BlockSpec((GROUPS, 16, COLS), lambda k, g: (0, 0, 0)),
        ],
        scratch_shapes=[
            pltpu.VMEM((GROUPS, BLOCK + 8, COLS), F32),
            pltpu.VMEM((GROUPS, STATE, COLS), F32),
            pltpu.VMEM((BLOCK, BLOCK), F32),
            pltpu.VMEM((BLOCK, 256), F32),
        ],
        compiler_params=pltpu.CompilerParams(vmem_limit_bytes=48 * 2**20),
        cost_estimate=pl.CostEstimate(flops=16 * 2**30, bytes_accessed=40 * 2**20, transcendentals=2**23),
        name="scan_backward",
    )(gm, gate, inner, z, y, hin, prm, bc, st, dt, r, rt, u, root, cross)


class Net:
    def __init__(self, send, recv):
        self.send, self.recv, self.copies = send, recv, []
        self.at = {name: lax.axis_index(name) for name in AXES}
        self.at["y"] = self.at["yh"] * 2 + self.at["yl"]

    def near(self, axis, step):
        return lax.rem(self.at[axis] + step + 4, 4)

    def device(self, axis, step):
        if axis == "c":
            return {"c": 1 - self.at["c"]}
        if axis == "yh":
            return {"yh": 1 - self.at["yh"]}
        place = self.near(axis, step)
        if axis == "y":
            return {"yh": place // 2, "yl": lax.rem(place, 2)}
        return {axis: place}

    def start(self, src, dst, axis, step=1):
        copy = Copy(
            pltpu.make_async_remote_copy(
                src_ref=src,
                dst_ref=dst,
                send_sem=self.send.at[len(self.copies)],
                recv_sem=self.recv.at[len(self.copies)],
                device_id=self.device(axis, step),
                device_id_type=MESH,
            )
        )
        self.copies.append(copy)
        return copy

    def barrier(self, peers):
        here = pltpu.get_barrier_semaphore()
        for axis, step in peers:
            pl.semaphore_signal(here, inc=1, device_id=self.device(axis, step), device_id_type=MESH)
        pl.semaphore_wait(here, len(peers))

    def finish(self):
        for copy in self.copies:
            copy.arrived()
        for copy in self.copies:
            copy.left()


class Copy:
    def __init__(self, copy):
        self.copy, self.here, self.gone = copy, False, False
        copy.start()

    def arrived(self):
        if not self.here:
            self.here = True
            self.copy.wait_recv()

    def left(self):
        if not self.gone:
            self.gone = True
            self.copy.wait_send()


def sems(n):
    return [pltpu.SemaphoreType.DMA((n,)), pltpu.SemaphoreType.DMA((n,))]


def rows(ref, first, count):
    return ref.at[pl.ds(pl.multiple_of(first, 16), count)]


def gather_kernel(x, cot, gain, wa, wo, ws, pk, normed_all, cot_all, wcat, wout, wsm, prm, low, send, recv, local):
    net = Net(send, recv)
    at = net.at
    yh, yl, cx, cc, z = at["yh"], at["yl"], at["x"], at["c"], at["z"]
    net.barrier([("z", 1), ("z", -1), ("x", 1), ("x", -1), ("y", 1), ("y", -1), ("c", 1), ("yh", 1)])
    wide = ((wcat, wa, 768),)
    thin = ((wout, wo, 384), (wsm, ws, 256))

    def spot(ref, n, y, xx, part=None):
        cut = pl.ds(0, 96) if part is None else pl.ds(48 * part, 48)
        return ref.at[lax.rem(y, 2), xx, cc, cut, pl.ds(pl.multiple_of((y // 2) * n, 128), n)]

    def line(ref, n, y, part=None):
        cut = pl.ds(0, 96) if part is None else pl.ds(48 * part, 48)
        return ref.at[lax.rem(y, 2), :, cc, cut, pl.ds(pl.multiple_of((y // 2) * n, 128), n)]

    def column(ref, xx, part=None):
        cut = pl.ds(0, 96) if part is None else pl.ds(48 * part, 48)
        return ref.at[:, xx, cc, cut, :]

    own = []
    for i, (ref, src, n) in enumerate(wide + thin):
        own.append(pltpu.make_async_copy(src, spot(ref, n, at["y"], cx), local.at[i]))
    own.append(pltpu.make_async_copy(pk, prm.at[yh], local.at[3]))
    own.append(pltpu.make_async_copy(cot, rows(cot_all, z * 256, 256), local.at[4]))
    for copy in own:
        copy.start()
    a1, b1 = [], []
    for ref, src, n in wide:
        for step in (1, -1):
            a1.append(net.start(src, spot(ref, n, at["y"], cx), "x", step))
    for ref, src, n in thin:
        for step in (1, -1):
            b1.append(net.start(src, spot(ref, n, at["y"], cx), "y", step))
    for ref, src, n in wide + thin:
        net.start(src, spot(ref, n, at["y"], cx), "c")
    net.start(pk, prm.at[yh], "yh")
    v = x[...].astype(F32)
    root = lax.rsqrt(jnp.mean(v * v, axis=1, keepdims=True) + EPS)
    low[...] = (v * root * gain[...]).astype(BF16)
    own_normed = pltpu.make_async_copy(low, rows(normed_all, z * 256, 256), local.at[5])
    own_normed.start()
    zs = [net.start(low, rows(normed_all, z * 256, 256), "z", step) for step in (1, -1)]
    a2, b2 = [], []
    for (part, step), copy in zip(((0, 1), (1, -1)), a1):
        copy.arrived()
        here = spot(wcat, 768, at["y"], net.near("x", -step), part)
        a2.append(net.start(here, here, "x", step))
    for i, (ref, src, n) in enumerate(thin):
        for (part, step), copy in zip(((0, 1), (1, -1)), b1[2 * i : 2 * i + 2]):
            copy.arrived()
            here = spot(ref, n, net.near("y", -step), cx, part)
            b2.append(net.start(here, here, "y", step))
    for i in (0, 1, 2):
        own[i].wait()
    for copy in a2:
        copy.arrived()
    here = line(wcat, 768, at["y"])
    a3 = [net.start(here, here, "y", step) for step in (1, -1)]
    for copy in b2:
        copy.arrived()
    b3 = []
    for ref, src, n in thin:
        here = column(ref, cx)
        b3 += [net.start(here, here, "x", step) for step in (1, -1)]
    for step in (1, 2, 3):
        here = spot(wcat, 768, at["y"], net.near("x", step))
        net.start(here, here, "c")
        for ref, src, n in thin:
            here = spot(ref, n, net.near("y", step), cx)
            net.start(here, here, "c")
    def hop(ref, first):
        out = []
        for (part, step), copy in zip(((0, 1), (1, -1)), first):
            copy.arrived()
            here = rows(ref, net.near("z", -step) * 256 + 128 * part, 128)
            out.append(net.start(here, here, "z", step))
        return out

    zs2 = hop(normed_all, zs)
    cs = [net.start(cot, rows(cot_all, z * 256, 256), "z", step) for step in (1, -1)]
    a4, b4 = [], []
    for (part, step), copy in zip(((0, 1), (1, -1)), a3):
        copy.arrived()
        here = line(wcat, 768, net.near("y", -step), part)
        a4.append(net.start(here, here, "y", step))
        here = line(wcat, 768, net.near("y", -step))
        net.start(here, here, "c")
    for i, (ref, src, n) in enumerate(thin):
        for (part, step), copy in zip(((0, 1), (1, -1)), b3[2 * i : 2 * i + 2]):
            copy.arrived()
            here = column(ref, net.near("x", -step), part)
            b4.append(net.start(here, here, "x", step))
            here = column(ref, net.near("x", -step))
            net.start(here, here, "c")
    for copy in a4:
        copy.arrived()
    here = line(wcat, 768, net.near("y", 2))
    net.start(here, here, "c")
    for copy in b4:
        copy.arrived()
    for ref, src, n in thin:
        here = column(ref, net.near("x", 2))
        net.start(here, here, "c")
    hop(cot_all, cs)
    net.finish()
    for i in (3, 4):
        own[i].wait()
    own_normed.wait()


def run_gather(x, cot, gain, wa, wo, ws, pk):
    shape = jax.ShapeDtypeStruct
    vmem = pl.BlockSpec(memory_space=pltpu.VMEM)
    return pl.pallas_call(
        gather_kernel,
        out_shape=[
            shape((LEN, D), BF16),
            shape((LEN, D), BF16),
            shape((2, 4, 2, 96, 1536), BF16),
            shape((2, 4, 2, 96, 768), BF16),
            shape((2, 4, 2, 96, 512), BF16),
            shape((2, 16, COLS), F32),
        ],
        in_specs=[vmem, ANY, vmem, ANY, ANY, ANY, ANY],
        out_specs=[ANY] * 6,
        scratch_shapes=[pltpu.VMEM((256, D), BF16)] + sems(64) + [pltpu.SemaphoreType.DMA((6,))],
        compiler_params=pltpu.CompilerParams(collective_id=0, has_side_effects=True, vmem_limit_bytes=24 * 2**20),
        name="gather_all",
    )(x, cot, gain, wa, wo, ws, pk)


def stats_kernel(part, out, slots, send, recv):
    net = Net(send, recv)
    peers = [("z", 1), ("z", -1), ("z", 2)]
    net.barrier(peers)
    z = net.at["z"]
    for axis, step in peers:
        net.start(part, slots.at[z], axis, step)
    slots[z] = part[...]
    net.finish()
    out[...] = (slots[0] + slots[1]) + (slots[2] + slots[3])


def run_stats(part):
    return pl.pallas_call(
        stats_kernel,
        out_shape=jax.ShapeDtypeStruct((16, 128), F32),
        in_specs=[pl.BlockSpec(memory_space=pltpu.VMEM)],
        out_specs=pl.BlockSpec(memory_space=pltpu.VMEM),
        scratch_shapes=[pltpu.VMEM((4, 16, 128), F32)] + sems(3),
        compiler_params=pltpu.CompilerParams(collective_id=1, has_side_effects=True),
        name="token_stats",
    )(part)


def maps_back_kernel(dbc, zin, bc_in, conv, gbc, acc, mine, slots, ext, send, recv):
    net = Net(send, recv)
    peers = [("z", 1), ("z", -1), ("z", 2)]
    net.barrier(peers)
    z = net.at["z"]
    mine[0:LEN, :] = dbc[...]
    mine[LEN : LEN + 16, :] = jnp.zeros((16, 256), BF16)
    for axis, step in peers:
        net.start(rows(mine, net.near("z", step) * 256, 272), slots.at[z], axis, step)
    slots[z] = mine[pl.ds(pl.multiple_of(z * 256, 16), 272), :]
    net.finish()
    total = (slots[0].astype(F32) + slots[1].astype(F32)) + (slots[2].astype(F32) + slots[3].astype(F32))
    zv = zin[...]
    sig = sigmoid(zv)
    dz = total * (sig * (1.0 + zv * (1.0 - sig)))
    live = iota((272, 256), 0) + z * 256 < LEN
    ext[...] = jnp.where(live, dz, 0.0)
    xi = bc_in[...]
    out = jnp.zeros((256, 256), F32)
    acc[...] = jnp.zeros_like(acc)
    for j in range(4):
        moved = ext[3 - j : 3 - j + 256, :]
        out = out + conv[j : j + 1, :] * moved
        acc[j : j + 1, :] = jnp.sum(xi * moved, axis=0, keepdims=True)
    acc[4:5, :] = jnp.sum(ext[0:256, :], axis=0, keepdims=True)
    gbc[...] = out.astype(BF16)


def run_maps_back(dbc, zin, bc_in, conv):
    vmem = pl.BlockSpec(memory_space=pltpu.VMEM)
    return pl.pallas_call(
        maps_back_kernel,
        out_shape=[jax.ShapeDtypeStruct((256, 256), BF16), jax.ShapeDtypeStruct((8, 256), F32)],
        in_specs=[vmem] * 4,
        out_specs=[vmem] * 2,
        scratch_shapes=[pltpu.VMEM((LEN + 16, 256), BF16), pltpu.VMEM((4, 272, 256), BF16), pltpu.VMEM((272, 256), F32)] + sems(3),
        compiler_params=pltpu.CompilerParams(collective_id=2, has_side_effects=True, vmem_limit_bytes=16 * 2**20),
        name="state_maps_back",
    )(dbc, zin, bc_in, conv)


def scatter_kernel(gn, dcat, dout, dsm, small, gn_out, cat_out, out_out, bc_out, step_out, small_out, ra, rb, rc, hcat, hout, hsm, gz, fa, fb, fc, s1a, s1b, s1c, s2a, s2b, s2c, e1a, e1b, e1c, e2a, e2b, e2c, gh, ge, sp0, sp1, sp2, sp3, bz, by, send, recv):
    net = Net(send, recv)
    at = net.at
    yh, yl, cx, cc, z, y = at["yh"], at["yl"], at["x"], at["c"], at["z"], at["y"]
    near = net.near
    net.barrier([("z", 1), ("z", -1), ("z", 2), ("x", 1), ("x", -1), ("x", 2), ("y", 1), ("y", -1), ("y", 2), ("c", 1)])
    cross = []
    for src, dst in ((dcat, ra), (dout, rb), (dsm, rc)):
        cross.append(net.start(src.at[:, :, 1 - cc], dst, "c"))
    far = near("z", 2) * 256
    g1 = [net.start(rows(gn, far + 128 * part, 128), gh.at[part], "z", step) for part, step in ((0, 1), (1, -1))]
    sp0[z] = small[32:48, :]
    q = [net.start(small.at[pl.ds(32, 16)], sp0.at[z], "z", step) for step in (1, -1, 2)]
    cross[0].arrived()
    hcat[...] = dcat[:, :, cc] + ra[...]
    fary = near("y", 2)

    def ycut(ref, owner, n, part=None):
        cut = pl.ds(0, 96) if part is None else pl.ds(48 * part, 48)
        return ref.at[lax.rem(owner, 2), :, cut, pl.ds(pl.multiple_of((owner // 2) * n, 128), n)]

    def xcut(ref, owner, part=None):
        cut = pl.ds(0, 96) if part is None else pl.ds(48 * part, 48)
        return ref.at[:, owner, cut, :]

    a1 = [net.start(ycut(hcat, fary, 768, part), s1a.at[part], "y", step) for part, step in ((0, 1), (1, -1))]
    cross[1].arrived()
    hout[...] = dout[:, :, cc] + rb[...]
    farx = near("x", 2)
    b1 = [net.start(xcut(hout, farx, part), s1b.at[part], "x", step) for part, step in ((0, 1), (1, -1))]
    cross[2].arrived()
    hsm[...] = dsm[:, :, cc] + rc[...]
    c1 = [net.start(xcut(hsm, farx, part), s1c.at[part], "x", step) for part, step in ((0, 1), (1, -1))]
    for copy in q:
        copy.arrived()
    sp1[cx, 0:32, :] = small[0:32, :]
    sp1[cx, 32:48, :] = (sp0[0] + sp0[1]) + (sp0[2] + sp0[3])
    q = [net.start(sp1.at[cx], sp1.at[cx], "x", step) for step in (1, -1, 2)]
    a2, b2, c2, g2 = [], [], [], []
    for (part, step), copy in zip(((0, 1), (1, -1)), g1):
        copy.arrived()
        block = near("z", step) * 256
        gz[part] = gn[pl.ds(pl.multiple_of(block, 16), 256), :]
        gz[part, 128 * part : 128 * part + 128, :] += gh[part]
        g2.append(net.start(gz.at[part], ge.at[part], "z", step))
    for (part, step), copy in zip(((0, 1), (1, -1)), a1):
        copy.arrived()
        owner = near("y", step)
        fa[part] = hcat[lax.rem(owner, 2), :, :, pl.ds(pl.multiple_of((owner // 2) * 768, 128), 768)]
        fa[part, :, 48 * part : 48 * part + 48, :] += s1a[part]
        a2.append(net.start(fa.at[part], s2a.at[part], "y", step))
    for first, held, fold, got, nxt, out in ((b1, hout, fb, s1b, s2b, b2), (c1, hsm, fc, s1c, s2c, c2)):
        for (part, step), copy in zip(((0, 1), (1, -1)), first):
            copy.arrived()
            fold[part] = held[:, near("x", step)]
            fold[part, :, 48 * part : 48 * part + 48, :] += got[part]
            out.append(net.start(fold.at[part], nxt.at[part], "x", step))
    for copy in q:
        copy.arrived()
    sp2[y] = (sp1[0] + sp1[1]) + (sp1[2] + sp1[3])
    q = [net.start(sp2.at[y], sp2.at[y], "y", step) for step in (1, -1, 2)]
    for copy in a2 + b2 + c2:
        copy.arrived()
    own = hcat[yl, :, :, pl.ds(pl.multiple_of(yh * 768, 128), 768)]
    e1a[...] = (own.astype(F32) + s2a[0].astype(F32) + s2a[1].astype(F32)).astype(BF16)
    e1b[...] = (hout[:, cx].astype(F32) + s2b[0].astype(F32) + s2b[1].astype(F32)).astype(BF16)
    e1c[...] = (hsm[:, cx].astype(F32) + s2c[0].astype(F32) + s2c[1].astype(F32)).astype(BF16)

    def ypart(ref, owner, n, part=None):
        cut = pl.ds(0, 96) if part is None else pl.ds(48 * part, 48)
        return ref.at[lax.rem(owner, 2), cut, pl.ds(pl.multiple_of((owner // 2) * n, 128), n)]

    def xpart(ref, owner, part):
        return ref.at[owner, pl.ds(48 * part, 48)]

    pa = [net.start(xpart(e1a, farx, part), e2a.at[2 + part, pl.ds(0, 48)], "x", step) for part, step in ((0, 1), (1, -1))]
    pb = [net.start(ypart(e1b, fary, 384, part), e2b.at[2 + part, pl.ds(0, 48)], "y", step) for part, step in ((0, 1), (1, -1))]
    pc = [net.start(ypart(e1c, fary, 256, part), e2c.at[2 + part, pl.ds(0, 48)], "y", step) for part, step in ((0, 1), (1, -1))]
    for copy in q:
        copy.arrived()
    sp3[cc] = (sp2[0] + sp2[1]) + (sp2[2] + sp2[3])
    q = [net.start(sp3.at[cc], sp3.at[cc], "c")]
    la, lb, lc = [], [], []
    for (part, step), copy in zip(((0, 1), (1, -1)), pa):
        copy.arrived()
        a2[part].left()
        fa[part, 0] = e1a[near("x", step)]
        fa[part, 0, 48 * part : 48 * part + 48, :] += e2a[2 + part, 0:48, :]
        la.append(net.start(fa.at[part, 0], e2a.at[part], "x", step))
    for first, held, fold, n, land, prev, out in ((pb, e1b, fb, 384, e2b, b2, lb), (pc, e1c, fc, 256, e2c, c2, lc)):
        for (part, step), copy in zip(((0, 1), (1, -1)), first):
            copy.arrived()
            owner = near("y", step)
            prev[part].left()
            fold[part, 0, :, 0:n] = held[lax.rem(owner, 2), :, pl.ds(pl.multiple_of((owner // 2) * n, 128), n)]
            fold[part, 0, 48 * part : 48 * part + 48, 0:n] += land[2 + part, 0:48, :]
            out.append(net.start(fold.at[part, 0, :, pl.ds(0, n)], land.at[part], "y", step))
    for copy in g2:
        copy.arrived()
    gn_out[...] = gn[pl.ds(pl.multiple_of(z * 256, 16), 256), :].astype(F32) + ge[0].astype(F32) + ge[1].astype(F32)
    for copy in q:
        copy.arrived()
    small_out[...] = sp3[0] + sp3[1]
    for copy in lc:
        copy.arrived()
    mine = e1c[yl, :, pl.ds(pl.multiple_of(yh * 256, 128), 256)]
    sm = mine.astype(F32) + e2c[0].astype(F32) + e2c[1].astype(F32)
    step_out[...] = sm[:, 128:]
    bz[z] = sm[:, :128]
    q = [net.start(bz.at[z], bz.at[z], "z", step) for step in (1, -1, 2)]
    for copy in lb:
        copy.arrived()
    mine = e1b[yl, :, pl.ds(pl.multiple_of(yh * 384, 128), 384)]
    out_out[...] = mine.astype(F32) + e2b[0].astype(F32) + e2b[1].astype(F32)
    for copy in la:
        copy.arrived()
    cat_out[...] = e1a[cx].astype(F32) + e2a[0].astype(F32) + e2a[1].astype(F32)
    for copy in q:
        copy.arrived()
    by[yh] = (bz[0] + bz[1]) + (bz[2] + bz[3])
    net.start(by.at[yh], by.at[yh], "y", 2).arrived()
    bc_out[:, :128] = by[0]
    bc_out[:, 128:] = by[1]
    net.finish()


def run_scatter(gn, dcat, dout, dsm, small):
    shape = jax.ShapeDtypeStruct
    vmem = pl.BlockSpec(memory_space=pltpu.VMEM)
    bf = lambda *s: pltpu.VMEM(s, BF16)
    f32 = lambda *s: pltpu.VMEM(s, F32)
    widths = (1536, 768, 512)
    scratch = [bf(2, 4, 96, n) for n in widths]
    scratch += [bf(2, 4, 96, n) for n in widths]
    scratch += [bf(2, 256, D)]
    scratch += [bf(2, 4, 96, 768), bf(2, 2, 96, 768), bf(2, 2, 96, 512)]
    scratch += [bf(2, 4, 48, 768), bf(2, 2, 48, 768), bf(2, 2, 48, 512)]
    scratch += [bf(2, 4, 96, 768), bf(2, 2, 96, 768), bf(2, 2, 96, 512)]
    scratch += [bf(4, 96, 768), bf(2, 96, 768), bf(2, 96, 512)]
    scratch += [bf(4, 96, 768), bf(4, 96, 384), bf(4, 96, 256)]
    scratch += [bf(2, 128, D), bf(2, 256, D)]
    scratch += [f32(4, 16, COLS), f32(4, 48, COLS), f32(4, 48, COLS), f32(2, 48, COLS)]
    scratch += [f32(4, 96, 128), f32(2, 96, 128)]
    return pl.pallas_call(
        scatter_kernel,
        out_shape=[
            shape((256, D), F32),
            shape((96, 768), F32),
            shape((96, 384), F32),
            shape((96, 256), F32),
            shape((96, 128), F32),
            shape((48, COLS), F32),
        ],
        in_specs=[vmem] * 5,
        out_specs=[vmem] * 6,
        scratch_shapes=scratch + sems(48),
        compiler_params=pltpu.CompilerParams(collective_id=3, has_side_effects=True, vmem_limit_bytes=56 * 2**20),
        name="scatter_all",
    )(gn, dcat, dout, dsm, small)


def ring_scatter(blocks, z):
    ahead = [(i, (i + 1) % 4) for i in range(4)]
    back = [(i, (i + 3) % 4) for i in range(4)]
    pick = lambda step: lax.dynamic_index_in_dim(blocks, lax.rem(z + step, 4), 0, keepdims=False)
    far = pick(2)
    first = lax.ppermute(far[:128], "z", ahead)
    second = lax.ppermute(far[128:], "z", back)
    right, left = pick(1), pick(3)
    right = jnp.concatenate([right[:128] + first, right[128:]], axis=0)
    left = jnp.concatenate([left[:128], left[128:] + second], axis=0)
    from_left = lax.ppermute(right, "z", ahead)
    from_right = lax.ppermute(left, "z", back)
    return pick(0).astype(F32) + from_left.astype(F32) + from_right.astype(F32)


def shards(tokens, norm_gain, w_gate, w_inner, w_bc, w_step, conv_inner, bias_inner, conv_bc, bias_bc, step_bias, decay_log, skip_gain, gate_gain, w_out, cotangent):
    z, yh = lax.axis_index("z"), lax.axis_index("yh")
    pad = lambda v, n: jnp.pad(v, ((0, 0), (0, n - v.shape[1])))
    head_row = lambda v: pad(v[None], COLS)
    pk = jnp.concatenate(
        [
            conv_inner,
            bias_inner[None],
            gate_gain[None],
            head_row(step_bias),
            head_row(decay_log),
            head_row(skip_gain),
            jnp.repeat(skip_gain, 64)[None],
            jnp.zeros((6, COLS), F32),
        ],
        axis=0,
    )
    wa = jnp.concatenate([w_gate, w_inner], axis=1)
    ws = jnp.concatenate([lax.dynamic_slice_in_dim(w_bc, yh * 128, 128, 1), pad(w_step, 128)], axis=1)
    normed_all, cot_all, wcat, wout, wsm, prm = run_gather(tokens, cotangent, norm_gain[None], wa, w_out, ws, pk)
    wcat, wout, wsm = wcat.reshape(D, 1536), wout.reshape(D, 768), wsm.reshape(D, 512)
    bc_in, z_bc, bc, s, st, dt, r, rt, u = run_maps(normed_all, wsm, prm, conv_bc, bias_bc[None])
    gate, inner, zs, y, gp, h, ss = run_fwd(normed_all, wcat, prm, bc, s, dt, r, rt)
    gain = prm[:, 5].reshape(-1)
    gm = dot(cot_all, wout)
    part = jnp.concatenate([jnp.sum(ss, axis=1).reshape(8, 128), jnp.sum(gm * gain * gp, axis=1).reshape(8, 128)], axis=0)
    stats = run_stats(part)
    root = lax.rsqrt(stats[:8].reshape(LEN, 1) / INNER + EPS)
    cross = root * root * root * (stats[8:].reshape(LEN, 1) / INNER)
    mixed = (gp * root * gain).astype(BF16)
    branch = ring_scatter(dot_nt(mixed, wout).astype(BF16).reshape(4, 256, D), z)
    residual = tokens.astype(F32)
    output = (residual + branch).astype(BF16)
    dout = dot_tn(cot_all, mixed).astype(BF16)
    cat, gstep, dbc, acc = run_bwd(gm, gate, inner, zs, y, h, prm, bc, st, dt, r, rt, u, root, cross)
    own = lambda v, n: lax.dynamic_slice_in_dim(v, z * 256, n, 0)
    z_own = lax.dynamic_slice_in_dim(jnp.pad(z_bc, ((0, 16), (0, 0))), z * 256, 272, 0)
    gbc, bc_acc = run_maps_back(dbc, z_own, own(bc_in, 256), conv_bc)
    dcat = dot_tn(normed_all, cat).astype(BF16)
    gsteps = jnp.concatenate([gstep[0], gstep[1]], axis=1)
    wsteps = jnp.concatenate([wsm[:, 128:256], wsm[:, 384:]], axis=1)
    gn32 = dot_nt(cat, wcat) + dot_nt(gsteps, wsteps)
    dstep = dot_tn(normed_all, gsteps)
    dbcw = dot_tn(own(normed_all, 256), gbc)
    dsm = jnp.concatenate([dbcw[:, :128], dstep[:, :128], dbcw[:, 128:], dstep[:, 128:]], axis=1).astype(BF16)
    wbc = jnp.concatenate([wsm[:, :128], wsm[:, 256:384]], axis=1)
    gn_bc = dot_nt(gbc, wbc)
    norm_part = (
        jnp.sum(gn32 * normed_all.astype(F32), axis=0) + jnp.sum(gn_bc * own(normed_all, 256).astype(F32), axis=0)
    ) / norm_gain
    small = jnp.concatenate(
        [acc.reshape(32, COLS), norm_part.reshape(4, COLS), pad(bc_acc, COLS), jnp.zeros((4, COLS), F32)], axis=0
    )
    gn_own, cat_g, out_g, bc_g, step_g, sums = run_scatter(
        gn32.astype(BF16), dcat.reshape(2, 4, 2, 96, 1536), dout.reshape(2, 4, 2, 96, 768), dsm.reshape(2, 4, 2, 96, 512), small
    )
    grad_normed = gn_own + gn_bc
    inv_root = lax.rsqrt(jnp.mean(residual * residual, axis=1, keepdims=True) + EPS)
    scaled = grad_normed * norm_gain
    tokens_grad = (
        cotangent.astype(F32)
        + inv_root * scaled
        - residual * (inv_root * inv_root * inv_root) * jnp.mean(scaled * residual, axis=1, keepdims=True)
    )
    mine = lax.dynamic_slice_in_dim(sums, yh * 16, 16, 0)
    return (
        output,
        tokens_grad,
        sums[32:36].reshape(-1),
        cat_g[:, :COLS],
        cat_g[:, COLS:],
        bc_g,
        step_g[:, :HEADS],
        mine[0:4],
        mine[4],
        sums[36:40, :256],
        sums[40, :256],
        mine[6, :HEADS],
        mine[7, :HEADS],
        jnp.sum(mine[9].reshape(HEADS, 64), axis=1),
        mine[5],
        out_g,
    )


def solution(mesh):
    fine = Mesh(mesh.devices.reshape(2, 4, 2, 2, 4), AXES)
    dp, tensor = ("yl", "x", "c"), ("yh", "z")
    tokens, weight = P(dp + tensor, None), P(dp, tensor)
    return jax.shard_map(
        shards,
        mesh=fine,
        in_specs=(
            tokens,
            P(),
            weight,
            weight,
            P(dp, None),
            weight,
            P(None, tensor),
            P(tensor),
            P(),
            P(),
            P(tensor),
            P(tensor),
            P(tensor),
            P(tensor),
            weight,
            tokens,
        ),
        out_specs=(
            tokens,
            tokens,
            P(),
            weight,
            weight,
            P(dp, None),
            weight,
            P(None, tensor),
            P(tensor),
            P(),
            P(),
            P(tensor),
            P(tensor),
            P(tensor),
            P(tensor),
            weight,
        ),
        check_vma=False,
    )
```

time: 1150 us -> 315 us (0.27); the launches traced: 1140 us -> 314 us
  waiting for transfers between devices: 428 us -> 8.59 us
  blocking collectives: 208 us -> 0 us
  Pallas kernels: 0 us -> 189 us
  other arithmetic: 206 us -> 18.3 us
  matrix products: 157 us -> 42.6 us
  local copies, waits for them, and re-layouts: 121 us -> 48.8 us
  between operations: 15.4 us -> 1.17 us
    unnamed x17 -> x0, waiting for transfers between devices: 195 us -> none
    pallas_call x0 -> x7, Pallas kernels: none -> 189 us  [the longest x1 61.1 us: run_gather(): pl.pallas_call(gather_kernel, out_shape=[shape((LEN, D), BF16), shape((LE...]
    psum x4 -> x0, blocking collectives: 170 us -> none  [the longest x1 74 us: shards(): norm_gain_sum = lax.psum(grad_norm_part, ('dp', 'tensor'))]
    reduce_scatter x3 -> x0, waiting for transfers between devices: 123 us -> none  [the longest x1 64.1 us: shards(): lax.psum_scatter(grad_bc_w, 'dp', scatter_dimension=0, tiled=True)]
    dot_general x20 -> x9, matrix products: 157 us -> 42.6 us  [the longest x4 19.9 us: dot_nt(): lax.dot_general(a, b, (((1,), (1,)), ((), ())), preferred_element_type=F32)]
    all_gather x5 -> x0, waiting for transfers between devices: 110 us -> none  [the longest x1 85.8 us: shards(): normed_all = lax.all_gather(normed, 'tensor', axis=0, tiled=True)]
    another operation x8 -> x0, other arithmetic: 94.5 us -> none
    reduce_sum x13 -> x3, other arithmetic: 48.4 us -> 3.85 us  [the longest x1 1.97 us: shards(): jnp.mean(residual * residual, axis=1, keepdims=True) + EPS]
  transfers between devices with their start and end apart: 13 -> 4, of which waited for: 8 -> 2; matrix products, arithmetic and copies ran while one was open for 32% -> 17% of each run, Pallas kernels for 0% -> 29%
where the time goes in v1:
time: 315 us; the launch traced here: 314 us
  Pallas kernels  189 us (60%)
  local copies, waits for them, and re-layouts  48.8 us (15%)
  matrix products  42.6 us (14%)
  other arithmetic  18.3 us (6%)
  waiting for transfers between devices  8.59 us (3%)
  starting transfers between devices  5.58 us (2%)
    pallas_call x1, Pallas kernels, run_gather(): pl.pallas_call(gather_kernel, out_shape=[shape((LEN, D), BF16), shape((LE...  61.1 us
    pallas_call x1, Pallas kernels, run_scatter(): pl.pallas_call(scatter_kernel, out_shape=[shape((256, D), F32), shape((96...  54 us
    pallas_call x1, Pallas kernels, run_bwd(): pl.pallas_call(bwd_kernel, grid=(BLOCKS, GROUPS), out_shape=[shape((LEN,...  29.2 us
    unnamed x114, local copies, waits for them, and re-layouts  24.6 us
    pallas_call x1, Pallas kernels, run_fwd(): pl.pallas_call(fwd_kernel, grid=(BLOCKS, GROUPS), out_shape=[wide, wide,...  23.3 us
    dot_general x4, matrix products, dot_nt(): lax.dot_general(a, b, (((1,), (1,)), ((), ())), preferred_element_type=F32)  19.9 us
    dot_general x4, matrix products, dot_tn(): lax.dot_general(a, b, (((0,), (0,)), ((), ())), preferred_element_type=F32)  14.6 us
    pallas_call x1, Pallas kernels, run_maps_back(): pl.pallas_call(maps_back_kernel, out_shape=[jax.ShapeDtypeStruct((256, 25...  8.93 us
  transfers between devices with their start and end apart: 4, of which 2 were waited for; matrix products, arithmetic and copies ran while one was open for 17% of the time, Pallas kernels for 29%

profile of v1, /device:TPU:0, one launch (start us, length us, event | category | flops | bytes accessed | tf_op | source)
XLA Modules:
  0.0 313.9 jit_solution(17751590677996462374)
XLA Ops:
  4.0 0.7 broadcast_in_dim.39
  4.8 0.7 broadcast_in_dim.33.gain
  5.5 0.8 copy.45
  6.4 0.9 pad_maximum_fusion.6.wa
  7.3 0.7 concatenate.45.pk
  8.1 1.1 copy-done.4
  9.2 1.1 copy-done.9
  10.3 0.9 copy-done.17
  11.2 61.1 %gather_all.1 = (bf16[1024,1536]{1,0:T(8,128)(2,1)S(1)}, bf16[1024,1536]{1,0:T(8,128)(2,1)S(1)}, bf16[2,4,2,96,1536]{4,3,2,1,0:T(8,128)(2,1)S(1)}, bf16[2,4,2,96...) custom-call(bf16[256,1536]{1,0:T(8,128)(2,1)S(1)} %copy-done.4, ...), custom_call_target="tpu_custom_call" | custom-call | tf_op jit(solution)/shard_map/gather_all/pallas_call | solution.py:584
  72.4 1.1 copy-done.6
  73.5 2.2 copy-done.22
  75.7 1.6 copy-done.23
  77.3 1.4 copy-done.25
  78.8 2.5 copy-done.7
  82.6 5.6 %state_maps.1 = (f32[1024,256]{1,0:T(8,128)S(1)}, f32[1024,256]{1,0:T(8,128)S(1)}, bf16[1024,256]{1,0:T(8,128)(2,1)S(1)}, f32[4,256,256]{2,1,0:T(8,128)S(1)}, f3...) custom-call(bf16[1024,1536]{1,0:T(8,128)(2,1)S(1)} %get-tuple-elemen, ...), custom_call_target="tpu_custom_call" | custom-call | tf_op jit(solution)/shard_map/state_maps/pallas_call | solution.py:130
  88.3 1.0 copy-done.11
  89.2 1.0 copy-done.18
  90.2 1.0 copy-done.27
  91.2 1.0 copy-done.33
  92.2 23.3 %scan_forward.1 = (f32[1024,768]{1,0:T(8,128)}, f32[1024,768]{1,0:T(8,128)}, f32[1024,768]{1,0:T(8,128)}, f32[1024,768]{1,0:T(8,128)}, f32[1024,768]{1,0:T(8,128...) custom-call(bf16[1024,1536]{1,0:T(8,128)(2,1)} %copy-done.2, bf16[1536,1536]{1,0:T(8,128)(2,1)} %bitcast.65, ...), custom_call_target="tpu_custom_call" | custom-call | flops 17179869184 | bytes 41943040 | tf_op jit(solution)/shard_map/scan_forward/pallas_call | solution.py:214
  115.5 0.8 copy-done.13
  116.3 1.1 copy-done.36
  117.4 1.2 reduce_sum.63
  118.7 8.1 %multiply_reduce_fusion.1 = (f32[1024]{0:T(1024)S(1)}, f32[1024,768]{1,0:T(8,128)}) fusion(f32[1024,768]{1,0:T(8,128)} %get-tuple-element.59, f32[768]{0:T(1024)S(1)} %mul.125, bf16[1024,1536]{1,0:T(8,128)(2,1)} %copy-done.23, bf16[1536,768]{1,0:T(8,128)(2,1)} %bitcast.69), kind=kOutput, calls=%fused_computation.6 | convolution fusion | flops 2418277376 | bytes 11803648 | tf_op jit(solution)/shard_map/dot_general | solution.py:30
  127.4 6.6 %token_stats.1 = f32[16,128]{1,0:T(8,128)} custom-call(f32[16,128]{1,0:T(8,128)} %pad_maximum_fusion.7.part), custom_call_target="tpu_custom_call" | custom-call | tf_op jit(solution)/shard_map/token_stats/pallas_call | solution.py:615
  134.7 6.0 %convolution_convert_fusion.1 = bf16[1024,1536]{1,0:T(8,128)(2,1)} fusion(bf16[1536,768]{1,0:T(8,128)(2,1)S(1)} %bitcast.70, f32[1024,768]{1,0:T(8,128)} %get-tuple-element.59, f32[1024]{0:T(1024)S(1)} %get-tuple-element.164, f32[768]{0:T(1024)S(1)} %mul.125), kind=kOutput, calls=%fused_computation.3 | convolution fusion | flops 2419851264 | bytes 8657920 | tf_op jit(solution)/shard_map/dot_general | solution.py:34
  140.7 2.7 dynamic-slice_bitcast_fusion.4
  143.3 1.1 collective-permute-start
  144.4 2.1 collective-permute-start.2
  146.6 1.3 fusion.30
  147.9 1.2 copy-done.24
  149.0 6.2 %convolution_convert_fusion.2 = bf16[1536,768]{1,0:T(8,128)(2,1)} fusion(bf16[1024,1536]{1,0:T(8,128)(2,1)S(1)} %copy-done.24, f32[1024,768]{1,0:T(8,128)} %get-tuple-element.59, f32[1024]{0:T(1024)S(1)} %get-tuple-element.164, f32[768]{0:T(1024)S(1)} %mul.125), kind=kOutput, calls=%fused_computation.4 | convolution fusion | flops 2419458048 | bytes 8657920 | tf_op jit(solution)/shard_map/dot_general | solution.py:38
  155.5 1.0 copy.47
  156.5 1.0 copy.49
  157.5 1.4 multiply_multiply_fusion.cross
  159.0 1.3 copy-done.32
  160.3 29.2 %scan_backward.1 = (bf16[1024,1536]{1,0:T(8,128)(2,1)}, bf16[2,1024,128]{2,1,0:T(8,128)(2,1)S(1)}, bf16[1024,256]{1,0:T(8,128)(2,1)S(1)}, f32[2,16,384]{2,1,0:T(8,128)S(1)}) custom-call(f32[1024,768]{1,0:T(8,128)} %get-tuple-element.169.gm, f32[1024,768]{1,0:T(8,128)} %get-tuple-element.63.gate, f32[1024,768]{1,0:T(8,128)} %get-tuple-element.64.inner, ...), custom_call_target="tpu_custom_call" | custom-call | flops 17179869184 | bytes 41943040 | tf_op jit(solution)/shard_map/scan_backward/pallas_call | solution.py:356
  189.6 9.3 %fusion.34 = f32[1024,1536]{1,0:T(8,128)} fusion(bf16[1024,1536]{1,0:T(8,128)(2,1)} %get-tuple-element.70, bf16[1536,1536]{1,0:T(8,128)(2,1)S(1)} %bitcast.68), kind=kOutput, calls=%fused_computation.85 | convolution fusion | flops 4831838208 | bytes 14155776 | tf_op jit(solution)/shard_map/dot_general | solution.py:34
  199.0 7.0 %convolution_convert_fusion = bf16[1536,1536]{1,0:T(8,128)(2,1)} fusion(bf16[1024,1536]{1,0:T(8,128)(2,1)S(1)} %copy-done.3, bf16[1024,1536]{1,0:T(8,128)(2,1)S(1)} %copy-done.50), kind=kOutput, calls=%fused_computation | convolution fusion | flops 4834197504 | bytes 11010048 | tf_op jit(solution)/shard_map/dot_general | solution.py:38
  205.9 1.1 slice_bitcast_fusion.1
  207.0 1.0 convolution_convert_fusion.4
  208.1 1.0 fusion.32
  209.1 1.1 constant_dynamic-slice_fusion.6.bc_in
  210.3 8.9 %state_maps_back.1 = (bf16[256,256]{1,0:T(8,128)(2,1)S(1)}, f32[8,256]{1,0:T(8,128)S(1)}) custom-call(bf16[1024,256]{1,0:T(8,128)(2,1)S(1)} %copy-done.15, f32[272,256]{1,0:T(8,128)S(1)} %pad_dynamic-slice_fusion.zin, f32[256,256]{1,0:T(8,128)S(1)} %constant_dynamic-slice_fusion.6.bc_in, f32[4,256]{1,0:T(4,128)S(1)} %copy-done.20), custom_call_target="tpu_custom_call" | custom-call | tf_op jit(solution)/shard_map/state_maps_back/pallas_call | solution.py:656
  219.7 1.0 fusion.31
  220.6 1.6 multiply_reduce_fusion.2
  222.2 3.0 multiply_reduce_fusion
  225.3 0.7 fusion.17.small
  226.1 2.7 pad_maximum_fusion.dsm
  228.8 54.0 %scatter_all.1 = (f32[256,1536]{1,0:T(8,128)}, f32[96,768]{1,0:T(8,128)}, f32[96,384]{1,0:T(8,128)}, f32[96,256]{1,0:T(8,128)}, f32[96,128]{1,0:T(8,128)}, /*index=5*/f32[48,384]{1,0:T(8,128)}) custom-call(bf16[1024,1536]{1,0:T(8,128)(2,1)} %get-tuple-element.138.gn, bf16[2,4,2,96,1536]{4,3,2,1,0:T(8,128)(2,1)} %bitcast.73, ...), custom_call_target="tpu_custom_call" | custom-call | tf_op jit(solution)/shard_map/scatter_all/pallas_call | solution.py:810
  282.9 1.5 constant_dynamic-slice_fusion.2
  284.3 1.5 fusion.15
  285.9 0.9 pad_maximum_fusion.2
  286.8 2.3 collective-permute-start.3
  289.2 0.9 pad_maximum_fusion.1
  290.1 1.3 fusion.24
  291.4 1.3 slice.147
  292.6 1.3 slice.146
  294.6 1.4 fusion.21
  297.3 2.0 fusion.1
  299.3 0.7 fusion.33
  300.0 4.2 %collective-permute-done.3 = bf16[256,1536]{1,0:T(8,128)(2,1)} collective-permute-done((bf16[256,1536]{1,0:T(8,128)(2,1)}, bf16[256,1536]{1,0:T(8,128)(2,1)}, u32[]{:S(2)}, u32[]{:S(2)}) %collective-permute-start.3) | collective-permute-done | bytes 786464 | tf_op jit(solution)/shard_map/ppermute | solution.py:839
  304.3 4.3 %collective-permute-done.1 = bf16[256,1536]{1,0:T(8,128)(2,1)} collective-permute-done((bf16[256,1536]{1,0:T(8,128)(2,1)}, bf16[256,1536]{1,0:T(8,128)(2,1)}, u32[]{:S(2)}, u32[]{:S(2)}) %collective-permute-start.1) | collective-permute-done | bytes 786464 | tf_op jit(solution)/shard_map/ppermute | solution.py:838
  308.6 4.0 %fusion.3 = (f32[256,1536]{1,0:T(8,128)}, bf16[256,1536]{1,0:T(8,128)(2,1)}) fusion(bf16[256,1536]{1,0:T(8,128)(2,1)S(1)} %copy-done.5, bf16[256,1536]{1,0:T(8,128)(2,1)S(1)} %copy-done.10, f32[256]{0:T(256)S(1)} %get-tuple-element.173, f32[256]{0:T(256)S(1)} %get-tuple-element.167, f32[256]{0:T(256)S(1)} %get-tuple-element.166, f32[1536]{0:T(1024)S(1)} %copy-done.47, ...), kind=kLoop, calls=%fused_computation.16 | loop fusion | flops 6291456 | bytes 9446404 | tf_op jit(solution)/shard_map/sub | solution.py:903
  (127 shorter events, 10.4 us)
Async XLA Ops:
  0.6 5.7 %copy-start = (bf16[96,256]{1,0:T(8,128)(2,1)S(1)}, bf16[96,256]{1,0:T(8,128)(2,1)}, u32[]{:S(2)}) copy-start(bf16[96,256]{1,0:T(8,128)(2,1)} %param.20) | copy-start | bytes 147460
  8.1 1.1 copy-start.4
  9.2 1.1 copy-start.9
  10.3 0.9 copy-start.17
  72.4 1.1 copy-start.6
  73.5 2.2 copy-start.22
  75.7 1.6 copy-start.23
  77.3 1.4 copy-start.25
  78.7 13.5 %copy-start.2 = (bf16[1024,1536]{1,0:T(8,128)(2,1)}, bf16[1024,1536]{1,0:T(8,128)(2,1)S(1)}, u32[]{:S(2)}) copy-start(bf16[1024,1536]{1,0:T(8,128)(2,1)S(1)} %get-tuple-element.50.normed) | copy-start | bytes 9437188
  78.7 2.5 copy-start.7
  81.3 0.7 copy-start.19
  82.0 0.7 copy-start.21
  88.2 1.0 copy-start.11
  89.2 1.0 copy-start.18
  90.2 1.0 copy-start.27
  91.2 1.0 copy-start.33
  92.2 23.3 %copy-start.29 = (f32[2,1024,128]{2,1,0:T(8,128)}, f32[2,1024,128]{2,1,0:T(8,128)S(1)}, u32[]{:S(2)}) copy-start(f32[2,1024,128]{2,1,0:T(8,128)S(1)} %get-tuple-element.56.dt) | copy-start | bytes 3145732
  92.2 23.3 %copy-start.31 = (f32[2,1024,128]{2,1,0:T(8,128)}, f32[2,1024,128]{2,1,0:T(8,128)S(1)}, u32[]{:S(2)}) copy-start(f32[2,1024,128]{2,1,0:T(8,128)S(1)} %get-tuple-element.57.r) | copy-start | bytes 3145732
  92.2 23.3 %copy-start.34 = (bf16[1024,256]{1,0:T(8,128)(2,1)}, bf16[1024,256]{1,0:T(8,128)(2,1)S(1)}, u32[]{:S(2)}) copy-start(bf16[1024,256]{1,0:T(8,128)(2,1)S(1)} %get-tuple-element.54.bc) | copy-start | bytes 1572868
  115.5 0.8 copy-start.13
  116.3 1.1 copy-start.36
  118.7 16.0 %copy-start.26 = (bf16[2,4,2,96,768]{4,3,2,1,0:T(8,128)(2,1)S(1)}, bf16[2,4,2,96,768]{4,3,2,1,0:T(8,128)(2,1)}, u32[]{:S(2)}) copy-start(bf16[2,4,2,96,768]{4,3,2,1,0:T(8,128)(2,1)} %copy-done.25) | copy-start | bytes 7077892
  140.7 5.9 %copy-start.8 = (bf16[2,4,2,96,512]{4,3,2,1,0:T(8,128)(2,1)S(1)}, bf16[2,4,2,96,512]{4,3,2,1,0:T(8,128)(2,1)}, u32[]{:S(2)}) copy-start(bf16[2,4,2,96,512]{4,3,2,1,0:T(8,128)(2,1)} %copy-done.6) | copy-start | bytes 4718596
  143.3 141.0 %collective-permute-start = (bf16[128,1536]{1,0:T(8,128)(2,1)}, bf16[128,1536]{1,0:T(8,128)(2,1)}, u32[]{:S(2)}, u32[]{:S(2)}) collective-permute-start(bf16[128,1536]{1,0:T(8,128)(2,1)} %get-tuple-element.141), channel_id=1, source_target_pairs={{0,1},{1,2},{2,3},{3,0},{4,5},{5,6},{6,7},{7,4},{8,9},{9,10},{10,1... | collective-permute-start | bytes 1179656 | tf_op jit(solution)/shard_map/ppermute | solution.py:833
  144.4 139.9 %collective-permute-start.2 = (bf16[128,1536]{1,0:T(8,128)(2,1)}, bf16[128,1536]{1,0:T(8,128)(2,1)}, u32[]{:S(2)}, u32[]{:S(2)}) collective-permute-start(bf16[128,1536]{1,0:T(8,128)(2,1)} %get-tuple-element.143), channel_id=1, source_target_pairs={{0,3},{1,0},{2,1},{3,2},{4,7},{5,4},{6,5},{7,6},{8,11},{9,8},{10,9... | collective-permute-start | bytes 1179656 | tf_op jit(solution)/shard_map/ppermute | solution.py:834
  146.6 2.5 copy-start.24
  149.0 9.9 %copy-start.35 = (bf16[1024,256]{1,0:T(8,128)(2,1)S(1)}, bf16[1024,256]{1,0:T(8,128)(2,1)}, u32[]{:S(2)}) copy-start(bf16[1024,256]{1,0:T(8,128)(2,1)} %copy-done.34) | copy-start | bytes 1572868
  155.2 3.8 %copy-start.28 = (f32[4,256,256]{2,1,0:T(8,128)S(1)}, f32[4,256,256]{2,1,0:T(8,128)}, u32[]{:S(2)}) copy-start(f32[4,256,256]{2,1,0:T(8,128)} %copy-done.27) | copy-start | bytes 3145732
  155.2 3.8 %copy-start.30 = (f32[2,1024,128]{2,1,0:T(8,128)S(1)}, f32[2,1024,128]{2,1,0:T(8,128)}, u32[]{:S(2)}) copy-start(f32[2,1024,128]{2,1,0:T(8,128)} %copy-done.29) | copy-start | bytes 3145732
  157.5 32.0 %slice-start = ((s8[4718592]{0:T(1024)(128)(4,1)}), s8[4194304]{0:T(1024)(128)(4,1)S(1)}, s32[]{:S(2)}) async-start(s8[4718592]{0:T(1024)(128)(4,1)} %bitcast.66), calls=%async_computation | async-start | bytes 8388608
  159.0 1.3 copy-start.32
  160.3 29.2 %slice-start.1 = ((s8[4718592]{0:T(1024)(128)(4,1)}), s8[524288]{0:T(1024)(128)(4,1)S(1)}, s32[]{:S(2)}) async-start(s8[4718592]{0:T(1024)(128)(4,1)} %bitcast.66), calls=%async_computation.1 | async-start | bytes 1048576
  189.6 9.4 %copy-start.14 = (bf16[1024,256]{1,0:T(8,128)(2,1)}, bf16[1024,256]{1,0:T(8,128)(2,1)S(1)}, u32[]{:S(2)}) copy-start(bf16[1024,256]{1,0:T(8,128)(2,1)S(1)} %get-tuple-element.72.dbc) | copy-start | bytes 1572868
  189.6 9.4 %copy-start.16 = (bf16[2,1024,128]{2,1,0:T(8,128)(2,1)}, bf16[2,1024,128]{2,1,0:T(8,128)(2,1)S(1)}, u32[]{:S(2)}) copy-start(bf16[2,1024,128]{2,1,0:T(8,128)(2,1)S(1)} %get-tuple-element.71) | copy-start | bytes 1572868
  189.6 9.3 %copy-start.3 = (bf16[1024,1536]{1,0:T(8,128)(2,1)S(1)}, bf16[1024,1536]{1,0:T(8,128)(2,1)}, u32[]{:S(2)}) copy-start(bf16[1024,1536]{1,0:T(8,128)(2,1)} %copy-done.2) | copy-start | bytes 9437188
  189.6 9.3 %copy-start.50 = (bf16[1024,1536]{1,0:T(8,128)(2,1)S(1)}, bf16[1024,1536]{1,0:T(8,128)(2,1)}, u32[]{:S(2)}) copy-start(bf16[1024,1536]{1,0:T(8,128)(2,1)} %get-tuple-element.70) | copy-start | bytes 9437188
  207.0 3.2 %copy-start.12 = (f32[1024,256]{1,0:T(8,128)S(1)}, f32[1024,256]{1,0:T(8,128)}, u32[]{:S(2)}) copy-start(f32[1024,256]{1,0:T(8,128)} %copy-done.11) | copy-start | bytes 3145732
  207.0 15.2 %slice-start.2 = ((s8[6291456]{0:T(1024)(128)(4,1)}), s8[4194304]{0:T(1024)(128)(4,1)S(1)}, s32[]{:S(2)}) async-start(s8[6291456]{0:T(1024)(128)(4,1)} %bitcast.71), calls=%async_computation.2 | async-start | bytes 8388608
  208.1 2.2 copy-start.15
  208.1 2.2 copy-start.20
  208.1 14.1 %slice-start.3 = ((s8[6291456]{0:T(1024)(128)(4,1)}), s8[2097152]{0:T(1024)(128)(4,1)S(1)}, s32[]{:S(2)}) async-start(s8[6291456]{0:T(1024)(128)(4,1)} %bitcast.71), calls=%async_computation.3 | async-start | bytes 4194304
  209.1 11.5 %copy-start.41 = (bf16[1536,128]{1,0:T(8,128)(2,1)S(1)}, bf16[1536,128]{1,0:T(8,128)(2,1)}, u32[]{:S(2)}) copy-start(bf16[1536,128]{1,0:T(8,128)(2,1)} %get-tuple-element.145) | copy-start | bytes 1179652
  209.1 11.5 %copy-start.42 = (bf16[1536,128]{1,0:T(8,128)(2,1)S(1)}, bf16[1536,128]{1,0:T(8,128)(2,1)}, u32[]{:S(2)}) copy-start(bf16[1536,128]{1,0:T(8,128)(2,1)} %get-tuple-element.146) | copy-start | bytes 1179652
  219.2 3.0 copy-start.39
  219.2 3.0 copy-start.40
  222.2 3.0 copy-start.47
  228.8 57.1 %copy-start.44 = (bf16[128,1536]{1,0:T(8,128)(2,1)S(1)}, bf16[128,1536]{1,0:T(8,128)(2,1)}, u32[]{:S(2)}) copy-start(bf16[128,1536]{1,0:T(8,128)(2,1)} %get-tuple-element.142) | copy-start | bytes 1179652
  282.8 6.4 %copy-start.43 = (bf16[128,1536]{1,0:T(8,128)(2,1)S(1)}, bf16[128,1536]{1,0:T(8,128)(2,1)}, u32[]{:S(2)}) copy-start(bf16[128,1536]{1,0:T(8,128)(2,1)} %get-tuple-element.144) | copy-start | bytes 1179652
  282.8 11.1 %copy-start.49 = (f32[96,128]{1,0:T(8,128)S(1)}, f32[96,128]{1,0:T(8,128)}, u32[]{:S(2)}) copy-start(f32[96,128]{1,0:T(8,128)} %get-tuple-element.82) | copy-start | bytes 147460
  282.8 14.5 %copy-start.5 = (bf16[256,1536]{1,0:T(8,128)(2,1)S(1)}, bf16[256,1536]{1,0:T(8,128)(2,1)}, u32[]{:S(2)}) copy-start(bf16[256,1536]{1,0:T(8,128)(2,1)} %x.13) | copy-start | bytes 2359300
  282.8 14.5 %copy-start.37 = (f32[256,1536]{1,0:T(8,128)S(1)}, f32[256,1536]{1,0:T(8,128)}, u32[]{:S(2)}) copy-start(f32[256,1536]{1,0:T(8,128)} %get-tuple-element.172) | copy-start | bytes 4718596
  286.8 12.5 %copy-start.45 = (f32[96,768]{1,0:T(8,128)S(1)}, f32[96,768]{1,0:T(8,128)}, u32[]{:S(2)}) copy-start(f32[96,768]{1,0:T(8,128)} %get-tuple-element.80) | copy-start | bytes 884740
  286.8 21.8 %copy-start.10 = (bf16[256,1536]{1,0:T(8,128)(2,1)S(1)}, bf16[256,1536]{1,0:T(8,128)(2,1)}, u32[]{:S(2)}) copy-start(bf16[256,1536]{1,0:T(8,128)(2,1)} %cot.1) | copy-start | bytes 2359300
  286.8 17.4 %collective-permute-start.3 = (bf16[256,1536]{1,0:T(8,128)(2,1)}, bf16[256,1536]{1,0:T(8,128)(2,1)}, u32[]{:S(2)}, u32[]{:S(2)}) collective-permute-start(bf16[256,1536]{1,0:T(8,128)(2,1)} %pad_maximum_fusion.2), channel_id=1, source_target_pairs={{0,3},{1,0},{2,1},{3,2},{4,7},{5,4},{6,5},{7,6},{8,11},{9,8},{10,9... | collective-permute-start | bytes 2359304 | tf_op jit(solution)/shard_map/ppermute | solution.py:839
  290.1 18.5 %collective-permute-start.1 = (bf16[256,1536]{1,0:T(8,128)(2,1)}, bf16[256,1536]{1,0:T(8,128)(2,1)}, u32[]{:S(2)}, u32[]{:S(2)}) collective-permute-start(bf16[256,1536]{1,0:T(8,128)(2,1)} %pad_maximum_fusion.1), channel_id=1, source_target_pairs={{0,1},{1,2},{2,3},{3,0},{4,5},{5,6},{6,7},{7,4},{8,9},{9,10},{10,1... | collective-permute-start | bytes 2359304 | tf_op jit(solution)/shard_map/ppermute | solution.py:838
  297.3 11.3 %copy-start.38 = (f32[256,1536]{1,0:T(8,128)S(1)}, f32[256,1536]{1,0:T(8,128)}, u32[]{:S(2)}) copy-start(f32[256,1536]{1,0:T(8,128)} %get-tuple-element.78) | copy-start | bytes 4718596
  308.6 5.3 %copy-start.1 = (bf16[96,256]{1,0:T(8,128)(2,1)S(1)}, bf16[96,256]{1,0:T(8,128)(2,1)}, u32[]{:S(2)}) copy-start(bf16[96,256]{1,0:T(8,128)(2,1)} %param.20) | copy-start | bytes 147460
  308.6 4.0 %copy-start.48 = (f32[96,256]{1,0:T(8,128)S(1)}, f32[96,256]{1,0:T(8,128)}, u32[]{:S(2)}) copy-start(f32[96,256]{1,0:T(8,128)} %get-tuple-element.195) | copy-start | bytes 294916
  308.6 4.6 %copy-start.46 = (f32[96,384]{1,0:T(8,128)S(1)}, f32[96,384]{1,0:T(8,128)}, u32[]{:S(2)}) copy-start(f32[96,384]{1,0:T(8,128)} %get-tuple-element.205) | copy-start | bytes 442372

commit v2 on v0

v2 whole, which is shorter than its diff:
```python
import jax
import jax.numpy as jnp
from jax import lax
from jax.experimental import pallas as pl
from jax.experimental.pallas import tpu as pltpu
from jax.sharding import Mesh
from jax.sharding import PartitionSpec as P

D = 1536
LEN = 1024
INNER = 3072
STATE = 128
BLOCK = 256
BLOCKS = LEN // BLOCK
GROUPS = 2
HEADS = 6
COLS = HEADS * 64
WIDE = GROUPS * COLS
STEPS = 2 * WIDE
PROJ = STEPS + GROUPS * 128
LOG2E = 1.4426950408889634
EPS = 1e-05
F32 = jnp.float32
BF16 = jnp.bfloat16
MESH = pl.DeviceIdType.MESH
AXES = ("yl", "x", "c", "yh", "z")
ANY = pl.BlockSpec(memory_space=pl.ANY)
VMEM = pl.BlockSpec(memory_space=pltpu.VMEM)
SHAPE = jax.ShapeDtypeStruct
ROOM = 60 * 2**20


def dot(a, b):
    return jnp.dot(a, b, preferred_element_type=F32)


def dot_nt(a, b):
    return lax.dot_general(a, b, (((1,), (1,)), ((), ())), preferred_element_type=F32)


def dot_tn(a, b):
    return lax.dot_general(a, b, (((0,), (0,)), ((), ())), preferred_element_type=F32)


def pieces(v, n):
    out = []
    for _ in range(n):
        hi = v.astype(BF16)
        out.append(hi)
        v = v - hi.astype(F32)
    return out


def dot_left(v, ones, n):
    return sum(dot(p, ones) for p in pieces(v, n))


def dot_right(ones, v, n):
    return sum(dot(ones, p) for p in pieces(v, n))


def iota(shape, axis):
    return lax.broadcasted_iota(jnp.int32, shape, axis)


def expander():
    row, col = iota((128, COLS), 0), iota((128, COLS), 1)
    return (row == lax.shift_right_logical(col, 6)).astype(BF16)


def reducer():
    row, col = iota((COLS, 128), 0), iota((COLS, 128), 1)
    return (col == lax.shift_right_logical(row, 6)).astype(BF16)


def sigmoid(v):
    return 1.0 / (1.0 + jnp.exp(-v))


def lower(strict=False):
    row, col = iota((BLOCK, BLOCK), 0), iota((BLOCK, BLOCK), 1)
    return ((row > col) if strict else (row >= col)).astype(BF16)


def upper():
    return (iota((BLOCK, BLOCK), 0) <= iota((BLOCK, BLOCK), 1)).astype(BF16)


def token_row(v):
    v = sum(v[:, 128 * i : 128 * (i + 1)] for i in range(v.shape[1] // 128))
    ones = jnp.ones((8, 128), BF16)
    return sum(dot_nt(ones, p) for p in pieces(v, 3))[0:1, :]


class Net:
    def __init__(self, send, recv):
        self.send, self.recv, self.copies = send, recv, []
        self.at = {name: lax.axis_index(name) for name in AXES}
        self.at["y"] = self.at["yh"] * 2 + self.at["yl"]
        self.places = {(a, s): lax.rem(self.at[a] + s + 4, 4) for a in ("x", "y", "z") for s in (1, -1, 2)}
        self.other = 1 - self.at["c"]
        self.targets = {("c", 1): {"c": self.other}}
        for (a, s), place in self.places.items():
            self.targets[a, s] = {"yh": place // 2, "yl": lax.rem(place, 2)} if a == "y" else {a: place}

    def near(self, axis, step):
        return self.places[axis, step]

    def plan(self, src, dst, axis, step=1):
        copy = Copy(self, len(self.copies), src, dst, self.targets[axis, step])
        self.copies.append(copy)
        return copy

    def start(self, src, dst, axis, step=1):
        return self.plan(lambda: src, lambda: dst, axis, step).start()

    def around(self, src, dst, axis):
        return [self.start(src, dst, axis, step) for step in (1, -1, 2)]

    def barrier(self, peers):
        here = pltpu.get_barrier_semaphore()
        for peer in peers:
            pl.semaphore_signal(here, inc=1, device_id=self.targets[peer], device_id_type=MESH)
        pl.semaphore_wait(here, len(peers))

    def finish(self):
        for copy in self.copies:
            copy.arrived()
        for copy in self.copies:
            copy.left()


class Copy:
    def __init__(self, net, index, src, dst, target):
        self.net, self.index, self.src, self.dst, self.target = net, index, src, dst, target
        self.here, self.gone = False, False

    def made(self):
        return pltpu.make_async_remote_copy(
            src_ref=self.src(),
            dst_ref=self.dst(),
            send_sem=self.net.send.at[self.index],
            recv_sem=self.net.recv.at[self.index],
            device_id=self.target,
            device_id_type=MESH,
        )

    def start(self):
        self.made().start()
        return self

    def arrived(self):
        if not self.here:
            self.here = True
            self.made().wait_recv()

    def left(self):
        if not self.gone:
            self.gone = True
            self.made().wait_send()


def sems(n):
    return [pltpu.SemaphoreType.DMA((n,)), pltpu.SemaphoreType.DMA((n,))]


def rows(ref, first, count):
    return ref.at[pl.ds(pl.multiple_of(first, 16), count)]


def lanes(first, count):
    return pl.ds(pl.multiple_of(first, 128), count)


def arrive(copies):
    for copy in copies:
        copy.arrived()


HALVES = ((0, 1), (1, -1))


class RingSum:
    def __init__(self, net, first, held, spans, scratch):
        self.net, self.first, self.second, self.held, self.spans = net, first, "y" if first == "x" else "x", held, spans
        self.half, self.fold, self.whole, self.mid, self.half2, self.fold2, self.whole2 = scratch
        self.width = sum(n for _, n in spans)
        self.one, self.two, self.three, self.four = [], [], [], []
        for part, step in HALVES:
            cut = pl.ds(48 * part, 48)
            if first == "x":
                self.plan(self.one, lambda cut=cut: held.at[:, net.near("x", 2), cut, lanes(spans[0][0], 2 * self.width)], lambda part=part: self.half.at[part], "x", step)
            else:
                lane = 0
                for base, n in spans:
                    self.plan(
                        self.one,
                        lambda cut=cut, base=base, n=n: self.ycut(held, net.near("y", 2), base, n, cut),
                        lambda part=part, lane=lane, n=n: self.half.at[part, :, :, lanes(lane, n)],
                        "y",
                        step,
                    )
                    lane += n
            self.plan(self.two, lambda part=part: self.fold.at[part], lambda part=part: self.whole.at[part], first, step)
            if first == "x":
                self.plan(self.three, lambda cut=cut: self.mid.at[lax.rem(net.near("y", 2), 2), cut, self.ylanes(net.near("y", 2))], lambda part=part: self.half2.at[part], "y", step)
            else:
                self.plan(self.three, lambda cut=cut: self.mid.at[net.near("x", 2), cut], lambda part=part: self.half2.at[part], "x", step)
            self.plan(self.four, lambda part=part: self.fold2.at[part], lambda part=part: self.whole2.at[part], self.second, step)

    def plan(self, to, src, dst, axis, step):
        to.append(self.net.plan(src, dst, axis, step))

    def ycut(self, ref, owner, base, n, cut):
        return ref.at[lax.rem(owner, 2), :, cut, lanes(base + (owner // 2) * n, n)]

    def ylanes(self, owner):
        return lanes((owner // 2) * self.width, self.width)

    def block(self, owner):
        if self.first == "x":
            return self.held[:, owner, :, lanes(self.spans[0][0], 2 * self.width)]
        got = [self.held[lax.rem(owner, 2), :, :, lanes(base + (owner // 2) * n, n)] for base, n in self.spans]
        return got[0] if len(got) == 1 else jnp.concatenate(got, axis=-1)

    def mid_block(self, owner):
        if self.first == "x":
            return self.mid[lax.rem(owner, 2), :, self.ylanes(owner)]
        return self.mid[owner]

    def step1(self):
        for copy in self.one:
            copy.start()

    def step2(self):
        arrive(self.one)
        for part, step in HALVES:
            self.fold[part] = self.block(self.net.near(self.first, step))
            self.fold[part, :, 48 * part : 48 * part + 48, :] += self.half[part]
            self.two[part].start()

    def step3(self):
        arrive(self.two)
        own = self.block(self.net.at[self.first]).astype(F32)
        self.mid[...] = (own + self.whole[0].astype(F32) + self.whole[1].astype(F32)).astype(BF16)
        for copy in self.three:
            copy.start()

    def step4(self):
        arrive(self.three)
        for part, step in HALVES:
            self.fold2[part] = self.mid_block(self.net.near(self.second, step))
            self.fold2[part, 48 * part : 48 * part + 48, :] += self.half2[part]
            self.four[part].start()

    def step5(self):
        arrive(self.four)
        own = self.mid_block(self.net.at[self.second]).astype(F32)
        return own + self.whole2[0].astype(F32) + self.whole2[1].astype(F32)


def ring_scratch(first, width):
    blocks, wide = (2, 2 * width) if first == "x" else (4, width)
    shapes = [(2, blocks, 48, wide), (2, blocks, 96, wide), (2, blocks, 96, wide), (blocks, 96, wide), (2, 48, width), (2, 96, width), (2, 96, width)]
    return [pltpu.VMEM(s, BF16) for s in shapes]


class TokenSum:
    def __init__(self, net, part, scratch):
        self.net, self.half, self.fold, self.whole = net, *scratch
        self.one = [
            net.plan(lambda p=p: rows(part, net.near("z", 2) * 256 + 128 * p, 128), lambda p=p: self.half.at[p], "z", step)
            for p, step in HALVES
        ]
        self.two = [net.plan(lambda p=p: self.fold.at[p], lambda p=p: self.whole.at[p], "z", step) for p, step in HALVES]

    def step1(self):
        for copy in self.one:
            copy.start()

    def step2(self):
        arrive(self.one)
        for p, _ in HALVES:
            self.fold[p, 128 * p : 128 * p + 128, :] += self.half[p]
            self.two[p].start()

    def step3(self):
        arrive(self.two)
        return self.whole[0].astype(F32) + self.whole[1].astype(F32)


def token_scratch():
    return [pltpu.VMEM((2, 128, D), BF16), pltpu.VMEM((2, 256, D), BF16), pltpu.VMEM((2, 256, D), BF16)]


def gather_kernel(x, gain, w_gate, w_inner, w_out, w_bc, w_step, conv, bias, gate_gain, step_bias, decay_log, skip, normed_all, wx, wout, wbc, prm, xv, low, stepv, pk, send, recv, local):
    net = Net(send, recv)
    at = net.at
    yh, cx, cc, z, y = at["yh"], at["x"], at["c"], at["z"], at["y"]
    load = pltpu.make_async_copy(x, xv, local.at[0])
    load.start()
    stepv[...] = jnp.zeros_like(stepv)
    stepv[:, 0:HEADS] = w_step[...]
    pk[...] = jnp.zeros_like(pk)
    pk[0:4, :] = conv[...]
    pk[4:5, :] = bias[...]
    pk[5:6, :] = gate_gain[...]
    pk[6:7, 0:HEADS] = step_bias[...]
    pk[7:8, 0:HEADS] = decay_log[...]
    pk[8:9, 0:HEADS] = skip[...]
    net.barrier([("z", 1), ("z", -1), ("x", 1), ("x", -1), ("y", 1), ("y", -1), ("y", 2), ("c", 1)])
    first = {
        "x": ((w_gate, wx, 0, COLS), (w_out, wout, 0, COLS)),
        "y": ((w_inner, wx, WIDE, COLS), (stepv, wx, STEPS, 128), (w_bc.at[:, lanes(yh * 128, 128)], wbc, 0, 128)),
    }

    def spot(ref, base, n, yy, xx, cut=slice(None)):
        cut = pl.ds(0, 96) if cut == slice(None) else cut
        return ref.at[lax.rem(yy, 2), xx, cc, cut, lanes(base + (yy // 2) * n, n)]

    own = [pltpu.make_async_copy(src, spot(ref, base, n, y, cx), local.at[1 + i]) for i, (src, ref, base, n) in enumerate(first["x"] + first["y"])]
    own.append(pltpu.make_async_copy(pk, prm.at[yh], local.at[6]))
    sent = {"x": [], "y": []}
    for axis in ("x", "y"):
        for src, ref, base, n in first[axis]:
            sent[axis].append([net.start(src, spot(ref, base, n, y, cx), axis, step) for _, step in HALVES])
    load.wait()
    v = xv[...].astype(F32)
    root = lax.rsqrt(jnp.mean(v * v, axis=1, keepdims=True) + EPS)
    low[...] = (v * root * gain[...]).astype(BF16)
    zs = [net.start(low, rows(normed_all, z * 256, 256), "z", step) for _, step in HALVES]
    own.append(pltpu.make_async_copy(low, rows(normed_all, z * 256, 256), local.at[7]))
    for copy in own:
        copy.start()
    for axis in ("x", "y"):
        for src, ref, base, n in first[axis]:
            net.start(src, spot(ref, base, n, y, cx), "c")
    net.start(pk, prm.at[yh], "y", 2)
    second = {"x": [], "y": []}
    for axis in ("x", "y"):
        for (src, ref, base, n), copies in zip(first[axis], sent[axis]):
            for (part, step), copy in zip(HALVES, copies):
                copy.arrived()
                cut = pl.ds(48 * part, 48)
                here = spot(ref, base, n, y, net.near("x", -step), cut) if axis == "x" else spot(ref, base, n, net.near("y", -step), cx, cut)
                second[axis].append(net.start(here, here, axis, step))
    for copy in own[:5]:
        copy.wait()
    third = {"x": [], "y": []}

    def line(axis, ref, base, n, place, cut=None):
        cut = pl.ds(0, 96) if cut is None else cut
        if axis == "x":
            return ref.at[lax.rem(place, 2), :, cc, cut, lanes(base + (place // 2) * n, n)]
        return ref.at[:, place, cc, cut, lanes(base, 2 * n)]

    then = {"x": "y", "y": "x"}
    for axis in ("x", "y"):
        arrive(second[axis])
        for src, ref, base, n in first[axis]:
            here = line(axis, ref, base, n, at[then[axis]])
            third[axis].append([net.start(here, here, then[axis], step) for _, step in HALVES])
    for axis in ("x", "y"):
        for src, ref, base, n in first[axis]:
            for step in (1, -1, 2):
                here = spot(ref, base, n, y, net.near("x", step)) if axis == "x" else spot(ref, base, n, net.near("y", step), cx)
                net.start(here, here, "c")
    fourth = {"x": [], "y": []}

    def pass_on(axis):
        for (src, ref, base, n), copies in zip(first[axis], third[axis]):
            for (part, step), copy in zip(HALVES, copies):
                copy.arrived()
                place = net.near(then[axis], -step)
                here = line(axis, ref, base, n, place, pl.ds(48 * part, 48))
                fourth[axis].append(net.start(here, here, then[axis], step))
                here = line(axis, ref, base, n, place)
                net.start(here, here, "c")

    pass_on("y")
    pass_on("x")
    for (part, step), copy in zip(HALVES, zs):
        copy.arrived()
        here = rows(normed_all, net.near("z", -step) * 256 + 128 * part, 128)
        net.start(here, here, "z", step)
    for axis in ("y", "x"):
        arrive(fourth[axis])
        for src, ref, base, n in first[axis]:
            here = line(axis, ref, base, n, net.near(then[axis], 2))
            net.start(here, here, "c")
    net.finish()
    for copy in own[5:]:
        copy.wait()


def run_gather(*args):
    return pl.pallas_call(
        gather_kernel,
        out_shape=[
            SHAPE((LEN, D), BF16),
            SHAPE((2, 4, 2, 96, PROJ), BF16),
            SHAPE((2, 4, 2, 96, WIDE), BF16),
            SHAPE((2, 4, 2, 96, 256), BF16),
            SHAPE((GROUPS, 16, COLS), F32),
        ],
        in_specs=[ANY, VMEM, ANY, ANY, ANY, ANY] + [VMEM] * 7,
        out_specs=[ANY] * 5,
        scratch_shapes=[
            pltpu.VMEM((256, D), BF16),
            pltpu.VMEM((256, D), BF16),
            pltpu.VMEM((96, 128), BF16),
            pltpu.VMEM((16, COLS), F32),
        ]
        + sems(96)
        + [pltpu.SemaphoreType.DMA((8,))],
        compiler_params=pltpu.CompilerParams(collective_id=0, has_side_effects=True, vmem_limit_bytes=ROOM),
        name="gather_all",
    )(*args)


def forward_kernel(
    x, wx, wout, wbc, prm, conv_bc, bias_bc, cot,
    gate_out, inner_out, z_out, y_out, gm_out, mixed_out, h_out, dt_out, r_out, u_out, bc_out, bcin_out, zbc_out, stats_out, cot_all,
    cots, gps, ext, extbc, state, stat, slots, send, recv, local,
):
    i = pl.program_id(0)
    net = Net(send, recv)
    z = net.at["z"]
    here = lambda step=0: rows(cots, (net.near("z", step) if step else z) * 256, 256)
    part = lambda p, step: rows(cots, net.near("z", -step) * 256 + 128 * p, 128)
    c1 = [net.plan(lambda: cot, lambda: here(), "z", step) for _, step in HALVES]
    c2 = [net.plan(lambda p=p, s=s: part(p, s), lambda p=p, s=s: part(p, s), "z", s) for p, s in HALVES]
    q = [net.plan(lambda: stat, lambda: slots.at[z], "z", step) for step in (1, -1, 2)]
    own = lambda: pltpu.make_async_copy(cot, here(), local.at[0])
    out = lambda: pltpu.make_async_copy(cots, cot_all, local.at[1])

    @pl.when(i == 0)
    def _():
        net.barrier([("z", 1), ("z", -1), ("z", 2)])
        own().start()
        for copy in c1:
            copy.start()
        ext[0:8, :] = jnp.zeros((8, WIDE), F32)
        extbc[0:8, :] = jnp.zeros((8, 256), F32)
        state[...] = jnp.zeros_like(state)

    @pl.when((i > 0) & (i < BLOCKS))
    def _():
        ext[0:8, :] = ext[BLOCK : BLOCK + 8, :]
        extbc[0:8, :] = extbc[BLOCK : BLOCK + 8, :]

    @pl.when(i == BLOCKS - 1)
    def _():
        for copy in c1:
            copy.arrived()
        for copy in c2:
            copy.start()

    @pl.when(i < BLOCKS)
    def _():
        xb = x[...]
        bc_in = dot(xb, wbc[...])
        bcin_out[...] = bc_in
        extbc[8 : BLOCK + 8, :] = bc_in
        zb = bias_bc[...] + sum(conv_bc[j : j + 1, :] * extbc[5 + j : 5 + j + BLOCK, :] for j in range(4))
        zbc_out[...] = zb
        bc = (zb * sigmoid(zb)).astype(BF16)
        bc_out[...] = bc
        b, c = bc[:, :STATE], bc[:, STATE:]
        scores = jnp.where(iota((BLOCK, BLOCK), 0) >= iota((BLOCK, BLOCK), 1), dot_nt(c, b), 0.0)
        tri, spread = lower(), expander()
        left = iota((BLOCK, 128), 1) < 64
        steps = dot(xb, wx[:, STEPS:])
        total = jnp.zeros((BLOCK, 128), F32)
        for g in range(GROUPS):
            cut = slice(g * COLS, (g + 1) * COLS)
            u = steps[:, 128 * g : 128 * (g + 1)] + prm[g, 6:7, 0:128]
            dt = jnp.maximum(u, 0.0) + jnp.log(1.0 + jnp.exp(-jnp.abs(u)))
            rate = -jnp.exp(prm[g, 7:8, 0:128]) * LOG2E
            r = dot_right(tri, dt * rate, 3)
            u_out[g] = u
            dt_out[g] = dt
            r_out[g] = r
            rt = jnp.transpose(r)
            gate = dot(xb, wx[:, cut])
            inner = dot(xb, wx[:, WIDE + g * COLS : WIDE + (g + 1) * COLS])
            gate_out[:, cut] = gate
            inner_out[:, cut] = inner
            ext[8 : BLOCK + 8, cut] = inner
            zv = prm[g, 4:5, :] + sum(prm[g, j : j + 1, :] * ext[5 + j : 5 + j + BLOCK, cut] for j in range(4))
            z_out[:, cut] = zv
            xv = zv * sigmoid(zv)
            last = r[BLOCK - 1 : BLOCK, :]
            w = xv * dot_left(dt, spread, 2)
            grow = dot_left(jnp.exp2(r), spread, 2)
            tail = dot_left(jnp.exp2(last - r), spread, 2)
            skip = dot_left(prm[g, 8:16, 0:128], spread, 3)[0:1, :]
            wl = w.astype(BF16)
            h = state[:, cut]
            h_out[0, g] = h
            parts = []
            for p in range(HEADS // 2):
                halves = []
                for n in (2 * p, 2 * p + 1):
                    gap = jnp.minimum(r[:, n : n + 1] - rt[n : n + 1, :], 0.0)
                    halves.append(dot((scores * jnp.exp2(gap)).astype(BF16), wl[:, 128 * p : 128 * (p + 1)]))
                parts.append(jnp.where(left, halves[0], halves[1]))
            yv = jnp.concatenate(parts, axis=1) + grow * dot(c, h.astype(BF16)) + skip * xv
            y_out[:, cut] = yv
            state[:, cut] = grow[BLOCK - 1 : BLOCK, :] * h + dot_tn(b, (tail * w).astype(BF16))
            gp = yv * (gate * sigmoid(gate))
            gps[pl.ds(pl.multiple_of(i * BLOCK, BLOCK), BLOCK), cut] = gp
            sq = gp * gp
            total = total + (sq[:, 0:128] + sq[:, 128:256] + sq[:, 256:384])
        stat[pl.ds(i, 1), :] = token_row(total)

    @pl.when(i == BLOCKS)
    def _():
        own().wait()

    @pl.when(i == 2 * BLOCKS - 1)
    def _():
        for copy in c2:
            copy.arrived()
        out().start()

    @pl.when(i >= BLOCKS)
    def _():
        t = i - BLOCKS
        block = lax.rem(z + t + lax.div(t, 2) - 2 * lax.div(t, 3), 4)
        at = pl.ds(pl.multiple_of(block * BLOCK, BLOCK), BLOCK)
        gm = dot(cots[at, :], wout[...])
        gm_out[at, :] = gm
        gain = jnp.concatenate([prm[0, 5:6, :], prm[1, 5:6, :]], axis=1)
        stat[pl.ds(BLOCKS + block, 1), :] = token_row(gm * gain * gps[at, :])

    @pl.when(i == 2 * BLOCKS - 1)
    def _():
        for copy in q:
            copy.start()
        slots[z] = stat[...]
        for copy in q:
            copy.arrived()
        sums = (slots[0] + slots[1]) + (slots[2] + slots[3])
        root = lax.rsqrt(sums[0:4, :] * (1.0 / INNER) + EPS)
        stats_out[0:4, :] = root
        stats_out[4:8, :] = root * root * root * (sums[4:8, :] * (1.0 / INNER))
        columns = jnp.transpose(stats_out[...])
        gain = jnp.concatenate([prm[0, 5:6, :], prm[1, 5:6, :]], axis=1)
        for k in range(BLOCKS):
            at = slice(k * BLOCK, (k + 1) * BLOCK)
            mixed_out[at, :] = (gps[at, :] * columns[:, k : k + 1] * gain).astype(BF16)
        for copy in c1 + c2 + q:
            copy.left()
        out().wait()


def run_forward(x, wx, wout, wbc, prm, conv_bc, bias_bc, cot):
    first = lambda k: jnp.minimum(k, BLOCKS - 1)
    const = lambda *s: pl.BlockSpec(s, lambda k: (0,) * len(s), pipeline_mode=pl.Buffered(1))
    keep = lambda *s: pl.BlockSpec(s, lambda k: (0,) * len(s))
    block = lambda n: pl.BlockSpec((BLOCK, n), lambda k: (first(k), 0))
    small = lambda: pl.BlockSpec((GROUPS, BLOCK, 128), lambda k: (0, first(k), 0))
    wide = SHAPE((LEN, WIDE), F32)
    narrow = SHAPE((GROUPS, LEN, 128), F32)
    return pl.pallas_call(
        forward_kernel,
        grid=(2 * BLOCKS,),
        out_shape=[
            wide,
            wide,
            wide,
            wide,
            wide,
            SHAPE((LEN, WIDE), BF16),
            SHAPE((BLOCKS, GROUPS, STATE, COLS), F32),
            narrow,
            narrow,
            narrow,
            SHAPE((LEN, 256), BF16),
            SHAPE((LEN, 256), F32),
            SHAPE((LEN, 256), F32),
            SHAPE((8, 256), F32),
            SHAPE((LEN, D), BF16),
        ],
        in_specs=[
            block(D),
            const(D, PROJ),
            const(D, WIDE),
            const(D, 256),
            const(GROUPS, 16, COLS),
            const(4, 256),
            const(1, 256),
            ANY,
        ],
        out_specs=[
            block(WIDE),
            block(WIDE),
            block(WIDE),
            block(WIDE),
            keep(LEN, WIDE),
            keep(LEN, WIDE),
            pl.BlockSpec((1, GROUPS, STATE, COLS), lambda k: (first(k), 0, 0, 0)),
            small(),
            small(),
            small(),
            block(256),
            block(256),
            block(256),
            keep(8, 256),
            ANY,
        ],
        scratch_shapes=[
            pltpu.VMEM((LEN, D), BF16),
            pltpu.VMEM((LEN, WIDE), F32),
            pltpu.VMEM((BLOCK + 8, WIDE), F32),
            pltpu.VMEM((BLOCK + 8, 256), F32),
            pltpu.VMEM((STATE, WIDE), F32),
            pltpu.VMEM((8, BLOCK), F32),
            pltpu.VMEM((4, 8, BLOCK), F32),
        ]
        + sems(7)
        + [pltpu.SemaphoreType.DMA((2,))],
        compiler_params=pltpu.CompilerParams(collective_id=1, has_side_effects=True, vmem_limit_bytes=ROOM),
        name="forward",
    )(x, wx, wout, wbc, prm, conv_bc, bias_bc, cot)


def backward_kernel(
    gm, gate, inner, zin, y, hin, prm, bc, dt, r, u, stats, part, dout, tokens,
    cat_out, dbc_out, acc, branch_out, wout_out,
    ext, dstate, dst, dbc, held, got, g1, g2, g3, s1, s2, s3, s4, s5, s6, s7, send, recv, local,
):
    k = pl.program_id(0)
    net = Net(send, recv)
    cc, z = net.at["c"], net.at["z"]
    cross = net.plan(lambda: dout.at[:, :, net.other], lambda: got, "c")
    token = TokenSum(net, part, (g1, g2, g3))
    ring = RingSum(net, "y", held, ((0, COLS),), (s1, s2, s3, s4, s5, s6, s7))
    loads = lambda: [
        pltpu.make_async_copy(dout.at[:, :, cc], held, local.at[0]),
        pltpu.make_async_copy(rows(part, net.near("z", 1) * 256, 256), g2.at[0], local.at[1]),
        pltpu.make_async_copy(rows(part, net.near("z", -1) * 256, 256), g2.at[1], local.at[2]),
        pltpu.make_async_copy(rows(part, z * 256, 256), branch_out, local.at[3]),
    ]

    @pl.when(k == 0)
    def _():
        net.barrier([("z", 1), ("z", -1), ("x", 1), ("x", -1), ("y", 1), ("y", -1), ("c", 1)])
        cross.start()
        token.step1()
        for copy in loads():
            copy.start()
        acc[...] = jnp.zeros_like(acc)
        ext[BLOCK : BLOCK + 8, :] = jnp.zeros((8, WIDE), F32)
        dstate[...] = jnp.zeros_like(dstate)

    @pl.when(k > 0)
    def _():
        ext[BLOCK : BLOCK + 8, :] = ext[0:8, :]

    b, c = bc[:, :STATE], bc[:, STATE:]
    valid = iota((BLOCK, BLOCK), 1) >= iota((BLOCK, BLOCK), 0)
    scores = jnp.where(valid, dot_nt(b, c), 0.0)
    both = jnp.concatenate([stats[pl.ds(BLOCKS - 1 - k, 1), :], stats[pl.ds(2 * BLOCKS - 1 - k, 1), :], jnp.zeros((6, BLOCK), F32)], axis=0)
    column = jnp.transpose(both)
    ir, cr = column[:, 0:1], column[:, 1:2]
    spread, fold = expander(), reducer()
    left = iota((BLOCK, 128), 1) < 64
    suffix, prefix = upper(), lower(strict=True)
    dst[...] = jnp.zeros_like(dst)
    dbc[...] = jnp.zeros_like(dbc)
    for g in range(GROUPS):
        if g == 0:

            @pl.when(k == 1)
            def _():
                ring.step2()

            @pl.when(k == 2)
            def _():
                ring.step3()

        else:

            @pl.when(k == 0)
            def _():
                for copy in loads():
                    copy.wait()
                cross.arrived()
                held[...] += got[...]
                ring.step1()

            @pl.when(k == 1)
            def _():
                token.step2()

            @pl.when(k == 2)
            def _():
                ring.step4()

        cut = slice(g * COLS, (g + 1) * COLS)
        yv = y[:, cut]
        gv = gate[:, cut]
        sig = sigmoid(gv)
        act = gv * sig
        gain = prm[g, 5:6, :]
        gp = yv * act
        gmix = gm[:, cut]
        gain_grad = gmix * gp * ir
        gated = ir * (gmix * gain) - gp * cr
        gs = gated * act
        cat_out[:, cut] = (gated * yv * sig * (1.0 + gv * (1.0 - sig))).astype(BF16)
        xi = inner[:, cut]
        zv = zin[:, cut]
        zs = sigmoid(zv)
        xv = zv * zs
        rv = r[g]
        rt = jnp.transpose(rv)
        last = rv[BLOCK - 1 : BLOCK, :]
        dte = dot_left(dt[g], spread, 2)
        grow = dot_left(jnp.exp2(rv), spread, 2)
        tail = dot_left(jnp.exp2(last - rv), spread, 2)
        skip = dot_left(prm[g, 8:16, 0:128], spread, 3)[0:1, :]
        w = xv * dte
        wl = w.astype(BF16)
        gl = gs.astype(BF16)
        h = hin[0, g]
        dh = dstate[:, cut]
        dhl = dh.astype(BF16)
        parts = []
        for p in range(HEADS // 2):
            halves = []
            pair = slice(128 * p, 128 * (p + 1))
            wp, gpair = wl[:, pair], gl[:, pair]
            zero = jnp.zeros_like(wp)
            for n in (2 * p, 2 * p + 1):
                decay = jnp.exp2(jnp.minimum(rt[n : n + 1, :] - rv[:, n : n + 1], 0.0))
                halves.append(dot((scores * decay).astype(BF16), gpair))
                mine = jnp.where(left, wp, zero) if n % 2 == 0 else jnp.where(left, zero, wp)
                dst[...] += dot_nt(mine, gpair) * decay
            parts.append(jnp.where(left, halves[0], halves[1]))
        dwi = jnp.concatenate(parts, axis=1)
        dws = tail * dot(b, dhl)
        dw = dwi + dws
        skipgrad = gs * xv
        diff = dot_left(gl.astype(F32) * (yv - skip * xv) - wl.astype(F32) * dwi, fold, 3)
        zsum = dot_left(w * dws, fold, 3)
        const = dot_left(jnp.sum(h * dh, axis=0, keepdims=True) * grow[BLOCK - 1 : BLOCK, :] + jnp.zeros((8, COLS), F32), fold, 3)
        da = dot_right(suffix, diff, 3) + dot_right(prefix, zsum, 3) + const[0:1, :]
        rate = -jnp.exp(prm[g, 7:8, 0:128])
        dstep = (dot_left(xv * dw, fold, 3) + rate * da) * sigmoid(u[g])
        cat_out[:, STEPS + 128 * g : STEPS + 128 * (g + 1)] = dstep.astype(BF16)
        gx = (grow * gs).astype(BF16)
        dbc[:, STATE:] += dot_nt(gx, h.astype(BF16))
        dbc[:, :STATE] += dot_nt((tail * w).astype(BF16), dhl)
        dstate[:, cut] = grow[BLOCK - 1 : BLOCK, :] * dh + dot_tn(c, gx)
        dx = dte * dw + skip * gs
        dz = dx * (zs * (1.0 + zv * (1.0 - zs)))
        ext[0:BLOCK, cut] = dz
        gi = jnp.zeros((BLOCK, COLS), F32)
        for j in range(4):
            moved = ext[3 - j : 3 - j + BLOCK, cut]
            gi = gi + prm[g, j : j + 1, :] * moved
            acc[g, j : j + 1, :] += jnp.sum(xi * moved, axis=0, keepdims=True)
        cat_out[:, WIDE + g * COLS : WIDE + (g + 1) * COLS] = gi.astype(BF16)
        acc[g, 4:5, :] += jnp.sum(dz, axis=0, keepdims=True)
        acc[g, 5:6, :] += jnp.sum(gain_grad, axis=0, keepdims=True)
        acc[g, 6:7, 0:128] += jnp.sum(dstep, axis=0, keepdims=True)
        acc[g, 7:8, 0:128] += jnp.sum(da * dt[g], axis=0, keepdims=True) * rate
        acc[g, 8:9, 0:128] += dot_left(jnp.sum(skipgrad, axis=0, keepdims=True) + jnp.zeros((8, COLS), F32), fold, 3)[0:1, :]
    ds = jnp.where(valid, dst[...], 0.0).astype(BF16)
    dbc_out[:, STATE:] = (dbc[:, STATE:] + dot_tn(ds, b)).astype(BF16)
    dbc_out[:, :STATE] = (dbc[:, :STATE] + dot(ds, c)).astype(BF16)

    @pl.when(k == BLOCKS - 1)
    def _():
        wout_out[...] = ring.step5()
        branch = branch_out[...].astype(F32) + token.step3()
        branch_out[...] = (tokens[...].astype(F32) + branch).astype(BF16)
        for copy in net.copies:
            copy.left()


def run_backward(gm, gate, inner, zin, y, hin, prm, bc, dt, r, u, stats, part, dout, tokens):
    rev = lambda k: BLOCKS - 1 - k
    cols = lambda n: pl.BlockSpec((BLOCK, n), lambda k: (rev(k), 0))
    small = lambda: pl.BlockSpec((GROUPS, BLOCK, 128), lambda k: (0, rev(k), 0))
    keep = lambda *s: pl.BlockSpec(s, lambda k: (0,) * len(s))
    return pl.pallas_call(
        backward_kernel,
        grid=(BLOCKS,),
        out_shape=[
            SHAPE((LEN, PROJ), BF16),
            SHAPE((LEN, 256), BF16),
            SHAPE((GROUPS, 16, COLS), F32),
            SHAPE((256, D), BF16),
            SHAPE((96, COLS), F32),
        ],
        in_specs=[cols(WIDE)] * 5
        + [
            pl.BlockSpec((1, GROUPS, STATE, COLS), lambda k: (rev(k), 0, 0, 0)),
            keep(GROUPS, 16, COLS),
            cols(256),
            small(),
            small(),
            small(),
            keep(8, 256),
            ANY,
            ANY,
            keep(256, D),
        ],
        out_specs=[cols(PROJ), cols(256), keep(GROUPS, 16, COLS), keep(256, D), keep(96, COLS)],
        scratch_shapes=[
            pltpu.VMEM((BLOCK + 8, WIDE), F32),
            pltpu.VMEM((STATE, WIDE), F32),
            pltpu.VMEM((BLOCK, BLOCK), F32),
            pltpu.VMEM((BLOCK, 256), F32),
            pltpu.VMEM((2, 4, 96, WIDE), BF16),
            pltpu.VMEM((2, 4, 96, WIDE), BF16),
        ]
        + token_scratch()
        + ring_scratch("y", COLS)
        + sems(13)
        + [pltpu.SemaphoreType.DMA((4,))],
        compiler_params=pltpu.CompilerParams(collective_id=2, has_side_effects=True, vmem_limit_bytes=ROOM),
        name="backward",
    )(gm, gate, inner, zin, y, hin, prm, bc, dt, r, u, stats, part, dout, tokens)


def tail_kernel(
    gn, dcat, dbc, zbc, bc_in, normed, acc, wbc, tokens, cot, gain, conv,
    tokens_out, gate_out, inner_out, bc_out, small_out,
    gnv, nv, mine, slots, zv, xi, wv, xv, ov, ext, gnbc, held, got, dbw, heldb, gotb, small, sp0, sp1, sp2, sp3, bz, by,
    g1, g2, g3, a1, a2, a3, a4, a5, a6, a7, b1, b2, b3, b4, b5, b6, b7, c1, c2, c3, c4, c5, c6, c7, send, recv, local,
):
    net = Net(send, recv)
    at = net.at
    yh, cx, cc, z, y = at["yh"], at["x"], at["c"], at["z"], at["y"]
    loads = [
        pltpu.make_async_copy(src, dst, local.at[i])
        for i, (src, dst) in enumerate(
            (
                (dcat.at[:, :, cc], held),
                (rows(gn, net.near("z", 1) * 256, 256), g2.at[0]),
                (rows(gn, net.near("z", -1) * 256, 256), g2.at[1]),
                (gn, gnv),
                (normed, nv),
                (rows(zbc, z * 256, 256), zv.at[pl.ds(0, 256)]),
                (rows(zbc, lax.rem(z * 256 + 256, LEN), 16), zv.at[pl.ds(256, 16)]),
                (rows(bc_in, z * 256, 256), xi),
                (wbc, wv),
                (tokens, xv),
                (cot, ov),
            )
        )
    ]
    token = TokenSum(net, gn, (g1, g2, g3))
    ring_gate = RingSum(net, "x", held, ((0, COLS),), (a1, a2, a3, a4, a5, a6, a7))
    ring_inner = RingSum(net, "y", held, ((WIDE, COLS), (STEPS, 128)), (b1, b2, b3, b4, b5, b6, b7))
    ring_bc = RingSum(net, "x", heldb, ((0, 128),), (c1, c2, c3, c4, c5, c6, c7))
    net.barrier([(a, s) for a in ("z", "x", "y") for s in (1, -1, 2)] + [("c", 1)])
    cross = net.start(dcat.at[:, :, net.other], got, "c")
    mine[0:LEN, :] = dbc[...]
    mine[LEN : LEN + 16, :] = jnp.zeros((16, 256), BF16)
    swap = [net.start(rows(mine, net.near("z", s) * 256, 272), slots.at[z], "z", s) for s in (1, -1, 2)]
    token.step1()
    for copy in loads:
        copy.start()
    slots[z] = mine[pl.ds(pl.multiple_of(z * 256, 16), 272), :]
    arrive(swap)
    for copy in loads:
        copy.wait()
    total = (slots[0].astype(F32) + slots[1].astype(F32)) + (slots[2].astype(F32) + slots[3].astype(F32))
    sig = sigmoid(zv[...])
    dz = total * (sig * (1.0 + zv[...] * (1.0 - sig)))
    ext[...] = jnp.where(iota((272, 256), 0) + z * 256 < LEN, dz, 0.0)
    gbc = jnp.zeros((256, 256), F32)
    small[0:16, :] = acc[0]
    small[16:32, :] = acc[1]
    small[32:48, :] = jnp.zeros((16, COLS), F32)
    for j in range(4):
        moved = ext[3 - j : 3 - j + 256, :]
        gbc = gbc + conv[j : j + 1, :] * moved
        small[36 + j : 37 + j, 0:256] = jnp.sum(xi[...] * moved, axis=0, keepdims=True)
    small[40:41, 0:256] = jnp.sum(ext[0:256, :], axis=0, keepdims=True)
    gbc = gbc.astype(BF16)
    own = pl.ds(pl.multiple_of(z * 256, 16), 256)
    dbw[...] = dot_tn(nv[own, :], gbc).astype(BF16).reshape(2, 4, 2, 96, 256)
    crossb = net.start(dbw.at[:, :, net.other], gotb, "c")
    gnbc[...] = dot_nt(gbc, wv[...])
    gain_row = gain[...]
    part = jnp.sum(gnbc[...] * nv[own, :].astype(F32), axis=0, keepdims=True)
    for k in range(BLOCKS):
        cut = slice(k * 256, (k + 1) * 256)
        part = part + jnp.sum(gnv[cut, :].astype(F32) * nv[cut, :].astype(F32), axis=0, keepdims=True)
    part = part / gain_row
    for k in range(4):
        small[32 + k : 33 + k, :] = part[:, k * COLS : (k + 1) * COLS]
    sp0[z] = small[32:48, :]
    q = net.around(sp0.at[z], sp0.at[z], "z")
    cross.arrived()
    held[...] += got[...]
    ring_inner.step1()
    ring_gate.step1()
    token.step2()
    crossb.arrived()
    heldb[...] = dbw[:, :, cc] + gotb[...]
    ring_bc.step1()
    arrive(q)
    sp1[cx, 0:32, :] = small[0:32, :]
    sp1[cx, 32:48, :] = (sp0[0] + sp0[1]) + (sp0[2] + sp0[3])
    q = net.around(sp1.at[cx], sp1.at[cx], "x")
    ring_gate.step2()
    ring_inner.step2()
    ring_bc.step2()
    arrive(q)
    sp2[y] = (sp1[0] + sp1[1]) + (sp1[2] + sp1[3])
    q = net.around(sp2.at[y], sp2.at[y], "y")
    ring_bc.step3()
    ring_gate.step3()
    ring_inner.step3()
    arrive(q)
    sp3[cc] = (sp2[0] + sp2[1]) + (sp2[2] + sp2[3])
    q = [net.start(sp3.at[cc], sp3.at[cc], "c")]
    ring_bc.step4()
    ring_gate.step4()
    ring_inner.step4()
    arrive(q)
    small_out[...] = sp3[0] + sp3[1]
    bz[z] = ring_bc.step5()
    q = net.around(bz.at[z], bz.at[z], "z")
    gate_out[...] = ring_gate.step5()
    inner_out[...] = ring_inner.step5()
    arrive(q)
    by[yh] = (bz[0] + bz[1]) + (bz[2] + bz[3])
    q = [net.start(by.at[yh], by.at[yh], "y", 2)]
    v = xv[...].astype(F32)
    root = lax.rsqrt(jnp.mean(v * v, axis=1, keepdims=True) + EPS)
    g = token.step3() + gnv[own, :].astype(F32) + gnbc[...]
    scaled = g * gain_row
    tokens_out[...] = ov[...].astype(F32) + root * scaled - v * (root * root * root) * jnp.mean(scaled * v, axis=1, keepdims=True)
    arrive(q)
    bc_out[:, :128] = by[0]
    bc_out[:, 128:] = by[1]
    net.finish()


def run_tail(gn, dcat, dbc, zbc, bc_in, normed, acc, wbc, tokens, cot, gain, conv):
    bf = lambda *s: pltpu.VMEM(s, BF16)
    f32 = lambda *s: pltpu.VMEM(s, F32)
    return pl.pallas_call(
        tail_kernel,
        out_shape=[
            SHAPE((256, D), F32),
            SHAPE((96, COLS), F32),
            SHAPE((96, COLS + 128), F32),
            SHAPE((96, 256), F32),
            SHAPE((48, COLS), F32),
        ],
        in_specs=[ANY, ANY, VMEM, ANY, ANY, ANY, VMEM, ANY, ANY, ANY, VMEM, VMEM],
        out_specs=[VMEM] * 5,
        scratch_shapes=[
            bf(LEN, D),
            bf(LEN, D),
            bf(LEN + 16, 256),
            bf(4, 272, 256),
            f32(272, 256),
            f32(256, 256),
            bf(D, 256),
            bf(256, D),
            bf(256, D),
            f32(272, 256),
            f32(256, D),
            bf(2, 4, 96, PROJ),
            bf(2, 4, 96, PROJ),
            bf(2, 4, 2, 96, 256),
            bf(2, 4, 96, 256),
            bf(2, 4, 96, 256),
            f32(48, COLS),
            f32(4, 16, COLS),
            f32(4, 48, COLS),
            f32(4, 48, COLS),
            f32(2, 48, COLS),
            f32(4, 96, 128),
            f32(2, 96, 128),
        ]
        + token_scratch()
        + ring_scratch("x", COLS)
        + ring_scratch("y", COLS + 128)
        + ring_scratch("x", 128)
        + sems(64)
        + [pltpu.SemaphoreType.DMA((11,))],
        compiler_params=pltpu.CompilerParams(collective_id=3, has_side_effects=True, vmem_limit_bytes=ROOM),
        name="tail",
    )(gn, dcat, dbc, zbc, bc_in, normed, acc, wbc, tokens, cot, gain, conv)


def finish_kernel(tokens, branch, inner, bc, small, gate, wout, tokens_out, branch_out, step_out, inner_out, bc_out, gate_out, wout_out, norm, conv, bias, conv_bc, bias_bc, step_bias, decay, skip, gain, sem):
    big = [
        pltpu.make_async_copy(src, dst, sem.at[i])
        for i, (src, dst) in enumerate(
            ((tokens, tokens_out), (branch, branch_out), (inner.at[:, pl.ds(0, COLS)], inner_out), (bc, bc_out), (gate, gate_out), (wout, wout_out))
        )
    ]
    for copy in big:
        copy.start()
    step_out[...] = inner[:, COLS : COLS + HEADS]
    for k in range(4):
        norm[:, k * COLS : (k + 1) * COLS] = small[32 + k : 33 + k, :]
    conv_bc[...] = small[36:40, 0:256]
    bias_bc[...] = small[40:41, 0:256]
    mine = small[pl.ds(pl.multiple_of(lax.axis_index("yh") * 16, 8), 16), :]
    conv[...] = mine[0:4, :]
    bias[...] = mine[4:5, :]
    gain[...] = mine[5:6, :]
    step_bias[...] = mine[6:7, 0:HEADS]
    decay[...] = mine[7:8, 0:HEADS]
    skip[...] = mine[8:9, 0:HEADS]
    for copy in big:
        copy.wait()


def run_finish(tokens, branch, inner, bc, small, gate, wout):
    f32 = lambda *s: SHAPE(s, F32)
    return pl.pallas_call(
        finish_kernel,
        out_shape=[
            f32(256, D),
            SHAPE((256, D), BF16),
            f32(96, HEADS),
            f32(96, COLS),
            f32(96, 256),
            f32(96, COLS),
            f32(96, COLS),
            f32(1, D),
            f32(4, COLS),
            f32(1, COLS),
            f32(4, 256),
            f32(1, 256),
            f32(1, HEADS),
            f32(1, HEADS),
            f32(1, HEADS),
            f32(1, COLS),
        ],
        in_specs=[ANY, ANY, VMEM, ANY, VMEM, ANY, ANY],
        out_specs=[ANY, ANY, VMEM] + [ANY] * 4 + [VMEM] * 9,
        scratch_shapes=[pltpu.SemaphoreType.DMA((6,))],
        compiler_params=pltpu.CompilerParams(vmem_limit_bytes=16 * 2**20),
        name="finish",
    )(tokens, branch, inner, bc, small, gate, wout)


def shards(tokens, norm_gain, w_gate, w_inner, w_bc, w_step, conv_inner, bias_inner, conv_bc, bias_bc, step_bias, decay_log, skip_gain, gate_gain, w_out, cotangent):
    row = lambda v: v.reshape(1, -1)
    gain = row(norm_gain)
    normed, wx, wout, wbc, prm = run_gather(
        tokens, gain, w_gate, w_inner, w_out, w_bc, w_step, conv_inner, row(bias_inner), row(gate_gain), row(step_bias), row(decay_log), row(skip_gain)
    )
    wx, wout, wbc = wx.reshape(D, PROJ), wout.reshape(D, WIDE), wbc.reshape(D, 256)
    gate, inner, zin, y, gm, mixed, hin, dt, r, u, bc, bc_in, zbc, stats, cot_all = run_forward(
        normed, wx, wout, wbc, prm, conv_bc, row(bias_bc), cotangent
    )
    part = dot_nt(mixed, wout).astype(BF16)
    dout = dot_tn(cot_all, mixed).astype(BF16).reshape(2, 4, 2, 96, WIDE)
    cat, dbc, acc, output, wout_grad = run_backward(gm, gate, inner, zin, y, hin, prm, bc, dt, r, u, stats, part, dout, tokens)
    gn = dot_nt(cat, wx).astype(BF16)
    dcat = dot_tn(normed, cat).astype(BF16).reshape(2, 4, 2, 96, PROJ)
    tokens_grad, gate_grad, inner_grad, bc_grad, small = run_tail(gn, dcat, dbc, zbc, bc_in, normed, acc, wbc, tokens, cotangent, gain, conv_bc)
    (
        tokens_grad, output, step_grad, inner_grad, bc_grad, gate_grad, wout_grad,
        norm, conv, bias, conv_bc_grad, bias_bc_grad, step_bias_grad, decay, skip, gate_gain_grad,
    ) = run_finish(tokens_grad, output, inner_grad, bc_grad, small, gate_grad, wout_grad)
    flat = lambda v: v.reshape(-1)
    return (
        output, tokens_grad, flat(norm), gate_grad, inner_grad, bc_grad, step_grad, conv, flat(bias), conv_bc_grad,
        flat(bias_bc_grad), flat(step_bias_grad), flat(decay), flat(skip), flat(gate_gain_grad), wout_grad,
    )


def solution(mesh):
    fine = Mesh(mesh.devices.reshape(2, 4, 2, 2, 4), AXES)
    dp, tensor = ("yl", "x", "c"), ("yh", "z")
    tokens, weight = P(dp + tensor, None), P(dp, tensor)
    heads, shared = P(tensor), P()
    return jax.shard_map(
        shards,
        mesh=fine,
        in_specs=(
            tokens, shared, weight, weight, P(dp, None), weight, P(None, tensor), heads,
            shared, shared, heads, heads, heads, heads, weight, tokens,
        ),
        out_specs=(
            tokens, tokens, shared, weight, weight, P(dp, None), weight, P(None, tensor), heads,
            shared, shared, heads, heads, heads, heads, weight,
        ),
        check_vma=False,
    )
```

time: 1150 us -> 217 us (0.19); the launches traced: 1140 us -> 217 us
  waiting for transfers between devices: 428 us -> 0 us
  blocking collectives: 208 us -> 0 us
  other arithmetic: 206 us -> 1.81 us
  Pallas kernels: 0 us -> 175 us
  matrix products: 157 us -> 28 us
  local copies, waits for them, and re-layouts: 121 us -> 10.9 us
  between operations: 15.4 us -> 0.77 us
    unnamed x17 -> x0, waiting for transfers between devices: 195 us -> none
    pallas_call x0 -> x5, Pallas kernels: none -> 175 us  [the longest x1 50.1 us: run_tail(): pl.pallas_call(tail_kernel, out_shape=[SHAPE((256, D), F32), SHAPE((96, C...]
    psum x4 -> x0, blocking collectives: 170 us -> none  [the longest x1 74 us: shards(): norm_gain_sum = lax.psum(grad_norm_part, ('dp', 'tensor'))]
    dot_general x20 -> x4, matrix products: 157 us -> 28 us  [the longest x2 16 us: dot_nt(): lax.dot_general(a, b, (((1,), (1,)), ((), ())), preferred_element_type=F32)]
    reduce_scatter x3 -> x0, waiting for transfers between devices: 123 us -> none  [the longest x1 64.1 us: shards(): lax.psum_scatter(grad_bc_w, 'dp', scatter_dimension=0, tiled=True)]
    all_gather x5 -> x0, waiting for transfers between devices: 110 us -> none  [the longest x1 85.8 us: shards(): normed_all = lax.all_gather(normed, 'tensor', axis=0, tiled=True)]
    another operation x8 -> x0, other arithmetic: 94.5 us -> none
    reduce_sum x13 -> x0, other arithmetic: 48.4 us -> none  [the longest x2 24.8 us: causal_conv(): weight[offset] * padded[:, offset:offset + values.shape[1], :]]
  transfers between devices with their start and end apart: 13 -> 0, of which waited for: 8 -> 0; matrix products, arithmetic and copies ran while one was open for 32% -> 0% of each run, Pallas kernels for 0% -> 0%
where the time goes in v2:
time: 217 us
  Pallas kernels  175 us (81%)
  matrix products  28 us (13%)
  local copies, waits for them, and re-layouts  10.9 us (5%)
    pallas_call x1, Pallas kernels, run_tail(): pl.pallas_call(tail_kernel, out_shape=[SHAPE((256, D), F32), SHAPE((96, C...  50.1 us
    pallas_call x1, Pallas kernels, run_gather(): pl.pallas_call(gather_kernel, out_shape=[SHAPE((LEN, D), BF16), SHAPE((2,...  43.5 us
    pallas_call x1, Pallas kernels, run_forward(): pl.pallas_call(forward_kernel, grid=(2 * BLOCKS,), out_shape=[wide, wide,...  41 us
    pallas_call x1, Pallas kernels, run_backward(): pl.pallas_call(backward_kernel, grid=(BLOCKS,), out_shape=[SHAPE((LEN, PR...  38.6 us
    dot_general x2, matrix products, dot_nt(): lax.dot_general(a, b, (((1,), (1,)), ((), ())), preferred_element_type=F32)  16 us
    dot_general x2, matrix products, dot_tn(): lax.dot_general(a, b, (((0,), (0,)), ((), ())), preferred_element_type=F32)  12.1 us
    unnamed x26, local copies, waits for them, and re-layouts  7.1 us

profile of v2, /device:TPU:0, one launch (start us, length us, event | category | flops | bytes accessed | tf_op | source)
XLA Modules:
  0.0 216.9 jit_solution(4081606131277916308)
XLA Ops:
  0.6 1.2 reshape.90.bias
  1.9 1.2 reshape.91.gate_gain
  3.1 1.3 reshape.89.gain
  4.4 1.4 copy.32.w_step
  5.8 43.5 %gather_all.1 = (bf16[1024,1536]{1,0:T(8,128)(2,1)}, bf16[2,4,2,96,1792]{4,3,2,1,0:T(8,128)(2,1)}, bf16[2,4,2,96,768]{4,3,2,1,0:T(8,128)(2,1)}, bf16[2,4,2,96,256]{4,3,2,1,0:T(8,128)(2,1)}, f32[2,16,384]{2,1,0:T(8,128)}) custom-call(bf16[256,1536]{1,0:T(8,128)(2,1)} %tokens.3, f32[1,1536]{1,0:T(1,128)} %reshape.89.gain, bf16[96,384]{1,0:T(8,128)(2,1)} %w_gate.1, ...), custom_call_target="tpu_custom_call" | custom-call | tf_op jit(solution)/shard_map/gather_all/pallas_call | solution.py:397
  49.3 0.0 copy-start.8
  49.3 41.0 %forward.1 = (f32[1024,768]{1,0:T(8,128)}, f32[1024,768]{1,0:T(8,128)}, f32[1024,768]{1,0:T(8,128)}, f32[1024,768]{1,0:T(8,128)}, f32[1024,768]{1,0:T(8,128)}, /...) custom-call(bf16[1024,1536]{1,0:T(8,128)(2,1)} %get-tuple-element.62, ...), custom_call_target="tpu_custom_call" | custom-call | tf_op jit(solution)/shard_map/forward/pallas_call | solution.py:566
  90.3 0.0 copy-done.8
  90.3 0.0 copy-start.10
  90.3 0.0 copy-start.11
  90.3 5.7 %convolution_convert_fusion.2.part = bf16[1024,1536]{1,0:T(8,128)(2,1)} fusion(bf16[1024,768]{1,0:T(8,128)(2,1)} %get-tuple-element.78, bf16[1536,768]{1,0:T(8,128)(2,1)S(1)} %bitcast.27), kind=kOutput, calls=%fused_computation.2 | convolution fusion | flops 2417491968 | bytes 7077888 | tf_op jit(solution)/shard_map/dot_general | solution.py:38
  96.0 0.0 copy-done.10
  96.0 0.0 copy-done.11
  96.0 3.9 %convolution_convert_fusion.3 = bf16[1536,768]{1,0:T(8,128)(2,1)} fusion(bf16[1024,1536]{1,0:T(8,128)(2,1)S(1)} %copy-done.10, bf16[1024,768]{1,0:T(8,128)(2,1)S(1)} %copy-done.11), kind=kOutput, calls=%fused_computation.3 | convolution fusion | flops 2417098752 | bytes 7077888 | tf_op jit(solution)/shard_map/dot_general | solution.py:42
  100.0 38.6 %backward.1 = (bf16[1024,1792]{1,0:T(8,128)(2,1)}, bf16[1024,256]{1,0:T(8,128)(2,1)}, f32[2,16,384]{2,1,0:T(8,128)}, bf16[256,1536]{1,0:T(8,128)(2,1)}, f32[96,384]{1,0:T(8,128)}) custom-call(f32[1024,768]{1,0:T(8,128)} %get-tuple-element.67.gm, f32[1024,768]{1,0:T(8,128)} %get-tuple-element.68.gate, f32[1024,768]{1,0:T(8,128)} %get-tuple-element.69.inner, ...), custom_call_target="tpu_custom_call" | custom-call | tf_op jit(solution)/shard_map/backward/pallas_call | solution.py:790
  138.5 0.0 copy-start.7
  138.6 0.0 copy-start.9
  138.6 10.3 %convolution_convert_fusion.1.gn = bf16[1024,1536]{1,0:T(8,128)(2,1)} fusion(bf16[1024,1792]{1,0:T(8,128)(2,1)} %get-tuple-element.80, bf16[1536,1792]{1,0:T(8,128)(2,1)} %bitcast.23), kind=kOutput, calls=%fused_computation.1 | convolution fusion | flops 5638717440 | bytes 12320768 | tf_op jit(solution)/shard_map/dot_general | solution.py:38
  148.9 0.0 copy-done.7
  148.9 0.0 copy-done.9
  148.9 8.1 %convolution_convert_fusion = bf16[1536,1792]{1,0:T(8,128)(2,1)} fusion(bf16[1024,1536]{1,0:T(8,128)(2,1)S(1)} %copy-done.7, bf16[1024,1792]{1,0:T(8,128)(2,1)S(1)} %copy-done.9), kind=kOutput, calls=%fused_computation | convolution fusion | flops 5639897088 | bytes 12320768 | tf_op jit(solution)/shard_map/dot_general | solution.py:42
  157.0 0.0 copy-start.1
  157.0 0.0 copy-start.3
  157.0 50.1 %tail.1 = (f32[256,1536]{1,0:T(8,128)}, f32[96,384]{1,0:T(8,128)}, f32[96,512]{1,0:T(8,128)}, f32[96,256]{1,0:T(8,128)}, f32[48,384]{1,0:T(8,128)}) custom-call(bf16[1024,1536]{1,0:T(8,128)(2,1)} %convolution_convert_fusion.1.gn, bf16[2,4,2,96,1792]{4,3,2,1,0:T(8,128)(2,1)} %bitcast.21, bf16[1024,256]{1,0:T(8,128)(2,1)} %get-tuple-element.81.dbc, ...), custom_call_target="tpu_custom_call" | custom-call | tf_op jit(solution)/shard_map/tail/pallas_call | solution.py:952
  207.1 0.0 copy-done.1
  207.1 0.0 copy-done.3
  207.1 0.0 copy-start
  207.1 1.4 copy-done
  208.5 0.0 copy-start.2
  208.5 0.9 copy-done.2
  209.5 0.0 copy-start.4
  209.5 0.9 copy-done.4
  210.4 0.0 copy-start.5
  210.4 0.9 copy-done.5
  211.3 0.0 copy-start.6
  211.3 0.9 copy-done.6
  212.2 2.2 %finish.1 = (f32[256,1536]{1,0:T(8,128)}, bf16[256,1536]{1,0:T(8,128)(2,1)}, f32[96,6]{1,0:T(8,128)S(1)}, f32[96,384]{1,0:T(8,128)}, f32[96,256]{1,0:T(8,128)}, ...) custom-call(f32[256,1536]{1,0:T(8,128)S(1)} %copy-done, ...), custom_call_target="tpu_custom_call" | custom-call | tf_op jit(solution)/shard_map/finish/pallas_call | solution.py:1026
  214.4 0.6 reduce.1
  215.0 0.6 reduce.2
  215.6 0.6 reduce
  216.2 0.7 copy.33
Async XLA Ops:
  49.3 41.0 %copy-start.8 = (bf16[2,4,2,96,768]{4,3,2,1,0:T(8,128)(2,1)S(1)}, bf16[2,4,2,96,768]{4,3,2,1,0:T(8,128)(2,1)}, u32[]{:S(2)}) copy-start(bf16[2,4,2,96,768]{4,3,2,1,0:T(8,128)(2,1)} %get-tuple-element.64) | copy-start | bytes 7077892
  90.3 5.7 %copy-start.10 = (bf16[1024,1536]{1,0:T(8,128)(2,1)S(1)}, bf16[1024,1536]{1,0:T(8,128)(2,1)}, u32[]{:S(2)}) copy-start(bf16[1024,1536]{1,0:T(8,128)(2,1)} %get-tuple-element.79) | copy-start | bytes 9437188
  90.3 5.7 %copy-start.11 = (bf16[1024,768]{1,0:T(8,128)(2,1)S(1)}, bf16[1024,768]{1,0:T(8,128)(2,1)}, u32[]{:S(2)}) copy-start(bf16[1024,768]{1,0:T(8,128)(2,1)} %get-tuple-element.78) | copy-start | bytes 4718596
  138.5 10.3 %copy-start.7 = (bf16[1024,1536]{1,0:T(8,128)(2,1)S(1)}, bf16[1024,1536]{1,0:T(8,128)(2,1)}, u32[]{:S(2)}) copy-start(bf16[1024,1536]{1,0:T(8,128)(2,1)} %get-tuple-element.62.x.normed) | copy-start | bytes 9437188
  138.6 10.3 %copy-start.9 = (bf16[1024,1792]{1,0:T(8,128)(2,1)S(1)}, bf16[1024,1792]{1,0:T(8,128)(2,1)}, u32[]{:S(2)}) copy-start(bf16[1024,1792]{1,0:T(8,128)(2,1)} %get-tuple-element.80) | copy-start | bytes 11010052
  157.0 50.1 %copy-start.1 = (bf16[256,1536]{1,0:T(8,128)(2,1)S(1)}, bf16[256,1536]{1,0:T(8,128)(2,1)}, u32[]{:S(2)}) copy-start(bf16[256,1536]{1,0:T(8,128)(2,1)} %get-tuple-element.86.branch) | copy-start | bytes 2359300
  157.0 50.1 %copy-start.3 = (f32[96,384]{1,0:T(8,128)S(1)}, f32[96,384]{1,0:T(8,128)}, u32[]{:S(2)}) copy-start(f32[96,384]{1,0:T(8,128)} %get-tuple-element.91.wout) | copy-start | bytes 442372
  207.1 1.4 copy-start
  208.5 0.9 copy-start.2
  209.5 0.9 copy-start.4
  210.4 0.9 copy-start.5
  211.3 0.9 copy-start.6

commit v3 on v2

--- a/solution.py
+++ b/solution.py
@@ -266,11 +266,10 @@
 
 
 class TokenSum:
-    def __init__(self, net, part, scratch):
-        self.net, self.half, self.fold, self.whole = net, *scratch
+    def __init__(self, net, scratch):
+        self.net, self.far, self.half, self.fold, self.whole = net, *scratch
         self.one = [
-            net.plan(lambda p=p: rows(part, net.near("z", 2) * 256 + 128 * p, 128), lambda p=p: self.half.at[p], "z", step)
-            for p, step in HALVES
+            net.plan(lambda p=p: self.far.at[pl.ds(128 * p, 128)], lambda p=p: self.half.at[p], "z", step) for p, step in HALVES
         ]
         self.two = [net.plan(lambda p=p: self.fold.at[p], lambda p=p: self.whole.at[p], "z", step) for p, step in HALVES]
 
@@ -290,24 +289,25 @@
 
 
 def token_scratch():
-    return [pltpu.VMEM((2, 128, D), BF16), pltpu.VMEM((2, 256, D), BF16), pltpu.VMEM((2, 256, D), BF16)]
-
-
-def gather_kernel(x, gain, w_gate, w_inner, w_out, w_bc, w_step, conv, bias, gate_gain, step_bias, decay_log, skip, normed_all, wx, wout, wbc, prm, xv, low, stepv, pk, send, recv, local):
+    return [pltpu.VMEM((256, D), BF16), pltpu.VMEM((2, 128, D), BF16), pltpu.VMEM((2, 256, D), BF16), pltpu.VMEM((2, 256, D), BF16)]
+
+
+def gather_kernel(x, gain, w_gate, w_inner, w_out, w_bc, w_step, conv, bias, gate_gain, step_bias, decay_log, skip, normed_all, wx, wout, wbc, prm, xv, low, stepv, stept, pk, send, recv, local):
     net = Net(send, recv)
     at = net.at
     yh, cx, cc, z, y = at["yh"], at["x"], at["c"], at["z"], at["y"]
     load = pltpu.make_async_copy(x, xv, local.at[0])
     load.start()
-    stepv[...] = jnp.zeros_like(stepv)
-    stepv[:, 0:HEADS] = w_step[...]
+    stept[...] = jnp.zeros_like(stept)
+    stept[0:HEADS, 0:96] = w_step[...].astype(F32)
+    stepv[...] = jnp.transpose(stept[...])[0:96, :].astype(BF16)
     pk[...] = jnp.zeros_like(pk)
     pk[0:4, :] = conv[...]
-    pk[4:5, :] = bias[...]
-    pk[5:6, :] = gate_gain[...]
-    pk[6:7, 0:HEADS] = step_bias[...]
-    pk[7:8, 0:HEADS] = decay_log[...]
-    pk[8:9, 0:HEADS] = skip[...]
+    pk[4:5, :] = bias[...].reshape(1, COLS)
+    pk[5:6, :] = gate_gain[...].reshape(1, COLS)
+    pk[6:7, 0:HEADS] = step_bias[...].reshape(1, HEADS)
+    pk[7:8, 0:HEADS] = decay_log[...].reshape(1, HEADS)
+    pk[8:9, 0:HEADS] = skip[...].reshape(1, HEADS)
     net.barrier([("z", 1), ("z", -1), ("x", 1), ("x", -1), ("y", 1), ("y", -1), ("y", 2), ("c", 1)])
     first = {
         "x": ((w_gate, wx, 0, COLS), (w_out, wout, 0, COLS)),
@@ -327,7 +327,7 @@
     load.wait()
     v = xv[...].astype(F32)
     root = lax.rsqrt(jnp.mean(v * v, axis=1, keepdims=True) + EPS)
-    low[...] = (v * root * gain[...]).astype(BF16)
+    low[...] = (v * root * gain[...].reshape(1, D)).astype(BF16)
     zs = [net.start(low, rows(normed_all, z * 256, 256), "z", step) for _, step in HALVES]
     own.append(pltpu.make_async_copy(low, rows(normed_all, z * 256, 256), local.at[7]))
     for copy in own:
@@ -409,6 +409,7 @@
             pltpu.VMEM((256, D), BF16),
             pltpu.VMEM((256, D), BF16),
             pltpu.VMEM((96, 128), BF16),
+            pltpu.VMEM((128, 128), F32),
             pltpu.VMEM((16, COLS), F32),
         ]
         + sems(96)
@@ -420,7 +421,7 @@
 
 def forward_kernel(
     x, wx, wout, wbc, prm, conv_bc, bias_bc, cot,
-    gate_out, inner_out, z_out, y_out, gm_out, mixed_out, h_out, dt_out, r_out, u_out, bc_out, bcin_out, zbc_out, stats_out, cot_all,
+    gate_out, inner_out, z_out, y_out, gm_out, mixed_out, h_out, dt_out, r_out, u_out, bc_out, bcin_out, zbc_out, stats_out, normed_t, cot_t,
     cots, gps, ext, extbc, state, stat, slots, send, recv, local,
 ):
     i = pl.program_id(0)
@@ -432,7 +433,6 @@
     c2 = [net.plan(lambda p=p, s=s: part(p, s), lambda p=p, s=s: part(p, s), "z", s) for p, s in HALVES]
     q = [net.plan(lambda: stat, lambda: slots.at[z], "z", step) for step in (1, -1, 2)]
     own = lambda: pltpu.make_async_copy(cot, here(), local.at[0])
-    out = lambda: pltpu.make_async_copy(cots, cot_all, local.at[1])
 
     @pl.when(i == 0)
     def _():
@@ -459,6 +459,9 @@
     @pl.when(i < BLOCKS)
     def _():
         xb = x[...]
+        turned = jnp.transpose(xb).reshape(2, 4, 2, 96, BLOCK)
+        for core in range(2):
+            normed_t[core] = turned[:, :, core]
         bc_in = dot(xb, wbc[...])
         bcin_out[...] = bc_in
         extbc[8 : BLOCK + 8, :] = bc_in
@@ -522,14 +525,17 @@
     def _():
         for copy in c2:
             copy.arrived()
-        out().start()
 
     @pl.when(i >= BLOCKS)
     def _():
         t = i - BLOCKS
         block = lax.rem(z + t + lax.div(t, 2) - 2 * lax.div(t, 3), 4)
         at = pl.ds(pl.multiple_of(block * BLOCK, BLOCK), BLOCK)
-        gm = dot(cots[at, :], wout[...])
+        cb = cots[at, :]
+        turned = jnp.transpose(cb).reshape(2, 4, 2, 96, BLOCK)
+        for core in range(2):
+            cot_t[core, :, :, :, at] = turned[:, :, core]
+        gm = dot(cb, wout[...])
         gm_out[at, :] = gm
         gain = jnp.concatenate([prm[0, 5:6, :], prm[1, 5:6, :]], axis=1)
         stat[pl.ds(BLOCKS + block, 1), :] = token_row(gm * gain * gps[at, :])
@@ -552,7 +558,6 @@
             mixed_out[at, :] = (gps[at, :] * columns[:, k : k + 1] * gain).astype(BF16)
         for copy in c1 + c2 + q:
             copy.left()
-        out().wait()
 
 
 def run_forward(x, wx, wout, wbc, prm, conv_bc, bias_bc, cot):
@@ -581,7 +586,8 @@
             SHAPE((LEN, 256), F32),
             SHAPE((LEN, 256), F32),
             SHAPE((8, 256), F32),
-            SHAPE((LEN, D), BF16),
+            SHAPE((2, 2, 4, 96, LEN), BF16),
+            SHAPE((2, 2, 4, 96, LEN), BF16),
         ],
         in_specs=[
             block(D),
@@ -608,7 +614,8 @@
             block(256),
             block(256),
             keep(8, 256),
-            ANY,
+            pl.BlockSpec((2, 2, 4, 96, BLOCK), lambda k: (0, 0, 0, 0, first(k))),
+            keep(2, 2, 4, 96, LEN),
         ],
         scratch_shapes=[
             pltpu.VMEM((LEN, D), BF16),
@@ -620,37 +627,43 @@
             pltpu.VMEM((4, 8, BLOCK), F32),
         ]
         + sems(7)
-        + [pltpu.SemaphoreType.DMA((2,))],
+        + [pltpu.SemaphoreType.DMA((1,))],
         compiler_params=pltpu.CompilerParams(collective_id=1, has_side_effects=True, vmem_limit_bytes=ROOM),
         name="forward",
     )(x, wx, wout, wbc, prm, conv_bc, bias_bc, cot)
 
 
 def backward_kernel(
-    gm, gate, inner, zin, y, hin, prm, bc, dt, r, u, stats, part, dout, tokens,
+    gm, gate, inner, zin, y, hin, prm, bc, dt, r, u, stats, mixed, wout, cot_t, tokens,
     cat_out, dbc_out, acc, branch_out, wout_out,
-    ext, dstate, dst, dbc, held, got, g1, g2, g3, s1, s2, s3, s4, s5, s6, s7, send, recv, local,
+    ext, dstate, dst, dbc, held, got, away, mv, wv, cv, ownb, g0, g1, g2, g3, s1, s2, s3, s4, s5, s6, s7, send, recv, local,
 ):
     k = pl.program_id(0)
     net = Net(send, recv)
     cc, z = net.at["c"], net.at["z"]
-    cross = net.plan(lambda: dout.at[:, :, net.other], lambda: got, "c")
-    token = TokenSum(net, part, (g1, g2, g3))
+    cross = net.plan(lambda: away, lambda: got, "c")
+    token = TokenSum(net, (g0, g1, g2, g3))
     ring = RingSum(net, "y", held, ((0, COLS),), (s1, s2, s3, s4, s5, s6, s7))
-    loads = lambda: [
-        pltpu.make_async_copy(dout.at[:, :, cc], held, local.at[0]),
-        pltpu.make_async_copy(rows(part, net.near("z", 1) * 256, 256), g2.at[0], local.at[1]),
-        pltpu.make_async_copy(rows(part, net.near("z", -1) * 256, 256), g2.at[1], local.at[2]),
-        pltpu.make_async_copy(rows(part, z * 256, 256), branch_out, local.at[3]),
-    ]
 
     @pl.when(k == 0)
     def _():
         net.barrier([("z", 1), ("z", -1), ("x", 1), ("x", -1), ("y", 1), ("y", -1), ("c", 1)])
+        loads = [pltpu.make_async_copy(src, dst, local.at[n]) for n, (src, dst) in enumerate(((mixed, mv), (wout, wv), (cot_t, cv)))]
+        for copy in loads:
+            copy.start()
+        loads[0].wait()
+        loads[1].wait()
+        branch = lambda place: dot_nt(mv[pl.ds(pl.multiple_of(place * 256, 256), 256), :], wv[...])
+        grads = lambda core: dot(cv[core].reshape(8 * 96, LEN), mv[...]).astype(BF16).reshape(2, 4, 96, WIDE)
+        g0[...] = branch(net.near("z", 2)).astype(BF16)
+        token.step1()
+        loads[2].wait()
+        away[...] = grads(net.other)
         cross.start()
-        token.step1()
-        for copy in loads():
-            copy.start()
+        g2[0] = branch(net.near("z", 1)).astype(BF16)
+        g2[1] = branch(net.near("z", -1)).astype(BF16)
+        ownb[...] = branch(z)
+        held[...] = grads(cc)
         acc[...] = jnp.zeros_like(acc)
         ext[BLOCK : BLOCK + 8, :] = jnp.zeros((8, WIDE), F32)
         dstate[...] = jnp.zeros_like(dstate)
@@ -675,29 +688,27 @@
 
             @pl.when(k == 1)
             def _():
+                cross.arrived()
+                held[...] += got[...]
+                ring.step1()
+
+            @pl.when(k == 3)
+            def _():
+                ring.step4()
+
+        else:
+
+            @pl.when(k == 0)
+            def _():
+                token.step2()
+
+            @pl.when(k == 1)
+            def _():
                 ring.step2()
 
             @pl.when(k == 2)
             def _():
                 ring.step3()
-
-        else:
-
-            @pl.when(k == 0)
-            def _():
-                for copy in loads():
-                    copy.wait()
-                cross.arrived()
-                held[...] += got[...]
-                ring.step1()
-
-            @pl.when(k == 1)
-            def _():
-                token.step2()
-
-            @pl.when(k == 2)
-            def _():
-                ring.step4()
 
         cut = slice(g * COLS, (g + 1) * COLS)
         yv = y[:, cut]
@@ -776,13 +787,12 @@
     @pl.when(k == BLOCKS - 1)
     def _():
         wout_out[...] = ring.step5()
-        branch = branch_out[...].astype(F32) + token.step3()
-        branch_out[...] = (tokens[...].astype(F32) + branch).astype(BF16)
+        branch_out[...] = (tokens[...].astype(F32) + (ownb[...] + token.step3())).astype(BF16)
         for copy in net.copies:
             copy.left()
 
 
-def run_backward(gm, gate, inner, zin, y, hin, prm, bc, dt, r, u, stats, part, dout, tokens):
+def run_backward(gm, gate, inner, zin, y, hin, prm, bc, dt, r, u, stats, mixed, wout, cot_t, tokens):
     rev = lambda k: BLOCKS - 1 - k
     cols = lambda n: pl.BlockSpec((BLOCK, n), lambda k: (rev(k), 0))
     small = lambda: pl.BlockSpec((GROUPS, BLOCK, 128), lambda k: (0, rev(k), 0))
@@ -808,6 +818,7 @@
             keep(8, 256),
             ANY,
             ANY,
+            ANY,
             keep(256, D),
         ],
         out_specs=[cols(PROJ), cols(256), keep(GROUPS, 16, COLS), keep(256, D), keep(96, COLS)],
@@ -818,59 +829,75 @@
             pltpu.VMEM((BLOCK, 256), F32),
             pltpu.VMEM((2, 4, 96, WIDE), BF16),
             pltpu.VMEM((2, 4, 96, WIDE), BF16),
+            pltpu.VMEM((2, 4, 96, WIDE), BF16),
+            pltpu.VMEM((LEN, WIDE), BF16),
+            pltpu.VMEM((D, WIDE), BF16),
+            pltpu.VMEM((2, 2, 4, 96, LEN), BF16),
+            pltpu.VMEM((256, D), F32),
         ]
         + token_scratch()
         + ring_scratch("y", COLS)
         + sems(13)
-        + [pltpu.SemaphoreType.DMA((4,))],
+        + [pltpu.SemaphoreType.DMA((3,))],
         compiler_params=pltpu.CompilerParams(collective_id=2, has_side_effects=True, vmem_limit_bytes=ROOM),
         name="backward",
-    )(gm, gate, inner, zin, y, hin, prm, bc, dt, r, u, stats, part, dout, tokens)
+    )(gm, gate, inner, zin, y, hin, prm, bc, dt, r, u, stats, mixed, wout, cot_t, tokens)
 
 
 def tail_kernel(
-    gn, dcat, dbc, zbc, bc_in, normed, acc, wbc, tokens, cot, gain, conv,
+    cat, wx, normed_t, normed, dbc, zbc, bc_in, acc, wbc, tokens, cot, gain, conv,
     tokens_out, gate_out, inner_out, bc_out, small_out,
-    gnv, nv, mine, slots, zv, xi, wv, xv, ov, ext, gnbc, held, got, dbw, heldb, gotb, small, sp0, sp1, sp2, sp3, bz, by,
-    g1, g2, g3, a1, a2, a3, a4, a5, a6, a7, b1, b2, b3, b4, b5, b6, b7, c1, c2, c3, c4, c5, c6, c7, send, recv, local,
+    catv, wxv, ntv, nv, mine, slots, zv, xi, wv, xv, ov, ext, gnbc, ownb, held, got, away, dbw, heldb, gotb, small, sp0, sp1, sp2, sp3, bz, by,
+    g0, g1, g2, g3, a1, a2, a3, a4, a5, a6, a7, b1, b2, b3, b4, b5, b6, b7, c1, c2, c3, c4, c5, c6, c7, send, recv, local,
 ):
     net = Net(send, recv)
     at = net.at
     yh, cx, cc, z, y = at["yh"], at["x"], at["c"], at["z"], at["y"]
-    loads = [
-        pltpu.make_async_copy(src, dst, local.at[i])
-        for i, (src, dst) in enumerate(
-            (
-                (dcat.at[:, :, cc], held),
-                (rows(gn, net.near("z", 1) * 256, 256), g2.at[0]),
-                (rows(gn, net.near("z", -1) * 256, 256), g2.at[1]),
-                (gn, gnv),
-                (normed, nv),
-                (rows(zbc, z * 256, 256), zv.at[pl.ds(0, 256)]),
-                (rows(zbc, lax.rem(z * 256 + 256, LEN), 16), zv.at[pl.ds(256, 16)]),
-                (rows(bc_in, z * 256, 256), xi),
-                (wbc, wv),
-                (tokens, xv),
-                (cot, ov),
-            )
-        )
-    ]
-    token = TokenSum(net, gn, (g1, g2, g3))
+    pairs = (
+        (cat, catv),
+        (wx, wxv),
+        (normed, nv),
+        (normed_t, ntv),
+        (rows(zbc, z * 256, 256), zv.at[pl.ds(0, 256)]),
+        (rows(zbc, lax.rem(z * 256 + 256, LEN), 16), zv.at[pl.ds(256, 16)]),
+        (rows(bc_in, z * 256, 256), xi),
+        (wbc, wv),
+        (tokens, xv),
+        (cot, ov),
+    )
+    loads = [pltpu.make_async_copy(src, dst, local.at[i]) for i, (src, dst) in enumerate(pairs)]
+    for copy in loads:
+        copy.start()
+    token = TokenSum(net, (g0, g1, g2, g3))
     ring_gate = RingSum(net, "x", held, ((0, COLS),), (a1, a2, a3, a4, a5, a6, a7))
     ring_inner = RingSum(net, "y", held, ((WIDE, COLS), (STEPS, 128)), (b1, b2, b3, b4, b5, b6, b7))
     ring_bc = RingSum(net, "x", heldb, ((0, 128),), (c1, c2, c3, c4, c5, c6, c7))
-    net.barrier([(a, s) for a in ("z", "x", "y") for s in (1, -1, 2)] + [("c", 1)])
-    cross = net.start(dcat.at[:, :, net.other], got, "c")
     mine[0:LEN, :] = dbc[...]
     mine[LEN : LEN + 16, :] = jnp.zeros((16, 256), BF16)
+    slots[z] = mine[pl.ds(pl.multiple_of(z * 256, 16), 272), :]
+    net.barrier([(a, s) for a in ("z", "x", "y") for s in (1, -1, 2)] + [("c", 1)])
     swap = [net.start(rows(mine, net.near("z", s) * 256, 272), slots.at[z], "z", s) for s in (1, -1, 2)]
+    gain_row = gain[...].reshape(1, D)
+    norm_part = jnp.zeros((1, D), F32)
+
+    def block(place):
+        cut = pl.ds(pl.multiple_of(place * 256, 256), 256)
+        got = dot_nt(catv[cut, :], wxv[...])
+        return got, jnp.sum(got * nv[cut, :].astype(F32), axis=0, keepdims=True)
+
+    for copy in loads[:3]:
+        copy.wait()
+    out, part = block(net.near("z", 2))
+    norm_part = norm_part + part
+    g0[...] = out.astype(BF16)
     token.step1()
-    for copy in loads:
-        copy.start()
-    slots[z] = mine[pl.ds(pl.multiple_of(z * 256, 16), 272), :]
+    grads = lambda core: dot(ntv[core].reshape(8 * 96, LEN), catv[...]).astype(BF16).reshape(2, 4, 96, PROJ)
+    loads[3].wait()
+    away[...] = grads(net.other)
+    cross = net.start(away, got, "c")
+    for copy in loads[4:]:
+        copy.wait()
     arrive(swap)
-    for copy in loads:
-        copy.wait()
     total = (slots[0].astype(F32) + slots[1].astype(F32)) + (slots[2].astype(F32) + slots[3].astype(F32))
     sig = sigmoid(zv[...])
     dz = total * (sig * (1.0 + zv[...] * (1.0 - sig)))
@@ -885,68 +912,71 @@
         small[36 + j : 37 + j, 0:256] = jnp.sum(xi[...] * moved, axis=0, keepdims=True)
     small[40:41, 0:256] = jnp.sum(ext[0:256, :], axis=0, keepdims=True)
     gbc = gbc.astype(BF16)
-    own = pl.ds(pl.multiple_of(z * 256, 16), 256)
-    dbw[...] = dot_tn(nv[own, :], gbc).astype(BF16).reshape(2, 4, 2, 96, 256)
-    crossb = net.start(dbw.at[:, :, net.other], gotb, "c")
+    own = pl.ds(pl.multiple_of(z * 256, 256), 256)
+    for core in range(2):
+        dbw[core] = dot(ntv[core, :, :, :, own].reshape(8 * 96, 256), gbc).astype(BF16).reshape(2, 4, 96, 256)
+    crossb = net.start(dbw.at[net.other], gotb, "c")
     gnbc[...] = dot_nt(gbc, wv[...])
-    gain_row = gain[...]
-    part = jnp.sum(gnbc[...] * nv[own, :].astype(F32), axis=0, keepdims=True)
-    for k in range(BLOCKS):
-        cut = slice(k * 256, (k + 1) * 256)
-        part = part + jnp.sum(gnv[cut, :].astype(F32) * nv[cut, :].astype(F32), axis=0, keepdims=True)
-    part = part / gain_row
-    for k in range(4):
-        small[32 + k : 33 + k, :] = part[:, k * COLS : (k + 1) * COLS]
-    sp0[z] = small[32:48, :]
-    q = net.around(sp0.at[z], sp0.at[z], "z")
+    norm_part = norm_part + jnp.sum(gnbc[...] * nv[own, :].astype(F32), axis=0, keepdims=True)
+    for p, step in HALVES:
+        out, part = block(net.near("z", step))
+        norm_part = norm_part + part
+        g2[p] = out.astype(BF16)
+    token.step2()
+    held[...] = grads(cc)
     cross.arrived()
     held[...] += got[...]
     ring_inner.step1()
     ring_gate.step1()
-    token.step2()
     crossb.arrived()
-    heldb[...] = dbw[:, :, cc] + gotb[...]
+    heldb[...] = dbw[cc] + gotb[...]
     ring_bc.step1()
+    out, part = block(z)
+    norm_part = (norm_part + part) / gain_row
+    ownb[...] = out + gnbc[...]
+    for k in range(4):
+        small[32 + k : 33 + k, :] = norm_part[:, k * COLS : (k + 1) * COLS]
+    sp0[z] = small[32:48, :]
+    q = net.around(sp0.at[z], sp0.at[z], "z")
+    ring_gate.step2()
+    ring_inner.step2()
+    ring_bc.step2()
     arrive(q)
     sp1[cx, 0:32, :] = small[0:32, :]
     sp1[cx, 32:48, :] = (sp0[0] + sp0[1]) + (sp0[2] + sp0[3])
     q = net.around(sp1.at[cx], sp1.at[cx], "x")
-    ring_gate.step2()
-    ring_inner.step2()
-    ring_bc.step2()
+    ring_bc.step3()
     arrive(q)
     sp2[y] = (sp1[0] + sp1[1]) + (sp1[2] + sp1[3])
     q = net.around(sp2.at[y], sp2.at[y], "y")
-    ring_bc.step3()
+    ring_bc.step4()
+    arrive(q)
+    sp3[cc] = (sp2[0] + sp2[1]) + (sp2[2] + sp2[3])
+    q = [net.start(sp3.at[cc], sp3.at[cc], "c")]
+    bz[z] = ring_bc.step5()
+    q += net.around(bz.at[z], bz.at[z], "z")
     ring_gate.step3()
     ring_inner.step3()
     arrive(q)
-    sp3[cc] = (sp2[0] + sp2[1]) + (sp2[2] + sp2[3])
-    q = [net.start(sp3.at[cc], sp3.at[cc], "c")]
-    ring_bc.step4()
+    small_out[...] = sp3[0] + sp3[1]
+    by[yh] = (bz[0] + bz[1]) + (bz[2] + bz[3])
+    q = [net.start(by.at[yh], by.at[yh], "y", 2)]
     ring_gate.step4()
     ring_inner.step4()
     arrive(q)
-    small_out[...] = sp3[0] + sp3[1]
-    bz[z] = ring_bc.step5()
-    q = net.around(bz.at[z], bz.at[z], "z")
+    bc_out[:, :128] = by[0]
+    bc_out[:, 128:] = by[1]
     gate_out[...] = ring_gate.step5()
     inner_out[...] = ring_inner.step5()
-    arrive(q)
-    by[yh] = (bz[0] + bz[1]) + (bz[2] + bz[3])
-    q = [net.start(by.at[yh], by.at[yh], "y", 2)]
     v = xv[...].astype(F32)
     root = lax.rsqrt(jnp.mean(v * v, axis=1, keepdims=True) + EPS)
-    g = token.step3() + gnv[own, :].astype(F32) + gnbc[...]
+    g = token.step3() + ownb[...]
     scaled = g * gain_row
     tokens_out[...] = ov[...].astype(F32) + root * scaled - v * (root * root * root) * jnp.mean(scaled * v, axis=1, keepdims=True)
-    arrive(q)
-    bc_out[:, :128] = by[0]
-    bc_out[:, 128:] = by[1]
     net.finish()
 
 
-def run_tail(gn, dcat, dbc, zbc, bc_in, normed, acc, wbc, tokens, cot, gain, conv):
+def run_tail(*args):
     bf = lambda *s: pltpu.VMEM(s, BF16)
     f32 = lambda *s: pltpu.VMEM(s, F32)
     return pl.pallas_call(
@@ -958,10 +988,12 @@
             SHAPE((96, 256), F32),
             SHAPE((48, COLS), F32),
         ],
-        in_specs=[ANY, ANY, VMEM, ANY, ANY, ANY, VMEM, ANY, ANY, ANY, VMEM, VMEM],
+        in_specs=[ANY] * 4 + [VMEM, ANY, ANY, VMEM, ANY, ANY, ANY, VMEM, VMEM],
         out_specs=[VMEM] * 5,
         scratch_shapes=[
-            bf(LEN, D),
+            bf(LEN, PROJ),
+            bf(D, PROJ),
+            bf(2, 2, 4, 96, LEN),
             bf(LEN, D),
             bf(LEN + 16, 256),
             bf(4, 272, 256),
@@ -972,9 +1004,11 @@
             bf(256, D),
             f32(272, 256),
             f32(256, D),
+            f32(256, D),
             bf(2, 4, 96, PROJ),
             bf(2, 4, 96, PROJ),
-            bf(2, 4, 2, 96, 256),
+            bf(2, 4, 96, PROJ),
+            bf(2, 2, 4, 96, 256),
             bf(2, 4, 96, 256),
             bf(2, 4, 96, 256),
             f32(48, COLS),
@@ -990,10 +1024,10 @@
         + ring_scratch("y", COLS + 128)
         + ring_scratch("x", 128)
         + sems(64)
-        + [pltpu.SemaphoreType.DMA((11,))],
+        + [pltpu.SemaphoreType.DMA((10,))],
         compiler_params=pltpu.CompilerParams(collective_id=3, has_side_effects=True, vmem_limit_bytes=ROOM),
         name="tail",
-    )(gn, dcat, dbc, zbc, bc_in, normed, acc, wbc, tokens, cot, gain, conv)
+    )(*args)
 
 
 def finish_kernel(tokens, branch, inner, bc, small, gate, wout, tokens_out, branch_out, step_out, inner_out, bc_out, gate_out, wout_out, norm, conv, bias, conv_bc, bias_bc, step_bias, decay, skip, gain, sem):
@@ -1005,18 +1039,17 @@
     ]
     for copy in big:
         copy.start()
-    step_out[...] = inner[:, COLS : COLS + HEADS]
-    for k in range(4):
-        norm[:, k * COLS : (k + 1) * COLS] = small[32 + k : 33 + k, :]
+    step_out[...] = jnp.transpose(jnp.concatenate([inner[:, COLS:], jnp.zeros((32, 128), F32)], axis=0))[0:HEADS, 0:96]
+    norm[...] = jnp.concatenate([small[32 + k : 33 + k, :] for k in range(4)], axis=1).reshape(D)
     conv_bc[...] = small[36:40, 0:256]
-    bias_bc[...] = small[40:41, 0:256]
+    bias_bc[...] = small[40:41, 0:256].reshape(256)
     mine = small[pl.ds(pl.multiple_of(lax.axis_index("yh") * 16, 8), 16), :]
     conv[...] = mine[0:4, :]
-    bias[...] = mine[4:5, :]
-    gain[...] = mine[5:6, :]
-    step_bias[...] = mine[6:7, 0:HEADS]
-    decay[...] = mine[7:8, 0:HEADS]
-    skip[...] = mine[8:9, 0:HEADS]
+    bias[...] = mine[4:5, :].reshape(COLS)
+    gain[...] = mine[5:6, :].reshape(COLS)
+    step_bias[...] = mine[6:7, 0:HEADS].reshape(HEADS)
+    decay[...] = mine[7:8, 0:HEADS].reshape(HEADS)
+    skip[...] = mine[8:9, 0:HEADS].reshape(HEADS)
     for copy in big:
         copy.wait()
 
@@ -1028,53 +1061,48 @@
         out_shape=[
             f32(256, D),
             SHAPE((256, D), BF16),
-            f32(96, HEADS),
+            f32(HEADS, 96),
             f32(96, COLS),
             f32(96, 256),
             f32(96, COLS),
             f32(96, COLS),
-            f32(1, D),
+            f32(D),
             f32(4, COLS),
-            f32(1, COLS),
+            f32(COLS),
             f32(4, 256),
-            f32(1, 256),
-            f32(1, HEADS),
-            f32(1, HEADS),
-            f32(1, HEADS),
-            f32(1, COLS),
+            f32(256),
+            f32(HEADS),
+            f32(HEADS),
+            f32(HEADS),
+            f32(COLS),
         ],
         in_specs=[ANY, ANY, VMEM, ANY, VMEM, ANY, ANY],
         out_specs=[ANY, ANY, VMEM] + [ANY] * 4 + [VMEM] * 9,
         scratch_shapes=[pltpu.SemaphoreType.DMA((6,))],
-        compiler_params=pltpu.CompilerParams(vmem_limit_bytes=16 * 2**20),
+        compiler_params=pltpu.CompilerParams(vmem_limit_bytes=ROOM),
         name="finish",
     )(tokens, branch, inner, bc, small, gate, wout)
 
 
 def shards(tokens, norm_gain, w_gate, w_inner, w_bc, w_step, conv_inner, bias_inner, conv_bc, bias_bc, step_bias, decay_log, skip_gain, gate_gain, w_out, cotangent):
-    row = lambda v: v.reshape(1, -1)
-    gain = row(norm_gain)
     normed, wx, wout, wbc, prm = run_gather(
-        tokens, gain, w_gate, w_inner, w_out, w_bc, w_step, conv_inner, row(bias_inner), row(gate_gain), row(step_bias), row(decay_log), row(skip_gain)
+        tokens, norm_gain, w_gate, w_inner, w_out, w_bc, w_step.T, conv_inner, bias_inner, gate_gain, step_bias, decay_log, skip_gain
     )
     wx, wout, wbc = wx.reshape(D, PROJ), wout.reshape(D, WIDE), wbc.reshape(D, 256)
-    gate, inner, zin, y, gm, mixed, hin, dt, r, u, bc, bc_in, zbc, stats, cot_all = run_forward(
-        normed, wx, wout, wbc, prm, conv_bc, row(bias_bc), cotangent
+    gate, inner, zin, y, gm, mixed, hin, dt, r, u, bc, bc_in, zbc, stats, normed_t, cot_t = run_forward(
+        normed, wx, wout, wbc, prm, conv_bc, bias_bc.reshape(1, 256), cotangent
     )
-    part = dot_nt(mixed, wout).astype(BF16)
-    dout = dot_tn(cot_all, mixed).astype(BF16).reshape(2, 4, 2, 96, WIDE)
-    cat, dbc, acc, output, wout_grad = run_backward(gm, gate, inner, zin, y, hin, prm, bc, dt, r, u, stats, part, dout, tokens)
-    gn = dot_nt(cat, wx).astype(BF16)
-    dcat = dot_tn(normed, cat).astype(BF16).reshape(2, 4, 2, 96, PROJ)
-    tokens_grad, gate_grad, inner_grad, bc_grad, small = run_tail(gn, dcat, dbc, zbc, bc_in, normed, acc, wbc, tokens, cotangent, gain, conv_bc)
+    cat, dbc, acc, output, wout_grad = run_backward(gm, gate, inner, zin, y, hin, prm, bc, dt, r, u, stats, mixed, wout, cot_t, tokens)
+    tokens_grad, gate_grad, inner_grad, bc_grad, small = run_tail(
+        cat, wx, normed_t, normed, dbc, zbc, bc_in, acc, wbc, tokens, cotangent, norm_gain, conv_bc
+    )
     (
         tokens_grad, output, step_grad, inner_grad, bc_grad, gate_grad, wout_grad,
         norm, conv, bias, conv_bc_grad, bias_bc_grad, step_bias_grad, decay, skip, gate_gain_grad,
     ) = run_finish(tokens_grad, output, inner_grad, bc_grad, small, gate_grad, wout_grad)
-    flat = lambda v: v.reshape(-1)
     return (
-        output, tokens_grad, flat(norm), gate_grad, inner_grad, bc_grad, step_grad, conv, flat(bias), conv_bc_grad,
-        flat(bias_bc_grad), flat(step_bias_grad), flat(decay), flat(skip), flat(gate_gain_grad), wout_grad,
+        output, tokens_grad, norm, gate_grad, inner_grad, bc_grad, step_grad.T, conv, bias, conv_bc_grad,
+        bias_bc_grad, step_bias_grad, decay, skip, gate_gain_grad, wout_grad,
     )
 
 

time: 217 us -> 281 us (1.29)
  Pallas kernels: 175 us -> 280 us
  matrix products: 28 us -> 0 us
  local copies, waits for them, and re-layouts: 10.9 us -> 0 us
    pallas_call x1, Pallas kernels: 2.23 us -> 86.2 us  [run_finish(): pl.pallas_call(finish_kernel, out_shape=[f32(256, D), SHAPE((256, D), BF1...]
    dot_general x4 -> x0, matrix products: 28 us -> none  [the longest x2 16 us: dot_nt(): lax.dot_general(a, b, (((1,), (1,)), ((), ())), preferred_element_type=F32)]
    pallas_call x1, Pallas kernels: 50.1 us -> 61.4 us  [run_tail(): pl.pallas_call(tail_kernel, out_shape=[SHAPE((256, D), F32), SHAPE((96, C...]
    pallas_call x1, Pallas kernels: 38.6 us -> 46.8 us  [run_backward(): pl.pallas_call(backward_kernel, grid=(BLOCKS,), out_shape=[SHAPE((LEN, PR...]
    unnamed x26 -> x0, local copies, waits for them, and re-layouts: 7.1 us -> none
    reshape x3 -> x0, local copies, waits for them, and re-layouts: 3.78 us -> none  [shards(): row = lambda v: v.reshape(1, -1)]
where the time goes in v3:
time: 281 us
  Pallas kernels  280 us (100%)
    pallas_call x1, Pallas kernels, run_finish(): pl.pallas_call(finish_kernel, out_shape=[f32(256, D), SHAPE((256, D), BF1...  86.2 us
    pallas_call x1, Pallas kernels, run_tail(): pl.pallas_call(tail_kernel, out_shape=[SHAPE((256, D), F32), SHAPE((96, C...  61.4 us
    pallas_call x1, Pallas kernels, run_backward(): pl.pallas_call(backward_kernel, grid=(BLOCKS,), out_shape=[SHAPE((LEN, PR...  46.8 us
    pallas_call x1, Pallas kernels, run_gather(): pl.pallas_call(gather_kernel, out_shape=[SHAPE((LEN, D), BF16), SHAPE((2,...  43.6 us
    pallas_call x1, Pallas kernels, run_forward(): pl.pallas_call(forward_kernel, grid=(2 * BLOCKS,), out_shape=[wide, wide,...  41.9 us

profile of v3, /device:TPU:0, one launch (start us, length us, event | category | flops | bytes accessed | tf_op | source)
XLA Modules:
  0.0 280.8 jit_solution(16236324713154810183)
XLA Ops:
  0.7 43.6 %gather_all.1 = (bf16[1024,1536]{1,0:T(8,128)(2,1)}, bf16[2,4,2,96,1792]{4,3,2,1,0:T(8,128)(2,1)}, bf16[2,4,2,96,768]{4,3,2,1,0:T(8,128)(2,1)}, bf16[2,4,2,96,256]{4,3,2,1,0:T(8,128)(2,1)}, f32[2,16,384]{2,1,0:T(8,128)}) custom-call(bf16[256,1536]{1,0:T(8,128)(2,1)} %tokens.3, f32[1536]{0:T(1024)} %gain.3, bf16[96,384]{1,0:T(8,128)(2,1)} %w_gate.1, ...), custom_call_target="tpu_custom_call" | custom-call | tf_op jit(solution)/shard_map/gather_all/pallas_call | solution.py:397
  44.2 41.9 %forward.1 = (f32[1024,768]{1,0:T(8,128)}, f32[1024,768]{1,0:T(8,128)}, f32[1024,768]{1,0:T(8,128)}, f32[1024,768]{1,0:T(8,128)}, f32[1024,768]{1,0:T(8,128)}, /...) custom-call(bf16[1024,1536]{1,0:T(8,128)(2,1)} %get-tuple-element.63, ...), custom_call_target="tpu_custom_call" | custom-call | tf_op jit(solution)/shard_map/forward/pallas_call | solution.py:571
  86.2 46.8 %backward.1 = (bf16[1024,1792]{1,0:T(8,128)(2,1)}, bf16[1024,256]{1,0:T(8,128)(2,1)}, f32[2,16,384]{2,1,0:T(8,128)}, bf16[256,1536]{1,0:T(8,128)(2,1)}, f32[96,384]{1,0:T(8,128)}) custom-call(f32[1024,768]{1,0:T(8,128)} %get-tuple-element.68.gm, f32[1024,768]{1,0:T(8,128)} %get-tuple-element.69.gate, f32[1024,768]{1,0:T(8,128)} %get-tuple-element.70.inner, ...), custom_call_target="tpu_custom_call" | custom-call | tf_op jit(solution)/shard_map/backward/pallas_call | solution.py:800
  133.0 61.4 %tail.1 = (f32[256,1536]{1,0:T(8,128)}, f32[96,384]{1,0:T(8,128)}, f32[96,512]{1,0:T(8,128)}, f32[96,256]{1,0:T(8,128)}, f32[48,384]{1,0:T(8,128)}) custom-call(bf16[1024,1792]{1,0:T(8,128)(2,1)} %get-tuple-element.81.cat, bf16[1536,1792]{1,0:T(8,128)(2,1)} %bitcast.7, bf16[2,2,4,96,1024]{4,3,2,1,0:T(8,128)(2,1)} %get-tuple-element.82.normed_t, ...), custom_call_target="tpu_custom_call" | custom-call | tf_op jit(solution)/shard_map/tail/pallas_call | solution.py:982
  194.4 86.2 %finish.1 = (f32[256,1536]{1,0:T(8,128)}, bf16[256,1536]{1,0:T(8,128)(2,1)}, f32[6,96]{1,0:T(8,128)}, f32[96,384]{1,0:T(8,128)}, f32[96,256]{1,0:T(8,128)}, /*in...) custom-call(f32[256,1536]{1,0:T(8,128)} %get-tuple-element.87.tokens, ...), custom_call_target="tpu_custom_call" | custom-call | tf_op jit(solution)/shard_map/finish/pallas_call | solution.py:1059

commit v4 on v3

--- a/solution.py
+++ b/solution.py
@@ -18,6 +18,7 @@
 WIDE = GROUPS * COLS
 STEPS = 2 * WIDE
 PROJ = STEPS + GROUPS * 128
+MORE = PROJ - WIDE
 LOG2E = 1.4426950408889634
 EPS = 1e-05
 F32 = jnp.float32
@@ -55,6 +56,18 @@
     return sum(dot(p, ones) for p in pieces(v, n))
 
 
+def spread(v, ones):
+    hi = v.astype(BF16).astype(F32)
+    low = pltpu.roll(v - hi, 64, 1)
+    return dot(jnp.where(iota(v.shape, 1) < 64, hi, low).astype(BF16), ones)
+
+
+def folded(v, ones):
+    hi = v.astype(BF16)
+    low = (v - hi.astype(F32)).astype(BF16)
+    return dot(hi, ones) + dot(low, ones)
+
+
 def dot_right(ones, v, n):
     return sum(dot(ones, p) for p in pieces(v, n))
 
@@ -65,7 +78,7 @@
 
 def expander():
     row, col = iota((128, COLS), 0), iota((128, COLS), 1)
-    return (row == lax.shift_right_logical(col, 6)).astype(BF16)
+    return ((row & 63) == lax.shift_right_logical(col, 6)).astype(BF16)
 
 
 def reducer():
@@ -74,7 +87,7 @@
 
 
 def sigmoid(v):
-    return 1.0 / (1.0 + jnp.exp(-v))
+    return 0.5 * jnp.tanh(0.5 * v) + 0.5
 
 
 def lower(strict=False):
@@ -180,53 +193,30 @@
 HALVES = ((0, 1), (1, -1))
 
 
-class RingSum:
-    def __init__(self, net, first, held, spans, scratch):
-        self.net, self.first, self.second, self.held, self.spans = net, first, "y" if first == "x" else "x", held, spans
-        self.half, self.fold, self.whole, self.mid, self.half2, self.fold2, self.whole2 = scratch
-        self.width = sum(n for _, n in spans)
-        self.one, self.two, self.three, self.four = [], [], [], []
-        for part, step in HALVES:
-            cut = pl.ds(48 * part, 48)
+class GridSum:
+    def __init__(self, net, first, held, spans, scratch, cut=(0, 96)):
+        self.net, self.first, self.held, self.spans = net, first, held, spans
+        self.land, self.mid, self.last = scratch
+        self.rows = pl.ds(*cut)
+        self.one, self.two = [], []
+        for slot, step in enumerate((2, 1, -1)):
             if first == "x":
-                self.plan(self.one, lambda cut=cut: held.at[:, net.near("x", 2), cut, lanes(spans[0][0], 2 * self.width)], lambda part=part: self.half.at[part], "x", step)
+                self.plan(self.one, lambda step=step: held.at[:, net.near("x", step), self.rows], lambda slot=slot: self.land.at[slot], "x", step)
             else:
-                lane = 0
-                for base, n in spans:
-                    self.plan(
-                        self.one,
-                        lambda cut=cut, base=base, n=n: self.ycut(held, net.near("y", 2), base, n, cut),
-                        lambda part=part, lane=lane, n=n: self.half.at[part, :, :, lanes(lane, n)],
-                        "y",
-                        step,
-                    )
-                    lane += n
-            self.plan(self.two, lambda part=part: self.fold.at[part], lambda part=part: self.whole.at[part], first, step)
-            if first == "x":
-                self.plan(self.three, lambda cut=cut: self.mid.at[lax.rem(net.near("y", 2), 2), cut, self.ylanes(net.near("y", 2))], lambda part=part: self.half2.at[part], "y", step)
-            else:
-                self.plan(self.three, lambda cut=cut: self.mid.at[net.near("x", 2), cut], lambda part=part: self.half2.at[part], "x", step)
-            self.plan(self.four, lambda part=part: self.fold2.at[part], lambda part=part: self.whole2.at[part], self.second, step)
+                self.plan(self.two, lambda step=step: self.mid.at[net.near("x", step)], lambda slot=slot: self.last.at[slot], "x", step)
+            lane = 0
+            for base, n in spans:
+                there = lambda step=step, base=base, n=n: lanes(base + (net.near("y", step) // 2) * n, n)
+                if first == "x":
+                    src = lambda step=step, there=there: self.mid.at[lax.rem(net.near("y", step), 2), :, there()]
+                    self.plan(self.two, src, lambda slot=slot, lane=lane, n=n: self.last.at[slot, :, pl.ds(lane, n)], "y", step)
+                else:
+                    src = lambda step=step, there=there: held.at[lax.rem(net.near("y", step), 2), :, self.rows, there()]
+                    self.plan(self.one, src, lambda slot=slot, lane=lane, n=n: self.land.at[slot, :, :, pl.ds(lane, n)], "y", step)
+                lane += n
 
     def plan(self, to, src, dst, axis, step):
         to.append(self.net.plan(src, dst, axis, step))
-
-    def ycut(self, ref, owner, base, n, cut):
-        return ref.at[lax.rem(owner, 2), :, cut, lanes(base + (owner // 2) * n, n)]
-
-    def ylanes(self, owner):
-        return lanes((owner // 2) * self.width, self.width)
-
-    def block(self, owner):
-        if self.first == "x":
-            return self.held[:, owner, :, lanes(self.spans[0][0], 2 * self.width)]
-        got = [self.held[lax.rem(owner, 2), :, :, lanes(base + (owner // 2) * n, n)] for base, n in self.spans]
-        return got[0] if len(got) == 1 else jnp.concatenate(got, axis=-1)
-
-    def mid_block(self, owner):
-        if self.first == "x":
-            return self.mid[lax.rem(owner, 2), :, self.ylanes(owner)]
-        return self.mid[owner]
 
     def step1(self):
         for copy in self.one:
@@ -234,35 +224,38 @@
 
     def step2(self):
         arrive(self.one)
-        for part, step in HALVES:
-            self.fold[part] = self.block(self.net.near(self.first, step))
-            self.fold[part, :, 48 * part : 48 * part + 48, :] += self.half[part]
-            self.two[part].start()
-
-    def step3(self):
+        at = self.net.at
+        if self.first == "x":
+            self.mid[...] = self.total(self.held[:, at["x"], self.rows], self.land, slice(None)).astype(BF16)
+        else:
+            lane = 0
+            for base, n in self.spans:
+                cut = slice(lane, lane + n)
+                own = self.held[at["yl"], :, self.rows, lanes(base + at["yh"] * n, n)]
+                self.mid[:, :, cut] = self.total(own, self.land, cut).astype(BF16)
+                lane += n
+        for copy in self.two:
+            copy.start()
+
+    def total(self, own, others, cut):
+        return (own.astype(F32) + others[0, ..., cut].astype(F32)) + (others[1, ..., cut].astype(F32) + others[2, ..., cut].astype(F32))
+
+    def step3(self, out):
         arrive(self.two)
-        own = self.block(self.net.at[self.first]).astype(F32)
-        self.mid[...] = (own + self.whole[0].astype(F32) + self.whole[1].astype(F32)).astype(BF16)
-        for copy in self.three:
-            copy.start()
-
-    def step4(self):
-        arrive(self.three)
-        for part, step in HALVES:
-            self.fold2[part] = self.mid_block(self.net.near(self.second, step))
-            self.fold2[part, 48 * part : 48 * part + 48, :] += self.half2[part]
-            self.four[part].start()
-
-    def step5(self):
-        arrive(self.four)
-        own = self.mid_block(self.net.at[self.second]).astype(F32)
-        return own + self.whole2[0].astype(F32) + self.whole2[1].astype(F32)
-
-
-def ring_scratch(first, width):
+        at = self.net.at
+        if self.first == "y":
+            out[self.rows, :] = self.total(self.mid[at["x"]], self.last, slice(None))
+            return
+        lane = 0
+        for base, n in self.spans:
+            cut = slice(lane, lane + n)
+            out[self.rows, cut] = self.total(self.mid[at["yl"], :, lanes(base + at["yh"] * n, n)], self.last, cut)
+            lane += n
+
+
+def grid_scratch(first, width, count=96):
     blocks, wide = (2, 2 * width) if first == "x" else (4, width)
-    shapes = [(2, blocks, 48, wide), (2, blocks, 96, wide), (2, blocks, 96, wide), (blocks, 96, wide), (2, 48, width), (2, 96, width), (2, 96, width)]
-    return [pltpu.VMEM(s, BF16) for s in shapes]
+    return [pltpu.VMEM(s, BF16) for s in ((3, blocks, count, wide), (blocks, count, wide), (3, count, width))]
 
 
 class TokenSum:
@@ -421,8 +414,8 @@
 
 def forward_kernel(
     x, wx, wout, wbc, prm, conv_bc, bias_bc, cot,
-    gate_out, inner_out, z_out, y_out, gm_out, mixed_out, h_out, dt_out, r_out, u_out, bc_out, bcin_out, zbc_out, stats_out, normed_t, cot_t,
-    cots, gps, ext, extbc, state, stat, slots, send, recv, local,
+    inner_out, z_out, y_out, h_out, dt_out, r_out, u_out, bc_out, bcin_out, zbc_out, normed_t, gains_out, mixed_out, gs_out, gg_out, cot_t,
+    cots, gps, acts, slopes, gms, mixed, gg, turned_c, ext, extbc, state, stat, slots, send, recv, local,
 ):
     i = pl.program_id(0)
     net = Net(send, recv)
@@ -433,6 +426,7 @@
     c2 = [net.plan(lambda p=p, s=s: part(p, s), lambda p=p, s=s: part(p, s), "z", s) for p, s in HALVES]
     q = [net.plan(lambda: stat, lambda: slots.at[z], "z", step) for step in (1, -1, 2)]
     own = lambda: pltpu.make_async_copy(cot, here(), local.at[0])
+    turn_out = lambda: pltpu.make_async_copy(turned_c, cot_t, local.at[1])
 
     @pl.when(i == 0)
     def _():
@@ -471,7 +465,7 @@
         bc_out[...] = bc
         b, c = bc[:, :STATE], bc[:, STATE:]
         scores = jnp.where(iota((BLOCK, BLOCK), 0) >= iota((BLOCK, BLOCK), 1), dot_nt(c, b), 0.0)
-        tri, spread = lower(), expander()
+        tri, ones = lower(), expander()
         left = iota((BLOCK, 128), 1) < 64
         steps = dot(xb, wx[:, STEPS:])
         total = jnp.zeros((BLOCK, 128), F32)
@@ -487,17 +481,16 @@
             rt = jnp.transpose(r)
             gate = dot(xb, wx[:, cut])
             inner = dot(xb, wx[:, WIDE + g * COLS : WIDE + (g + 1) * COLS])
-            gate_out[:, cut] = gate
             inner_out[:, cut] = inner
             ext[8 : BLOCK + 8, cut] = inner
             zv = prm[g, 4:5, :] + sum(prm[g, j : j + 1, :] * ext[5 + j : 5 + j + BLOCK, cut] for j in range(4))
             z_out[:, cut] = zv
             xv = zv * sigmoid(zv)
             last = r[BLOCK - 1 : BLOCK, :]
-            w = xv * dot_left(dt, spread, 2)
-            grow = dot_left(jnp.exp2(r), spread, 2)
-            tail = dot_left(jnp.exp2(last - r), spread, 2)
-            skip = dot_left(prm[g, 8:16, 0:128], spread, 3)[0:1, :]
+            w = xv * spread(dt, ones)
+            grow = spread(jnp.exp2(r), ones)
+            tail = spread(jnp.exp2(last - r), ones)
+            skip = spread(prm[g, 8:16, 0:128], ones)[0:1, :]
             wl = w.astype(BF16)
             h = state[:, cut]
             h_out[0, g] = h
@@ -511,8 +504,13 @@
             yv = jnp.concatenate(parts, axis=1) + grow * dot(c, h.astype(BF16)) + skip * xv
             y_out[:, cut] = yv
             state[:, cut] = grow[BLOCK - 1 : BLOCK, :] * h + dot_tn(b, (tail * w).astype(BF16))
-            gp = yv * (gate * sigmoid(gate))
-            gps[pl.ds(pl.multiple_of(i * BLOCK, BLOCK), BLOCK), cut] = gp
+            sig = sigmoid(gate)
+            act = gate * sig
+            gp = yv * act
+            here_now = pl.ds(pl.multiple_of(i * BLOCK, BLOCK), BLOCK)
+            gps[here_now, cut] = gp
+            acts[here_now, cut] = act
+            slopes[here_now, cut] = yv * (sig + act * (1.0 - sig))
             sq = gp * gp
             total = total + (sq[:, 0:128] + sq[:, 128:256] + sq[:, 256:384])
         stat[pl.ds(i, 1), :] = token_row(total)
@@ -534,9 +532,9 @@
         cb = cots[at, :]
         turned = jnp.transpose(cb).reshape(2, 4, 2, 96, BLOCK)
         for core in range(2):
-            cot_t[core, :, :, :, at] = turned[:, :, core]
+            turned_c[core, :, :, :, at] = turned[:, :, core]
         gm = dot(cb, wout[...])
-        gm_out[at, :] = gm
+        gms[at, :] = gm
         gain = jnp.concatenate([prm[0, 5:6, :], prm[1, 5:6, :]], axis=1)
         stat[pl.ds(BLOCKS + block, 1), :] = token_row(gm * gain * gps[at, :])
 
@@ -547,17 +545,35 @@
         slots[z] = stat[...]
         for copy in q:
             copy.arrived()
+            copy.left()
         sums = (slots[0] + slots[1]) + (slots[2] + slots[3])
         root = lax.rsqrt(sums[0:4, :] * (1.0 / INNER) + EPS)
-        stats_out[0:4, :] = root
-        stats_out[4:8, :] = root * root * root * (sums[4:8, :] * (1.0 / INNER))
-        columns = jnp.transpose(stats_out[...])
+        stat[0:4, :] = root
+        stat[4:8, :] = root * root * root * (sums[4:8, :] * (1.0 / INNER))
+        columns = jnp.transpose(stat[...])
         gain = jnp.concatenate([prm[0, 5:6, :], prm[1, 5:6, :]], axis=1)
+        turn_out().start()
+        gain_grad = jnp.zeros((1, WIDE), F32)
+        outs = []
         for k in range(BLOCKS):
             at = slice(k * BLOCK, (k + 1) * BLOCK)
-            mixed_out[at, :] = (gps[at, :] * columns[:, k : k + 1] * gain).astype(BF16)
+            gp, gm = gps[at, :], gms[at, :]
+            normal = gp * columns[:, k : k + 1]
+            gain_grad = gain_grad + jnp.sum(gm * normal, axis=0, keepdims=True)
+            mixed[at, :] = (normal * gain).astype(BF16)
+            gated = (gm * gain) * columns[:, k : k + 1] - gp * columns[:, BLOCKS + k : BLOCKS + k + 1]
+            gms[at, :] = gated * acts[at, :]
+            gg[at, :] = (gated * slopes[at, :]).astype(BF16)
+            block = pl.ds(k * BLOCK, BLOCK)
+            for src, dst in ((mixed, mixed_out), (gms, gs_out), (gg, gg_out)):
+                outs.append(pltpu.make_async_copy(src.at[block], dst.at[block], local.at[2 + len(outs)]))
+                outs[-1].start()
+        gains_out[...] = jnp.concatenate([gain_grad, jnp.zeros((7, WIDE), F32)], axis=0)
         for copy in c1 + c2 + q:
             copy.left()
+        for copy in outs:
+            copy.wait()
+        turn_out().wait()
 
 
 def run_forward(x, wx, wout, wbc, prm, conv_bc, bias_bc, cot):
@@ -575,9 +591,6 @@
             wide,
             wide,
             wide,
-            wide,
-            wide,
-            SHAPE((LEN, WIDE), BF16),
             SHAPE((BLOCKS, GROUPS, STATE, COLS), F32),
             narrow,
             narrow,
@@ -585,8 +598,11 @@
             SHAPE((LEN, 256), BF16),
             SHAPE((LEN, 256), F32),
             SHAPE((LEN, 256), F32),
-            SHAPE((8, 256), F32),
             SHAPE((2, 2, 4, 96, LEN), BF16),
+            SHAPE((8, WIDE), F32),
+            SHAPE((LEN, WIDE), BF16),
+            wide,
+            SHAPE((LEN, WIDE), BF16),
             SHAPE((2, 2, 4, 96, LEN), BF16),
         ],
         in_specs=[
@@ -603,9 +619,6 @@
             block(WIDE),
             block(WIDE),
             block(WIDE),
-            block(WIDE),
-            keep(LEN, WIDE),
-            keep(LEN, WIDE),
             pl.BlockSpec((1, GROUPS, STATE, COLS), lambda k: (first(k), 0, 0, 0)),
             small(),
             small(),
@@ -613,13 +626,19 @@
             block(256),
             block(256),
             block(256),
-            keep(8, 256),
             pl.BlockSpec((2, 2, 4, 96, BLOCK), lambda k: (0, 0, 0, 0, first(k))),
-            keep(2, 2, 4, 96, LEN),
-        ],
+            keep(8, WIDE),
+        ]
+        + [ANY] * 4,
         scratch_shapes=[
             pltpu.VMEM((LEN, D), BF16),
             pltpu.VMEM((LEN, WIDE), F32),
+            pltpu.VMEM((LEN, WIDE), F32),
+            pltpu.VMEM((LEN, WIDE), F32),
+            pltpu.VMEM((LEN, WIDE), F32),
+            pltpu.VMEM((LEN, WIDE), BF16),
+            pltpu.VMEM((LEN, WIDE), BF16),
+            pltpu.VMEM((2, 2, 4, 96, LEN), BF16),
             pltpu.VMEM((BLOCK + 8, WIDE), F32),
             pltpu.VMEM((BLOCK + 8, 256), F32),
             pltpu.VMEM((STATE, WIDE), F32),
@@ -627,44 +646,51 @@
             pltpu.VMEM((4, 8, BLOCK), F32),
         ]
         + sems(7)
-        + [pltpu.SemaphoreType.DMA((1,))],
+        + [pltpu.SemaphoreType.DMA((14,))],
         compiler_params=pltpu.CompilerParams(collective_id=1, has_side_effects=True, vmem_limit_bytes=ROOM),
         name="forward",
     )(x, wx, wout, wbc, prm, conv_bc, bias_bc, cot)
 
 
 def backward_kernel(
-    gm, gate, inner, zin, y, hin, prm, bc, dt, r, u, stats, mixed, wout, cot_t, tokens,
-    cat_out, dbc_out, acc, branch_out, wout_out,
-    ext, dstate, dst, dbc, held, got, away, mv, wv, cv, ownb, g0, g1, g2, g3, s1, s2, s3, s4, s5, s6, s7, send, recv, local,
+    gs_in, inner, zin, y, hin, prm, bc, dt, r, u, gains, mixed, wout, cot_t, gg, normed_t, tokens,
+    cat_out, dbc_out, acc, branch_out, wout_out, wgate_out,
+    ext, dstate, dst, dbc, held, got, away, mv, wv, cv, gv, nv, ownb, g0, g1, g2, g3, s1, s2, s3, t1, t2, t3, send, recv, local,
 ):
     k = pl.program_id(0)
     net = Net(send, recv)
     cc, z = net.at["c"], net.at["z"]
-    cross = net.plan(lambda: away, lambda: got, "c")
+    cross = [net.plan(lambda n=n: away.at[n], lambda n=n: got.at[n], "c") for n in range(2)]
     token = TokenSum(net, (g0, g1, g2, g3))
-    ring = RingSum(net, "y", held, ((0, COLS),), (s1, s2, s3, s4, s5, s6, s7))
+    rings = (GridSum(net, "y", held.at[0], ((0, COLS),), (s1, s2, s3)), GridSum(net, "x", held.at[1], ((0, COLS),), (t1, t2, t3)))
 
     @pl.when(k == 0)
     def _():
-        net.barrier([("z", 1), ("z", -1), ("x", 1), ("x", -1), ("y", 1), ("y", -1), ("c", 1)])
-        loads = [pltpu.make_async_copy(src, dst, local.at[n]) for n, (src, dst) in enumerate(((mixed, mv), (wout, wv), (cot_t, cv)))]
+        loads = [pltpu.make_async_copy(src, dst, local.at[n]) for n, (src, dst) in enumerate(((mixed, mv), (wout, wv), (cot_t, cv), (gg, gv), (normed_t, nv)))]
         for copy in loads:
             copy.start()
+        net.barrier([("z", 1), ("z", -1)] + [(a, s) for a in ("x", "y") for s in (1, -1, 2)] + [("c", 1)])
         loads[0].wait()
         loads[1].wait()
         branch = lambda place: dot_nt(mv[pl.ds(pl.multiple_of(place * 256, 256), 256), :], wv[...])
-        grads = lambda core: dot(cv[core].reshape(8 * 96, LEN), mv[...]).astype(BF16).reshape(2, 4, 96, WIDE)
+        grads = lambda left, right, core: dot(left[core].reshape(8 * 96, LEN), right[...]).astype(BF16).reshape(2, 4, 96, WIDE)
         g0[...] = branch(net.near("z", 2)).astype(BF16)
         token.step1()
         loads[2].wait()
-        away[...] = grads(net.other)
-        cross.start()
+        away[0] = grads(cv, mv, net.other)
+        cross[0].start()
+        loads[3].wait()
+        loads[4].wait()
+        away[1] = grads(nv, gv, net.other)
+        cross[1].start()
         g2[0] = branch(net.near("z", 1)).astype(BF16)
         g2[1] = branch(net.near("z", -1)).astype(BF16)
         ownb[...] = branch(z)
-        held[...] = grads(cc)
+        held[0] = grads(cv, mv, cc)
+        held[1] = grads(nv, gv, cc)
         acc[...] = jnp.zeros_like(acc)
+        for g in range(GROUPS):
+            acc[g, 5:6, :] = gains[0:1, g * COLS : (g + 1) * COLS]
         ext[BLOCK : BLOCK + 8, :] = jnp.zeros((8, WIDE), F32)
         dstate[...] = jnp.zeros_like(dstate)
 
@@ -675,10 +701,7 @@
     b, c = bc[:, :STATE], bc[:, STATE:]
     valid = iota((BLOCK, BLOCK), 1) >= iota((BLOCK, BLOCK), 0)
     scores = jnp.where(valid, dot_nt(b, c), 0.0)
-    both = jnp.concatenate([stats[pl.ds(BLOCKS - 1 - k, 1), :], stats[pl.ds(2 * BLOCKS - 1 - k, 1), :], jnp.zeros((6, BLOCK), F32)], axis=0)
-    column = jnp.transpose(both)
-    ir, cr = column[:, 0:1], column[:, 1:2]
-    spread, fold = expander(), reducer()
+    ones, fold = expander(), reducer()
     left = iota((BLOCK, 128), 1) < 64
     suffix, prefix = upper(), lower(strict=True)
     dst[...] = jnp.zeros_like(dst)
@@ -688,40 +711,25 @@
 
             @pl.when(k == 1)
             def _():
-                cross.arrived()
-                held[...] += got[...]
-                ring.step1()
+                token.step2()
 
             @pl.when(k == 3)
             def _():
-                ring.step4()
+                for ring in rings:
+                    ring.step2()
 
         else:
 
             @pl.when(k == 0)
             def _():
-                token.step2()
-
-            @pl.when(k == 1)
-            def _():
-                ring.step2()
-
-            @pl.when(k == 2)
-            def _():
-                ring.step3()
+                for n in range(2):
+                    cross[n].arrived()
+                    held[n] += got[n]
+                    rings[n].step1()
 
         cut = slice(g * COLS, (g + 1) * COLS)
         yv = y[:, cut]
-        gv = gate[:, cut]
-        sig = sigmoid(gv)
-        act = gv * sig
-        gain = prm[g, 5:6, :]
-        gp = yv * act
-        gmix = gm[:, cut]
-        gain_grad = gmix * gp * ir
-        gated = ir * (gmix * gain) - gp * cr
-        gs = gated * act
-        cat_out[:, cut] = (gated * yv * sig * (1.0 + gv * (1.0 - sig))).astype(BF16)
+        gs = gs_in[:, cut]
         xi = inner[:, cut]
         zv = zin[:, cut]
         zs = sigmoid(zv)
@@ -729,10 +737,10 @@
         rv = r[g]
         rt = jnp.transpose(rv)
         last = rv[BLOCK - 1 : BLOCK, :]
-        dte = dot_left(dt[g], spread, 2)
-        grow = dot_left(jnp.exp2(rv), spread, 2)
-        tail = dot_left(jnp.exp2(last - rv), spread, 2)
-        skip = dot_left(prm[g, 8:16, 0:128], spread, 3)[0:1, :]
+        dte = spread(dt[g], ones)
+        grow = spread(jnp.exp2(rv), ones)
+        tail = spread(jnp.exp2(last - rv), ones)
+        skip = spread(prm[g, 8:16, 0:128], ones)[0:1, :]
         w = xv * dte
         wl = w.astype(BF16)
         gl = gs.astype(BF16)
@@ -745,23 +753,28 @@
             pair = slice(128 * p, 128 * (p + 1))
             wp, gpair = wl[:, pair], gl[:, pair]
             zero = jnp.zeros_like(wp)
+            w_low = pltpu.roll(w[:, pair] - wp.astype(F32), 64, 1).astype(BF16)
+            g_low = (gs[:, pair] - gpair.astype(F32)).astype(BF16)
+            g_turn = pltpu.roll(gpair.astype(F32), 64, 1).astype(BF16)
             for n in (2 * p, 2 * p + 1):
                 decay = jnp.exp2(jnp.minimum(rt[n : n + 1, :] - rv[:, n : n + 1], 0.0))
                 halves.append(dot((scores * decay).astype(BF16), gpair))
-                mine = jnp.where(left, wp, zero) if n % 2 == 0 else jnp.where(left, zero, wp)
-                dst[...] += dot_nt(mine, gpair) * decay
+                pick = (lambda a, b: jnp.where(left, a, b)) if n % 2 == 0 else (lambda a, b: jnp.where(left, b, a))
+                one = jnp.concatenate([pick(wp, w_low), pick(wp, zero)], axis=1)
+                two = jnp.concatenate([pick(gpair, g_turn), g_low], axis=1)
+                dst[...] += dot_nt(one, two) * decay
             parts.append(jnp.where(left, halves[0], halves[1]))
         dwi = jnp.concatenate(parts, axis=1)
         dws = tail * dot(b, dhl)
         dw = dwi + dws
         skipgrad = gs * xv
-        diff = dot_left(gl.astype(F32) * (yv - skip * xv) - wl.astype(F32) * dwi, fold, 3)
-        zsum = dot_left(w * dws, fold, 3)
-        const = dot_left(jnp.sum(h * dh, axis=0, keepdims=True) * grow[BLOCK - 1 : BLOCK, :] + jnp.zeros((8, COLS), F32), fold, 3)
+        diff = folded(gl.astype(F32) * (yv - skip * xv) - wl.astype(F32) * dwi, fold)
+        zsum = folded(w * dws, fold)
+        const = folded(jnp.sum(h * dh, axis=0, keepdims=True) * grow[BLOCK - 1 : BLOCK, :] + jnp.zeros((8, COLS), F32), fold)
         da = dot_right(suffix, diff, 3) + dot_right(prefix, zsum, 3) + const[0:1, :]
         rate = -jnp.exp(prm[g, 7:8, 0:128])
-        dstep = (dot_left(xv * dw, fold, 3) + rate * da) * sigmoid(u[g])
-        cat_out[:, STEPS + 128 * g : STEPS + 128 * (g + 1)] = dstep.astype(BF16)
+        dstep = (folded(xv * dw, fold) + rate * da) * sigmoid(u[g])
+        cat_out[:, WIDE + 128 * g : WIDE + 128 * (g + 1)] = dstep.astype(BF16)
         gx = (grow * gs).astype(BF16)
         dbc[:, STATE:] += dot_nt(gx, h.astype(BF16))
         dbc[:, :STATE] += dot_nt((tail * w).astype(BF16), dhl)
@@ -774,40 +787,43 @@
             moved = ext[3 - j : 3 - j + BLOCK, cut]
             gi = gi + prm[g, j : j + 1, :] * moved
             acc[g, j : j + 1, :] += jnp.sum(xi * moved, axis=0, keepdims=True)
-        cat_out[:, WIDE + g * COLS : WIDE + (g + 1) * COLS] = gi.astype(BF16)
+        cat_out[:, cut] = gi.astype(BF16)
         acc[g, 4:5, :] += jnp.sum(dz, axis=0, keepdims=True)
-        acc[g, 5:6, :] += jnp.sum(gain_grad, axis=0, keepdims=True)
         acc[g, 6:7, 0:128] += jnp.sum(dstep, axis=0, keepdims=True)
         acc[g, 7:8, 0:128] += jnp.sum(da * dt[g], axis=0, keepdims=True) * rate
-        acc[g, 8:9, 0:128] += dot_left(jnp.sum(skipgrad, axis=0, keepdims=True) + jnp.zeros((8, COLS), F32), fold, 3)[0:1, :]
+        acc[g, 8:9, 0:128] += folded(jnp.sum(skipgrad, axis=0, keepdims=True) + jnp.zeros((8, COLS), F32), fold)[0:1, :]
     ds = jnp.where(valid, dst[...], 0.0).astype(BF16)
     dbc_out[:, STATE:] = (dbc[:, STATE:] + dot_tn(ds, b)).astype(BF16)
     dbc_out[:, :STATE] = (dbc[:, :STATE] + dot(ds, c)).astype(BF16)
 
     @pl.when(k == BLOCKS - 1)
     def _():
-        wout_out[...] = ring.step5()
+        rings[0].step3(wout_out)
+        rings[1].step3(wgate_out)
         branch_out[...] = (tokens[...].astype(F32) + (ownb[...] + token.step3())).astype(BF16)
         for copy in net.copies:
             copy.left()
 
 
-def run_backward(gm, gate, inner, zin, y, hin, prm, bc, dt, r, u, stats, mixed, wout, cot_t, tokens):
+def run_backward(*args):
     rev = lambda k: BLOCKS - 1 - k
     cols = lambda n: pl.BlockSpec((BLOCK, n), lambda k: (rev(k), 0))
     small = lambda: pl.BlockSpec((GROUPS, BLOCK, 128), lambda k: (0, rev(k), 0))
     keep = lambda *s: pl.BlockSpec(s, lambda k: (0,) * len(s))
+    bf = lambda *s: pltpu.VMEM(s, BF16)
+    f32 = lambda *s: pltpu.VMEM(s, F32)
     return pl.pallas_call(
         backward_kernel,
         grid=(BLOCKS,),
         out_shape=[
-            SHAPE((LEN, PROJ), BF16),
+            SHAPE((LEN, MORE), BF16),
             SHAPE((LEN, 256), BF16),
             SHAPE((GROUPS, 16, COLS), F32),
             SHAPE((256, D), BF16),
             SHAPE((96, COLS), F32),
+            SHAPE((96, COLS), F32),
         ],
-        in_specs=[cols(WIDE)] * 5
+        in_specs=[cols(WIDE)] * 4
         + [
             pl.BlockSpec((1, GROUPS, STATE, COLS), lambda k: (rev(k), 0, 0, 0)),
             keep(GROUPS, 16, COLS),
@@ -815,45 +831,47 @@
             small(),
             small(),
             small(),
-            keep(8, 256),
-            ANY,
-            ANY,
-            ANY,
-            keep(256, D),
-        ],
-        out_specs=[cols(PROJ), cols(256), keep(GROUPS, 16, COLS), keep(256, D), keep(96, COLS)],
+            keep(8, WIDE),
+        ]
+        + [ANY] * 5
+        + [keep(256, D)],
+        out_specs=[cols(MORE), cols(256), keep(GROUPS, 16, COLS), keep(256, D), keep(96, COLS), keep(96, COLS)],
         scratch_shapes=[
-            pltpu.VMEM((BLOCK + 8, WIDE), F32),
-            pltpu.VMEM((STATE, WIDE), F32),
-            pltpu.VMEM((BLOCK, BLOCK), F32),
-            pltpu.VMEM((BLOCK, 256), F32),
-            pltpu.VMEM((2, 4, 96, WIDE), BF16),
-            pltpu.VMEM((2, 4, 96, WIDE), BF16),
-            pltpu.VMEM((2, 4, 96, WIDE), BF16),
-            pltpu.VMEM((LEN, WIDE), BF16),
-            pltpu.VMEM((D, WIDE), BF16),
-            pltpu.VMEM((2, 2, 4, 96, LEN), BF16),
-            pltpu.VMEM((256, D), F32),
+            f32(BLOCK + 8, WIDE),
+            f32(STATE, WIDE),
+            f32(BLOCK, BLOCK),
+            f32(BLOCK, 256),
+            bf(2, 2, 4, 96, WIDE),
+            bf(2, 2, 4, 96, WIDE),
+            bf(2, 2, 4, 96, WIDE),
+            bf(LEN, WIDE),
+            bf(D, WIDE),
+            bf(2, 2, 4, 96, LEN),
+            bf(LEN, WIDE),
+            bf(2, 2, 4, 96, LEN),
+            f32(256, D),
         ]
         + token_scratch()
-        + ring_scratch("y", COLS)
-        + sems(13)
-        + [pltpu.SemaphoreType.DMA((3,))],
+        + grid_scratch("y", COLS)
+        + grid_scratch("x", COLS)
+        + sems(24)
+        + [pltpu.SemaphoreType.DMA((5,))],
         compiler_params=pltpu.CompilerParams(collective_id=2, has_side_effects=True, vmem_limit_bytes=ROOM),
         name="backward",
-    )(gm, gate, inner, zin, y, hin, prm, bc, dt, r, u, stats, mixed, wout, cot_t, tokens)
+    )(*args)
 
 
 def tail_kernel(
-    cat, wx, normed_t, normed, dbc, zbc, bc_in, acc, wbc, tokens, cot, gain, conv,
-    tokens_out, gate_out, inner_out, bc_out, small_out,
-    catv, wxv, ntv, nv, mine, slots, zv, xi, wv, xv, ov, ext, gnbc, ownb, held, got, away, dbw, heldb, gotb, small, sp0, sp1, sp2, sp3, bz, by,
-    g0, g1, g2, g3, a1, a2, a3, a4, a5, a6, a7, b1, b2, b3, b4, b5, b6, b7, c1, c2, c3, c4, c5, c6, c7, send, recv, local,
+    gg, cat, wx, normed_t, normed, dbc, zbc, bc_in, acc, wbc, tokens, cot, gain, conv,
+    tokens_out, inner_out, bc_out, small_out,
+    ggv, catv, wxv, ntv, nv, mine, slots, zv, xi, wv, xv, ov, ext, gnbc, ownb, held, got, away, dbw, heldb, gotb, small, sp0, sp1, sp2, sp3, bz, by,
+    g0, g1, g2, g3, a1, a2, a3, b1, b2, b3, c1, c2, c3, send, recv, local,
 ):
     net = Net(send, recv)
     at = net.at
     yh, cx, cc, z, y = at["yh"], at["x"], at["c"], at["z"], at["y"]
     pairs = (
+        (gg, ggv),
         (cat, catv),
         (wx, wxv),
         (normed, nv),
@@ -869,9 +887,9 @@
     for copy in loads:
         copy.start()
     token = TokenSum(net, (g0, g1, g2, g3))
-    ring_gate = RingSum(net, "x", held, ((0, COLS),), (a1, a2, a3, a4, a5, a6, a7))
-    ring_inner = RingSum(net, "y", held, ((WIDE, COLS), (STEPS, 128)), (b1, b2, b3, b4, b5, b6, b7))
-    ring_bc = RingSum(net, "x", heldb, ((0, 128),), (c1, c2, c3, c4, c5, c6, c7))
+    spans = ((0, COLS), (WIDE, 128))
+    rings = (GridSum(net, "x", held, spans, (a1, a2, a3), (0, 48)), GridSum(net, "y", held, spans, (b1, b2, b3), (48, 48)))
+    ring_bc = GridSum(net, "x", heldb, ((0, 128),), (c1, c2, c3))
     mine[0:LEN, :] = dbc[...]
     mine[LEN : LEN + 16, :] = jnp.zeros((16, 256), BF16)
     slots[z] = mine[pl.ds(pl.multiple_of(z * 256, 16), 272), :]
@@ -882,20 +900,20 @@
 
     def block(place):
         cut = pl.ds(pl.multiple_of(place * 256, 256), 256)
-        got = dot_nt(catv[cut, :], wxv[...])
+        got = dot_nt(ggv[cut, :], wxv[:, 0:WIDE]) + dot_nt(catv[cut, :], wxv[:, WIDE:])
         return got, jnp.sum(got * nv[cut, :].astype(F32), axis=0, keepdims=True)
 
-    for copy in loads[:3]:
+    for copy in loads[:4]:
         copy.wait()
     out, part = block(net.near("z", 2))
     norm_part = norm_part + part
     g0[...] = out.astype(BF16)
     token.step1()
-    grads = lambda core: dot(ntv[core].reshape(8 * 96, LEN), catv[...]).astype(BF16).reshape(2, 4, 96, PROJ)
-    loads[3].wait()
+    grads = lambda core: dot(ntv[core].reshape(8 * 96, LEN), catv[...]).astype(BF16).reshape(2, 4, 96, MORE)
+    loads[4].wait()
     away[...] = grads(net.other)
     cross = net.start(away, got, "c")
-    for copy in loads[4:]:
+    for copy in loads[5:]:
         copy.wait()
     arrive(swap)
     total = (slots[0].astype(F32) + slots[1].astype(F32)) + (slots[2].astype(F32) + slots[3].astype(F32))
@@ -918,61 +936,57 @@
     crossb = net.start(dbw.at[net.other], gotb, "c")
     gnbc[...] = dot_nt(gbc, wv[...])
     norm_part = norm_part + jnp.sum(gnbc[...] * nv[own, :].astype(F32), axis=0, keepdims=True)
+    held[...] = grads(cc)
+    cross.arrived()
+    held[...] += got[...]
+    for ring in rings:
+        ring.step1()
+    crossb.arrived()
+    heldb[...] = dbw[cc] + gotb[...]
+    ring_bc.step1()
     for p, step in HALVES:
         out, part = block(net.near("z", step))
         norm_part = norm_part + part
         g2[p] = out.astype(BF16)
     token.step2()
-    held[...] = grads(cc)
-    cross.arrived()
-    held[...] += got[...]
-    ring_inner.step1()
-    ring_gate.step1()
-    crossb.arrived()
-    heldb[...] = dbw[cc] + gotb[...]
-    ring_bc.step1()
     out, part = block(z)
     norm_part = (norm_part + part) / gain_row
     ownb[...] = out + gnbc[...]
     for k in range(4):
         small[32 + k : 33 + k, :] = norm_part[:, k * COLS : (k + 1) * COLS]
-    sp0[z] = small[32:48, :]
-    q = net.around(sp0.at[z], sp0.at[z], "z")
-    ring_gate.step2()
-    ring_inner.step2()
+    sp1[cx] = small[...]
+    q = net.around(sp1.at[cx], sp1.at[cx], "x")
     ring_bc.step2()
-    arrive(q)
-    sp1[cx, 0:32, :] = small[0:32, :]
-    sp1[cx, 32:48, :] = (sp0[0] + sp0[1]) + (sp0[2] + sp0[3])
-    q = net.around(sp1.at[cx], sp1.at[cx], "x")
-    ring_bc.step3()
+    v = xv[...].astype(F32)
+    root = lax.rsqrt(jnp.mean(v * v, axis=1, keepdims=True) + EPS)
     arrive(q)
     sp2[y] = (sp1[0] + sp1[1]) + (sp1[2] + sp1[3])
     q = net.around(sp2.at[y], sp2.at[y], "y")
-    ring_bc.step4()
+    ring_bc.step3(by.at[yh])
+    qb = [net.start(by.at[yh], by.at[yh], "y", 2)]
+    for ring in rings:
+        ring.step2()
     arrive(q)
     sp3[cc] = (sp2[0] + sp2[1]) + (sp2[2] + sp2[3])
     q = [net.start(sp3.at[cc], sp3.at[cc], "c")]
-    bz[z] = ring_bc.step5()
-    q += net.around(bz.at[z], bz.at[z], "z")
-    ring_gate.step3()
-    ring_inner.step3()
+    arrive(qb)
+    bz[z, :, 0:128] = by[0]
+    bz[z, :, 128:256] = by[1]
+    qb = net.around(bz.at[z], bz.at[z], "z")
     arrive(q)
-    small_out[...] = sp3[0] + sp3[1]
-    by[yh] = (bz[0] + bz[1]) + (bz[2] + bz[3])
-    q = [net.start(by.at[yh], by.at[yh], "y", 2)]
-    ring_gate.step4()
-    ring_inner.step4()
-    arrive(q)
-    bc_out[:, :128] = by[0]
-    bc_out[:, 128:] = by[1]
-    gate_out[...] = ring_gate.step5()
-    inner_out[...] = ring_inner.step5()
-    v = xv[...].astype(F32)
-    root = lax.rsqrt(jnp.mean(v * v, axis=1, keepdims=True) + EPS)
+    small[...] = sp3[0] + sp3[1]
+    sp0[z] = small[32:48, :]
+    q = net.around(sp0.at[z], sp0.at[z], "z")
+    small_out[0:32, :] = small[0:32, :]
+    for ring in rings:
+        ring.step3(inner_out)
     g = token.step3() + ownb[...]
     scaled = g * gain_row
     tokens_out[...] = ov[...].astype(F32) + root * scaled - v * (root * root * root) * jnp.mean(scaled * v, axis=1, keepdims=True)
+    arrive(qb)
+    bc_out[...] = (bz[0] + bz[1]) + (bz[2] + bz[3])
+    arrive(q)
+    small_out[32:48, :] = (sp0[0] + sp0[1]) + (sp0[2] + sp0[3])
     net.finish()
 
 
@@ -983,15 +997,15 @@
         tail_kernel,
         out_shape=[
             SHAPE((256, D), F32),
-            SHAPE((96, COLS), F32),
             SHAPE((96, COLS + 128), F32),
             SHAPE((96, 256), F32),
             SHAPE((48, COLS), F32),
         ],
-        in_specs=[ANY] * 4 + [VMEM, ANY, ANY, VMEM, ANY, ANY, ANY, VMEM, VMEM],
-        out_specs=[VMEM] * 5,
+        in_specs=[ANY] * 5 + [VMEM, ANY, ANY, VMEM, ANY, ANY, ANY, VMEM, VMEM],
+        out_specs=[VMEM] * 4,
         scratch_shapes=[
-            bf(LEN, PROJ),
+            bf(LEN, WIDE),
+            bf(LEN, MORE),
             bf(D, PROJ),
             bf(2, 2, 4, 96, LEN),
             bf(LEN, D),
@@ -1005,9 +1019,9 @@
             f32(272, 256),
             f32(256, D),
             f32(256, D),
-            bf(2, 4, 96, PROJ),
-            bf(2, 4, 96, PROJ),
-            bf(2, 4, 96, PROJ),
+            bf(2, 4, 96, MORE),
+            bf(2, 4, 96, MORE),
+            bf(2, 4, 96, MORE),
             bf(2, 2, 4, 96, 256),
             bf(2, 4, 96, 256),
             bf(2, 4, 96, 256),
@@ -1016,72 +1030,88 @@
             f32(4, 48, COLS),
             f32(4, 48, COLS),
             f32(2, 48, COLS),
-            f32(4, 96, 128),
+            f32(4, 96, 256),
             f32(2, 96, 128),
         ]
         + token_scratch()
-        + ring_scratch("x", COLS)
-        + ring_scratch("y", COLS + 128)
-        + ring_scratch("x", 128)
+        + grid_scratch("x", COLS + 128, 48)
+        + grid_scratch("y", COLS + 128, 48)
+        + grid_scratch("x", 128)
         + sems(64)
-        + [pltpu.SemaphoreType.DMA((10,))],
+        + [pltpu.SemaphoreType.DMA((11,))],
         compiler_params=pltpu.CompilerParams(collective_id=3, has_side_effects=True, vmem_limit_bytes=ROOM),
         name="tail",
     )(*args)
 
 
-def finish_kernel(tokens, branch, inner, bc, small, gate, wout, tokens_out, branch_out, step_out, inner_out, bc_out, gate_out, wout_out, norm, conv, bias, conv_bc, bias_bc, step_bias, decay, skip, gain, sem):
-    big = [
-        pltpu.make_async_copy(src, dst, sem.at[i])
-        for i, (src, dst) in enumerate(
-            ((tokens, tokens_out), (branch, branch_out), (inner.at[:, pl.ds(0, COLS)], inner_out), (bc, bc_out), (gate, gate_out), (wout, wout_out))
-        )
-    ]
-    for copy in big:
+def finish_kernel(tokens, branch, inner, bc, small, gate, wout, tokens_out, branch_out, inner_out, bc_out, gate_out, wout_out, step_out, norm, conv, bias, conv_bc, bias_bc, step_bias, decay, skip, gain, tv, rv, iv, cv, gv, wv, sem):
+    trips = (
+        (tokens, tv, tokens_out),
+        (branch, rv, branch_out),
+        (inner.at[:, pl.ds(0, COLS)], iv, inner_out),
+        (bc, cv, bc_out),
+        (gate, gv, gate_out),
+        (wout, wv, wout_out),
+    )
+    reads = [pltpu.make_async_copy(src, via, sem.at[i]) for i, (src, via, dst) in enumerate(trips)]
+    copies = [pltpu.make_async_copy(via, dst, sem.at[len(trips) + i]) for i, (src, via, dst) in enumerate(trips)]
+    for copy in reads:
+        copy.start()
+    for read, copy in zip(reads, copies):
+        read.wait()
         copy.start()
     step_out[...] = jnp.transpose(jnp.concatenate([inner[:, COLS:], jnp.zeros((32, 128), F32)], axis=0))[0:HEADS, 0:96]
-    norm[...] = jnp.concatenate([small[32 + k : 33 + k, :] for k in range(4)], axis=1).reshape(D)
+    for k in range(4):
+        norm[:, k * COLS : (k + 1) * COLS] = small[32 + k : 33 + k, :]
     conv_bc[...] = small[36:40, 0:256]
-    bias_bc[...] = small[40:41, 0:256].reshape(256)
+    bias_bc[...] = small[40:41, 0:256]
     mine = small[pl.ds(pl.multiple_of(lax.axis_index("yh") * 16, 8), 16), :]
     conv[...] = mine[0:4, :]
-    bias[...] = mine[4:5, :].reshape(COLS)
-    gain[...] = mine[5:6, :].reshape(COLS)
-    step_bias[...] = mine[6:7, 0:HEADS].reshape(HEADS)
-    decay[...] = mine[7:8, 0:HEADS].reshape(HEADS)
-    skip[...] = mine[8:9, 0:HEADS].reshape(HEADS)
-    for copy in big:
+    bias[...] = mine[4:5, :]
+    gain[...] = mine[5:6, :]
+    step_bias[...] = mine[6:7, 0:HEADS]
+    decay[...] = mine[7:8, 0:HEADS]
+    skip[...] = mine[8:9, 0:HEADS]
+    for copy in copies:
         copy.wait()
 
 
-def run_finish(tokens, branch, inner, bc, small, gate, wout):
+def run_finish(*args):
     f32 = lambda *s: SHAPE(s, F32)
     return pl.pallas_call(
         finish_kernel,
         out_shape=[
             f32(256, D),
             SHAPE((256, D), BF16),
-            f32(HEADS, 96),
             f32(96, COLS),
             f32(96, 256),
             f32(96, COLS),
             f32(96, COLS),
-            f32(D),
+            f32(HEADS, 96),
+            f32(1, D),
             f32(4, COLS),
-            f32(COLS),
+            f32(1, COLS),
             f32(4, 256),
-            f32(256),
-            f32(HEADS),
-            f32(HEADS),
-            f32(HEADS),
-            f32(COLS),
+            f32(1, 256),
+            f32(1, HEADS),
+            f32(1, HEADS),
+            f32(1, HEADS),
+            f32(1, COLS),
         ],
         in_specs=[ANY, ANY, VMEM, ANY, VMEM, ANY, ANY],
-        out_specs=[ANY, ANY, VMEM] + [ANY] * 4 + [VMEM] * 9,
-        scratch_shapes=[pltpu.SemaphoreType.DMA((6,))],
+        out_specs=[ANY] * 6 + [VMEM] * 10,
+        scratch_shapes=[
+            pltpu.VMEM((256, D), F32),
+            pltpu.VMEM((256, D), BF16),
+            pltpu.VMEM((96, COLS), F32),
+            pltpu.VMEM((96, 256), F32),
+            pltpu.VMEM((96, COLS), F32),
+            pltpu.VMEM((96, COLS), F32),
+            pltpu.SemaphoreType.DMA((12,)),
+        ],
         compiler_params=pltpu.CompilerParams(vmem_limit_bytes=ROOM),
         name="finish",
-    )(tokens, branch, inner, bc, small, gate, wout)
+    )(*args)
 
 
 def shards(tokens, norm_gain, w_gate, w_inner, w_bc, w_step, conv_inner, bias_inner, conv_bc, bias_bc, step_bias, decay_log, skip_gain, gate_gain, w_out, cotangent):
@@ -1089,20 +1119,23 @@
         tokens, norm_gain, w_gate, w_inner, w_out, w_bc, w_step.T, conv_inner, bias_inner, gate_gain, step_bias, decay_log, skip_gain
     )
     wx, wout, wbc = wx.reshape(D, PROJ), wout.reshape(D, WIDE), wbc.reshape(D, 256)
-    gate, inner, zin, y, gm, mixed, hin, dt, r, u, bc, bc_in, zbc, stats, normed_t, cot_t = run_forward(
+    inner, zin, y, hin, dt, r, u, bc, bc_in, zbc, normed_t, gains, mixed, gs, gg, cot_t = run_forward(
         normed, wx, wout, wbc, prm, conv_bc, bias_bc.reshape(1, 256), cotangent
     )
-    cat, dbc, acc, output, wout_grad = run_backward(gm, gate, inner, zin, y, hin, prm, bc, dt, r, u, stats, mixed, wout, cot_t, tokens)
-    tokens_grad, gate_grad, inner_grad, bc_grad, small = run_tail(
-        cat, wx, normed_t, normed, dbc, zbc, bc_in, acc, wbc, tokens, cotangent, norm_gain, conv_bc
+    cat, dbc, acc, output, wout_grad, gate_grad = run_backward(
+        gs, inner, zin, y, hin, prm, bc, dt, r, u, gains, mixed, wout, cot_t, gg, normed_t, tokens
+    )
+    tokens_grad, inner_grad, bc_grad, small = run_tail(
+        gg, cat, wx, normed_t, normed, dbc, zbc, bc_in, acc, wbc, tokens, cotangent, norm_gain, conv_bc
     )
     (
-        tokens_grad, output, step_grad, inner_grad, bc_grad, gate_grad, wout_grad,
+        tokens_grad, output, inner_grad, bc_grad, gate_grad, wout_grad, step_grad,
         norm, conv, bias, conv_bc_grad, bias_bc_grad, step_bias_grad, decay, skip, gate_gain_grad,
     ) = run_finish(tokens_grad, output, inner_grad, bc_grad, small, gate_grad, wout_grad)
+    flat = lambda v: v.reshape(-1)
     return (
-        output, tokens_grad, norm, gate_grad, inner_grad, bc_grad, step_grad.T, conv, bias, conv_bc_grad,
-        bias_bc_grad, step_bias_grad, decay, skip, gate_gain_grad, wout_grad,
+        output, tokens_grad, flat(norm), gate_grad, inner_grad, bc_grad, step_grad.T, conv, flat(bias), conv_bc_grad,
+        flat(bias_bc_grad), flat(step_bias_grad), flat(decay), flat(skip), flat(gate_gain_grad), wout_grad,
     )
 
 

time: 281 us -> 185 us (0.66)
  Pallas kernels: 280 us -> 180 us
  other arithmetic: 0 us -> 3.86 us
    pallas_call x1, Pallas kernels: 86.2 us -> 4.7 us  [run_finish(): pl.pallas_call(finish_kernel, out_shape=[f32(256, D), SHAPE((256, D), BF1...]
    pallas_call x1, Pallas kernels: 61.4 us -> 46.5 us  [run_tail(): pl.pallas_call(tail_kernel, out_shape=[SHAPE((256, D), F32), SHAPE((96, C...]
    pallas_call x1, Pallas kernels: 46.8 us -> 42.4 us  [run_backward(): pl.pallas_call(backward_kernel, grid=(BLOCKS,), out_shape=[SHAPE((LEN, MO...]
    pallas_call x0 -> x3, other arithmetic: none -> 3.86 us  [run_finish(): pl.pallas_call(finish_kernel, out_shape=[f32(256, D), SHAPE((256, D), BF1...]
where the time goes in v4:
time: 185 us; the launch traced here: 184 us
  Pallas kernels  180 us (97%)
  other arithmetic  3.86 us (2%)
    pallas_call x1, Pallas kernels, run_tail(): pl.pallas_call(tail_kernel, out_shape=[SHAPE((256, D), F32), SHAPE((96, C...  46.5 us
    pallas_call x1, Pallas kernels, run_gather(): pl.pallas_call(gather_kernel, out_shape=[SHAPE((LEN, D), BF16), SHAPE((2,...  43.6 us
    pallas_call x1, Pallas kernels, run_forward(): pl.pallas_call(forward_kernel, grid=(2 * BLOCKS,), out_shape=[wide, wide,...  42.8 us
    pallas_call x1, Pallas kernels, run_backward(): pl.pallas_call(backward_kernel, grid=(BLOCKS,), out_shape=[SHAPE((LEN, MO...  42.4 us
    pallas_call x1, Pallas kernels, run_finish(): pl.pallas_call(finish_kernel, out_shape=[f32(256, D), SHAPE((256, D), BF1...  4.7 us
    pallas_call x3, other arithmetic, run_finish(): pl.pallas_call(finish_kernel, out_shape=[f32(256, D), SHAPE((256, D), BF1...  3.86 us

profile of v4, /device:TPU:0, one launch (start us, length us, event | category | flops | bytes accessed | tf_op | source)
XLA Modules:
  0.0 184.5 jit_solution(6832016210868761651)
XLA Ops:
  0.7 43.6 %gather_all.1 = (bf16[1024,1536]{1,0:T(8,128)(2,1)}, bf16[2,4,2,96,1792]{4,3,2,1,0:T(8,128)(2,1)}, bf16[2,4,2,96,768]{4,3,2,1,0:T(8,128)(2,1)}, bf16[2,4,2,96,256]{4,3,2,1,0:T(8,128)(2,1)}, f32[2,16,384]{2,1,0:T(8,128)}) custom-call(bf16[256,1536]{1,0:T(8,128)(2,1)} %tokens.3, f32[1536]{0:T(1024)} %gain.3, bf16[96,384]{1,0:T(8,128)(2,1)} %w_gate.1, ...), custom_call_target="tpu_custom_call" | custom-call | tf_op jit(solution)/shard_map/gather_all/pallas_call | solution.py:390
  44.2 42.8 %forward.1 = (f32[1024,768]{1,0:T(8,128)}, f32[1024,768]{1,0:T(8,128)}, f32[1024,768]{1,0:T(8,128)}, f32[4,2,128,384]{3,2,1,0:T(8,128)}, f32[2,1024,128]{2,1,0:T...) custom-call(bf16[1024,1536]{1,0:T(8,128)(2,1)} %get-tuple-element.63, ...), custom_call_target="tpu_custom_call" | custom-call | tf_op jit(solution)/shard_map/forward/pallas_call | solution.py:587
  87.0 42.4 %backward.1 = (bf16[1024,1024]{1,0:T(8,128)(2,1)}, bf16[1024,256]{1,0:T(8,128)(2,1)}, f32[2,16,384]{2,1,0:T(8,128)}, bf16[256,1536]{1,0:T(8,128)(2,1)}, f32[96,384]{1,0:T(8,128)}, /*index=5*/f32[96,384]{1,0:T(8,128)}) custom-call(f32[1024,768]{1,0:T(8,128)} %get-tuple-element.69.gs_in, f32[1024,768]{1,0:T(8,128)} %get-tuple-element.70.inner, ...), custom_call_target="tpu_custom_call" | custom-call | tf_op jit(solution)/shard_map/backward/pallas_call | solution.py:815
  129.4 46.5 %tail.1 = (f32[256,1536]{1,0:T(8,128)}, f32[96,512]{1,0:T(8,128)}, f32[96,256]{1,0:T(8,128)}, f32[48,384]{1,0:T(8,128)}) custom-call(bf16[1024,768]{1,0:T(8,128)(2,1)} %get-tuple-element.68.gg, bf16[1024,1024]{1,0:T(8,128)(2,1)} %get-tuple-element.82.cat, bf16[1536,1792]{1,0:T(8,128)(2,1)} %bitcast.11, ...), custom_call_target="tpu_custom_call" | custom-call | tf_op jit(solution)/shard_map/tail/pallas_call | solution.py:996
  175.9 4.7 %finish.1 = (f32[256,1536]{1,0:T(8,128)}, bf16[256,1536]{1,0:T(8,128)(2,1)}, f32[96,384]{1,0:T(8,128)}, f32[96,256]{1,0:T(8,128)}, f32[96,384]{1,0:T(8,128)}, /*...) custom-call(f32[256,1536]{1,0:T(8,128)} %get-tuple-element.87.tokens, ...), custom_call_target="tpu_custom_call" | custom-call | tf_op jit(solution)/shard_map/finish/pallas_call | solution.py:1081
  180.6 1.3 reduce.1
  181.9 1.3 reduce.2
  183.1 1.3 reduce

commit v5 on v4

--- a/solution.py
+++ b/solution.py
@@ -285,155 +285,152 @@
     return [pltpu.VMEM((256, D), BF16), pltpu.VMEM((2, 128, D), BF16), pltpu.VMEM((2, 256, D), BF16), pltpu.VMEM((2, 256, D), BF16)]
 
 
-def gather_kernel(x, gain, w_gate, w_inner, w_out, w_bc, w_step, conv, bias, gate_gain, step_bias, decay_log, skip, normed_all, wx, wout, wbc, prm, xv, low, stepv, stept, pk, send, recv, local):
-    net = Net(send, recv)
-    at = net.at
-    yh, cx, cc, z, y = at["yh"], at["x"], at["c"], at["z"], at["y"]
-    load = pltpu.make_async_copy(x, xv, local.at[0])
-    load.start()
-    stept[...] = jnp.zeros_like(stept)
-    stept[0:HEADS, 0:96] = w_step[...].astype(F32)
-    stepv[...] = jnp.transpose(stept[...])[0:96, :].astype(BF16)
-    pk[...] = jnp.zeros_like(pk)
-    pk[0:4, :] = conv[...]
-    pk[4:5, :] = bias[...].reshape(1, COLS)
-    pk[5:6, :] = gate_gain[...].reshape(1, COLS)
-    pk[6:7, 0:HEADS] = step_bias[...].reshape(1, HEADS)
-    pk[7:8, 0:HEADS] = decay_log[...].reshape(1, HEADS)
-    pk[8:9, 0:HEADS] = skip[...].reshape(1, HEADS)
-    net.barrier([("z", 1), ("z", -1), ("x", 1), ("x", -1), ("y", 1), ("y", -1), ("y", 2), ("c", 1)])
-    first = {
-        "x": ((w_gate, wx, 0, COLS), (w_out, wout, 0, COLS)),
-        "y": ((w_inner, wx, WIDE, COLS), (stepv, wx, STEPS, 128), (w_bc.at[:, lanes(yh * 128, 128)], wbc, 0, 128)),
-    }
-
-    def spot(ref, base, n, yy, xx, cut=slice(None)):
-        cut = pl.ds(0, 96) if cut == slice(None) else cut
-        return ref.at[lax.rem(yy, 2), xx, cc, cut, lanes(base + (yy // 2) * n, n)]
-
-    own = [pltpu.make_async_copy(src, spot(ref, base, n, y, cx), local.at[1 + i]) for i, (src, ref, base, n) in enumerate(first["x"] + first["y"])]
-    own.append(pltpu.make_async_copy(pk, prm.at[yh], local.at[6]))
-    sent = {"x": [], "y": []}
-    for axis in ("x", "y"):
-        for src, ref, base, n in first[axis]:
-            sent[axis].append([net.start(src, spot(ref, base, n, y, cx), axis, step) for _, step in HALVES])
-    load.wait()
-    v = xv[...].astype(F32)
-    root = lax.rsqrt(jnp.mean(v * v, axis=1, keepdims=True) + EPS)
-    low[...] = (v * root * gain[...].reshape(1, D)).astype(BF16)
-    zs = [net.start(low, rows(normed_all, z * 256, 256), "z", step) for _, step in HALVES]
-    own.append(pltpu.make_async_copy(low, rows(normed_all, z * 256, 256), local.at[7]))
-    for copy in own:
-        copy.start()
-    for axis in ("x", "y"):
-        for src, ref, base, n in first[axis]:
-            net.start(src, spot(ref, base, n, y, cx), "c")
-    net.start(pk, prm.at[yh], "y", 2)
-    second = {"x": [], "y": []}
-    for axis in ("x", "y"):
-        for (src, ref, base, n), copies in zip(first[axis], sent[axis]):
-            for (part, step), copy in zip(HALVES, copies):
-                copy.arrived()
-                cut = pl.ds(48 * part, 48)
-                here = spot(ref, base, n, y, net.near("x", -step), cut) if axis == "x" else spot(ref, base, n, net.near("y", -step), cx, cut)
-                second[axis].append(net.start(here, here, axis, step))
-    for copy in own[:5]:
-        copy.wait()
-    third = {"x": [], "y": []}
-
-    def line(axis, ref, base, n, place, cut=None):
-        cut = pl.ds(0, 96) if cut is None else cut
-        if axis == "x":
-            return ref.at[lax.rem(place, 2), :, cc, cut, lanes(base + (place // 2) * n, n)]
-        return ref.at[:, place, cc, cut, lanes(base, 2 * n)]
-
-    then = {"x": "y", "y": "x"}
-    for axis in ("x", "y"):
-        arrive(second[axis])
-        for src, ref, base, n in first[axis]:
-            here = line(axis, ref, base, n, at[then[axis]])
-            third[axis].append([net.start(here, here, then[axis], step) for _, step in HALVES])
-    for axis in ("x", "y"):
-        for src, ref, base, n in first[axis]:
-            for step in (1, -1, 2):
-                here = spot(ref, base, n, y, net.near("x", step)) if axis == "x" else spot(ref, base, n, net.near("y", step), cx)
-                net.start(here, here, "c")
-    fourth = {"x": [], "y": []}
-
-    def pass_on(axis):
-        for (src, ref, base, n), copies in zip(first[axis], third[axis]):
-            for (part, step), copy in zip(HALVES, copies):
-                copy.arrived()
-                place = net.near(then[axis], -step)
-                here = line(axis, ref, base, n, place, pl.ds(48 * part, 48))
-                fourth[axis].append(net.start(here, here, then[axis], step))
-                here = line(axis, ref, base, n, place)
-                net.start(here, here, "c")
-
-    pass_on("y")
-    pass_on("x")
-    for (part, step), copy in zip(HALVES, zs):
-        copy.arrived()
-        here = rows(normed_all, net.near("z", -step) * 256 + 128 * part, 128)
-        net.start(here, here, "z", step)
-    for axis in ("y", "x"):
-        arrive(fourth[axis])
-        for src, ref, base, n in first[axis]:
-            here = line(axis, ref, base, n, net.near(then[axis], 2))
-            net.start(here, here, "c")
-    net.finish()
-    for copy in own[5:]:
-        copy.wait()
-
-
-def run_gather(*args):
-    return pl.pallas_call(
-        gather_kernel,
-        out_shape=[
-            SHAPE((LEN, D), BF16),
-            SHAPE((2, 4, 2, 96, PROJ), BF16),
-            SHAPE((2, 4, 2, 96, WIDE), BF16),
-            SHAPE((2, 4, 2, 96, 256), BF16),
-            SHAPE((GROUPS, 16, COLS), F32),
-        ],
-        in_specs=[ANY, VMEM, ANY, ANY, ANY, ANY] + [VMEM] * 7,
-        out_specs=[ANY] * 5,
-        scratch_shapes=[
-            pltpu.VMEM((256, D), BF16),
-            pltpu.VMEM((256, D), BF16),
-            pltpu.VMEM((96, 128), BF16),
-            pltpu.VMEM((128, 128), F32),
-            pltpu.VMEM((16, COLS), F32),
-        ]
-        + sems(96)
-        + [pltpu.SemaphoreType.DMA((8,))],
-        compiler_params=pltpu.CompilerParams(collective_id=0, has_side_effects=True, vmem_limit_bytes=ROOM),
-        name="gather_all",
-    )(*args)
-
-
-def forward_kernel(
-    x, wx, wout, wbc, prm, conv_bc, bias_bc, cot,
-    inner_out, z_out, y_out, h_out, dt_out, r_out, u_out, bc_out, bcin_out, zbc_out, normed_t, gains_out, mixed_out, gs_out, gg_out, cot_t,
+def front_kernel(
+    x, gain, w_gate, w_inner, w_out, w_bc, w_step, conv, bias, gate_gain, step_bias, decay_log, skip_gain, conv_bc, bias_bc, cot,
+    inner_out, z_out, y_out, h_out, dt_out, r_out, u_out, bc_out, bcin_out, zbc_out, normed_t, gains_out,
+    mixed_out, gs_out, gg_out, cot_t, normed_out, wx_out, wout_out, wbc_out, prm_out,
+    normed, wx, wout, wbc, prm, xv, stepv, stept, pk,
     cots, gps, acts, slopes, gms, mixed, gg, turned_c, ext, extbc, state, stat, slots, send, recv, local,
 ):
     i = pl.program_id(0)
     net = Net(send, recv)
-    z = net.at["z"]
-    here = lambda step=0: rows(cots, (net.near("z", step) if step else z) * 256, 256)
-    part = lambda p, step: rows(cots, net.near("z", -step) * 256 + 128 * p, 128)
-    c1 = [net.plan(lambda: cot, lambda: here(), "z", step) for _, step in HALVES]
-    c2 = [net.plan(lambda p=p, s=s: part(p, s), lambda p=p, s=s: part(p, s), "z", s) for p, s in HALVES]
+    at = net.at
+    yh, cx, cc, z, y = at["yh"], at["x"], at["c"], at["z"], at["y"]
+    own_rows = lambda ref: rows(ref, z * 256, 256)
+    order = ((0, 1), (1, -1), (1, 1), (0, -1))
+    part = lambda ref, p, s: rows(ref, net.near("z", -s) * 256 + 128 * p, 128)
+    c1 = [
+        net.plan(lambda p=p: cot.at[pl.ds(128 * p, 128)], lambda p=p: rows(cots, z * 256 + 128 * p, 128), "z", s) for p, s in order
+    ]
+    c2 = [net.plan(lambda p=p, s=s: part(cots, p, s), lambda p=p, s=s: part(cots, p, s), "z", s) for p, s in HALVES]
     q = [net.plan(lambda: stat, lambda: slots.at[z], "z", step) for step in (1, -1, 2)]
-    own = lambda: pltpu.make_async_copy(cot, here(), local.at[0])
-    turn_out = lambda: pltpu.make_async_copy(turned_c, cot_t, local.at[1])
+    spot_o = lambda xx, cut=pl.ds(0, 96): wout.at[at["yl"], xx, cc, cut, lanes(yh * COLS, COLS)]
+    line_o = lambda yy, cut=pl.ds(0, 96): wout.at[lax.rem(yy, 2), :, cc, cut, lanes((yy // 2) * COLS, COLS)]
+    same = lambda ref, axis, step=1: net.plan(ref, ref, axis, step)
+    o1 = [net.plan(lambda: w_out, lambda: spot_o(cx), "x", step) for _, step in HALVES]
+    o2 = [same(lambda p=p, s=s: spot_o(net.near("x", -s), pl.ds(48 * p, 48)), "x", s) for p, s in HALVES]
+    o3 = [same(lambda: line_o(y), "y", step) for _, step in HALVES]
+    o4 = [same(lambda p=p, s=s: line_o(net.near("y", -s), pl.ds(48 * p, 48)), "y", s) for p, s in HALVES]
+    oc = [same(lambda: line_o(y), "c")] + [same(lambda s=s: line_o(net.near("y", s)), "c") for s in (1, -1, 2)]
+    own = lambda: pltpu.make_async_copy(cot, own_rows(cots), local.at[0])
+    pairs = ((normed, normed_out), (wx, wx_out), (wbc, wbc_out), (prm, prm_out), (wout, wout_out), (turned_c, cot_t))
+    leave = lambda n: pltpu.make_async_copy(*pairs[n], local.at[1 + n])
 
     @pl.when(i == 0)
     def _():
-        net.barrier([("z", 1), ("z", -1), ("z", 2)])
+        load = pltpu.make_async_copy(x, xv, local.at[7])
+        load.start()
         own().start()
+        stept[...] = jnp.zeros_like(stept)
+        stept[0:HEADS, 0:96] = w_step[...].astype(F32)
+        stepv[...] = jnp.transpose(stept[...])[0:96, :].astype(BF16)
+        pk[...] = jnp.zeros_like(pk)
+        pk[0:4, :] = conv[...]
+        pk[4:5, :] = bias[...].reshape(1, COLS)
+        pk[5:6, :] = gate_gain[...].reshape(1, COLS)
+        pk[6:7, 0:HEADS] = step_bias[...].reshape(1, HEADS)
+        pk[7:8, 0:HEADS] = decay_log[...].reshape(1, HEADS)
+        pk[8:9, 0:HEADS] = skip_gain[...].reshape(1, HEADS)
+        net.barrier([("z", 1), ("z", -1), ("z", 2), ("x", 1), ("x", -1), ("y", 1), ("y", -1), ("y", 2), ("c", 1)])
+        first = {
+            "x": ((w_gate, wx, 0, COLS), (w_bc.at[:, lanes(yh * 128, 128)], wbc, 0, 128)),
+            "y": ((w_inner, wx, WIDE, COLS), (stepv, wx, STEPS, 128)),
+        }
+        then = {"x": "y", "y": "x"}
+        done = []
+
+        def go(src, dst, axis, step=1):
+            done.append(net.start(src, dst, axis, step))
+            return done[-1]
+
+        def spot(ref, base, n, yy, xx, cut=pl.ds(0, 96)):
+            return ref.at[lax.rem(yy, 2), xx, cc, cut, lanes(base + (yy // 2) * n, n)]
+
+        def line(axis, ref, base, n, place, cut=pl.ds(0, 96)):
+            if axis == "x":
+                return ref.at[lax.rem(place, 2), :, cc, cut, lanes(base + (place // 2) * n, n)]
+            return ref.at[:, place, cc, cut, lanes(base, 2 * n)]
+
+        sent = {"x": [], "y": []}
+        for axis in ("x", "y"):
+            for src, ref, base, n in first[axis]:
+                sent[axis].append([go(src, spot(ref, base, n, y, cx), axis, step) for _, step in HALVES])
+        load.wait()
+        v = xv[...].astype(F32)
+        root = lax.rsqrt(jnp.mean(v * v, axis=1, keepdims=True) + EPS)
+        normed[pl.ds(pl.multiple_of(z * 256, 256), 256), :] = (v * root * gain[...].reshape(1, D)).astype(BF16)
+        zs = {}
+        for p, s in order:
+            here = rows(normed, z * 256 + 128 * p, 128)
+            zs[p, s] = go(here, here, "z", s)
+        mine = [
+            pltpu.make_async_copy(src, spot(ref, base, n, y, cx), local.at[8 + k])
+            for k, (src, ref, base, n) in enumerate(first["x"] + first["y"])
+        ]
+        mine.append(pltpu.make_async_copy(pk, prm.at[yh], local.at[12]))
+        mine.append(pltpu.make_async_copy(w_out, spot_o(cx), local.at[13]))
+        for copy in mine:
+            copy.start()
+        for copy in o1:
+            copy.start()
+        for axis in ("x", "y"):
+            for src, ref, base, n in first[axis]:
+                go(src, spot(ref, base, n, y, cx), "c")
+        go(pk, prm.at[yh], "y", 2)
+        second = {"x": [], "y": []}
+        for axis in ("x", "y"):
+            for (src, ref, base, n), copies in zip(first[axis], sent[axis]):
+                for (p, s), copy in zip(HALVES, copies):
+                    copy.arrived()
+                    cut = pl.ds(48 * p, 48)
+                    here = spot(ref, base, n, y, net.near("x", -s), cut) if axis == "x" else spot(ref, base, n, net.near("y", -s), cx, cut)
+                    second[axis].append(go(here, here, axis, s))
+        for copy in mine:
+            copy.wait()
+        third = {"x": [], "y": []}
+        for axis in ("x", "y"):
+            arrive(second[axis])
+            for src, ref, base, n in first[axis]:
+                here = line(axis, ref, base, n, at[then[axis]])
+                third[axis].append([go(here, here, then[axis], s) for _, s in HALVES])
+        for copy, start in zip(o1, o2):
+            copy.arrived()
+            start.start()
+        for axis in ("x", "y"):
+            for src, ref, base, n in first[axis]:
+                for s in (1, -1, 2):
+                    here = spot(ref, base, n, y, net.near("x", s)) if axis == "x" else spot(ref, base, n, net.near("y", s), cx)
+                    go(here, here, "c")
+        for p, s in HALVES:
+            zs[p, s].arrived()
+            here = part(normed, p, s)
+            go(here, here, "z", s)
         for copy in c1:
             copy.start()
+        fourth = {"x": [], "y": []}
+        for axis in ("x", "y"):
+            for (src, ref, base, n), copies in zip(first[axis], third[axis]):
+                for (p, s), copy in zip(HALVES, copies):
+                    copy.arrived()
+                    place = net.near(then[axis], -s)
+                    here = line(axis, ref, base, n, place, pl.ds(48 * p, 48))
+                    fourth[axis].append(go(here, here, then[axis], s))
+                    here = line(axis, ref, base, n, place)
+                    go(here, here, "c")
+        arrive(o2)
+        for copy in o3:
+            copy.start()
+        for axis in ("x", "y"):
+            arrive(fourth[axis])
+            for src, ref, base, n in first[axis]:
+                here = line(axis, ref, base, n, net.near(then[axis], 2))
+                go(here, here, "c")
+        for copy in done:
+            copy.arrived()
+        for copy in done:
+            copy.left()
+        for n in range(4):
+            leave(n).start()
         ext[0:8, :] = jnp.zeros((8, WIDE), F32)
         extbc[0:8, :] = jnp.zeros((8, 256), F32)
         state[...] = jnp.zeros_like(state)
@@ -443,23 +440,27 @@
         ext[0:8, :] = ext[BLOCK : BLOCK + 8, :]
         extbc[0:8, :] = extbc[BLOCK : BLOCK + 8, :]
 
-    @pl.when(i == BLOCKS - 1)
+    @pl.when(i == 2)
     def _():
-        for copy in c1:
+        for copy, start in zip(c1[:2], c2):
             copy.arrived()
-        for copy in c2:
+            start.start()
+        for copy, start in zip(o3, o4):
+            copy.arrived()
+            start.start()
+        for copy in oc[:3]:
             copy.start()
 
     @pl.when(i < BLOCKS)
     def _():
-        xb = x[...]
+        xb = normed[pl.ds(pl.multiple_of(i * BLOCK, BLOCK), BLOCK), :]
         turned = jnp.transpose(xb).reshape(2, 4, 2, 96, BLOCK)
         for core in range(2):
             normed_t[core] = turned[:, :, core]
-        bc_in = dot(xb, wbc[...])
+        bc_in = dot(xb, wbc[...].reshape(D, 256))
         bcin_out[...] = bc_in
         extbc[8 : BLOCK + 8, :] = bc_in
-        zb = bias_bc[...] + sum(conv_bc[j : j + 1, :] * extbc[5 + j : 5 + j + BLOCK, :] for j in range(4))
+        zb = bias_bc[...].reshape(1, 256) + sum(conv_bc[j : j + 1, :] * extbc[5 + j : 5 + j + BLOCK, :] for j in range(4))
         zbc_out[...] = zb
         bc = (zb * sigmoid(zb)).astype(BF16)
         bc_out[...] = bc
@@ -467,9 +468,17 @@
         scores = jnp.where(iota((BLOCK, BLOCK), 0) >= iota((BLOCK, BLOCK), 1), dot_nt(c, b), 0.0)
         tri, ones = lower(), expander()
         left = iota((BLOCK, 128), 1) < 64
-        steps = dot(xb, wx[:, STEPS:])
+        weight = lambda first, n: wx[:, :, :, :, first : first + n].reshape(D, n)
+        steps = dot(xb, weight(STEPS, 256))
         total = jnp.zeros((BLOCK, 128), F32)
         for g in range(GROUPS):
+            if g == 1:
+
+                @pl.when(i == BLOCKS - 1)
+                def _():
+                    arrive(o4)
+                    oc[3].start()
+
             cut = slice(g * COLS, (g + 1) * COLS)
             u = steps[:, 128 * g : 128 * (g + 1)] + prm[g, 6:7, 0:128]
             dt = jnp.maximum(u, 0.0) + jnp.log(1.0 + jnp.exp(-jnp.abs(u)))
@@ -479,8 +488,8 @@
             dt_out[g] = dt
             r_out[g] = r
             rt = jnp.transpose(r)
-            gate = dot(xb, wx[:, cut])
-            inner = dot(xb, wx[:, WIDE + g * COLS : WIDE + (g + 1) * COLS])
+            gate = dot(xb, weight(g * COLS, COLS))
+            inner = dot(xb, weight(WIDE + g * COLS, COLS))
             inner_out[:, cut] = inner
             ext[8 : BLOCK + 8, cut] = inner
             zv = prm[g, 4:5, :] + sum(prm[g, j : j + 1, :] * ext[5 + j : 5 + j + BLOCK, cut] for j in range(4))
@@ -518,6 +527,12 @@
     @pl.when(i == BLOCKS)
     def _():
         own().wait()
+        arrive(oc)
+        leave(4).start()
+
+    @pl.when(i == BLOCKS + 1)
+    def _():
+        arrive(c1)
 
     @pl.when(i == 2 * BLOCKS - 1)
     def _():
@@ -533,7 +548,7 @@
         turned = jnp.transpose(cb).reshape(2, 4, 2, 96, BLOCK)
         for core in range(2):
             turned_c[core, :, :, :, at] = turned[:, :, core]
-        gm = dot(cb, wout[...])
+        gm = dot(cb, wout[...].reshape(D, WIDE))
         gms[at, :] = gm
         gain = jnp.concatenate([prm[0, 5:6, :], prm[1, 5:6, :]], axis=1)
         stat[pl.ds(BLOCKS + block, 1), :] = token_row(gm * gain * gps[at, :])
@@ -552,9 +567,9 @@
         stat[4:8, :] = root * root * root * (sums[4:8, :] * (1.0 / INNER))
         columns = jnp.transpose(stat[...])
         gain = jnp.concatenate([prm[0, 5:6, :], prm[1, 5:6, :]], axis=1)
-        turn_out().start()
+        leave(5).start()
         gain_grad = jnp.zeros((1, WIDE), F32)
-        outs = []
+        moved = []
         for k in range(BLOCKS):
             at = slice(k * BLOCK, (k + 1) * BLOCK)
             gp, gm = gps[at, :], gms[at, :]
@@ -566,26 +581,28 @@
             gg[at, :] = (gated * slopes[at, :]).astype(BF16)
             block = pl.ds(k * BLOCK, BLOCK)
             for src, dst in ((mixed, mixed_out), (gms, gs_out), (gg, gg_out)):
-                outs.append(pltpu.make_async_copy(src.at[block], dst.at[block], local.at[2 + len(outs)]))
-                outs[-1].start()
+                moved.append(pltpu.make_async_copy(src.at[block], dst.at[block], local.at[14 + len(moved)]))
+                moved[-1].start()
         gains_out[...] = jnp.concatenate([gain_grad, jnp.zeros((7, WIDE), F32)], axis=0)
-        for copy in c1 + c2 + q:
+        for copy in c1 + c2 + q + o1 + o2 + o3 + o4 + oc:
             copy.left()
-        for copy in outs:
+        for copy in moved:
             copy.wait()
-        turn_out().wait()
-
-
-def run_forward(x, wx, wout, wbc, prm, conv_bc, bias_bc, cot):
+        for n in range(len(pairs)):
+            leave(n).wait()
+
+
+def run_front(*args):
     first = lambda k: jnp.minimum(k, BLOCKS - 1)
-    const = lambda *s: pl.BlockSpec(s, lambda k: (0,) * len(s), pipeline_mode=pl.Buffered(1))
     keep = lambda *s: pl.BlockSpec(s, lambda k: (0,) * len(s))
     block = lambda n: pl.BlockSpec((BLOCK, n), lambda k: (first(k), 0))
     small = lambda: pl.BlockSpec((GROUPS, BLOCK, 128), lambda k: (0, first(k), 0))
     wide = SHAPE((LEN, WIDE), F32)
     narrow = SHAPE((GROUPS, LEN, 128), F32)
+    bf = lambda *s: pltpu.VMEM(s, BF16)
+    f32 = lambda *s: pltpu.VMEM(s, F32)
     return pl.pallas_call(
-        forward_kernel,
+        front_kernel,
         grid=(2 * BLOCKS,),
         out_shape=[
             wide,
@@ -604,17 +621,13 @@
             wide,
             SHAPE((LEN, WIDE), BF16),
             SHAPE((2, 2, 4, 96, LEN), BF16),
+            SHAPE((LEN, D), BF16),
+            SHAPE((2, 4, 2, 96, PROJ), BF16),
+            SHAPE((2, 4, 2, 96, WIDE), BF16),
+            SHAPE((2, 4, 2, 96, 256), BF16),
+            SHAPE((GROUPS, 16, COLS), F32),
         ],
-        in_specs=[
-            block(D),
-            const(D, PROJ),
-            const(D, WIDE),
-            const(D, 256),
-            const(GROUPS, 16, COLS),
-            const(4, 256),
-            const(1, 256),
-            ANY,
-        ],
+        in_specs=[ANY, VMEM, ANY, ANY, ANY, ANY] + [VMEM] * 9 + [ANY],
         out_specs=[
             block(WIDE),
             block(WIDE),
@@ -629,27 +642,36 @@
             pl.BlockSpec((2, 2, 4, 96, BLOCK), lambda k: (0, 0, 0, 0, first(k))),
             keep(8, WIDE),
         ]
-        + [ANY] * 4,
+        + [ANY] * 9,
         scratch_shapes=[
-            pltpu.VMEM((LEN, D), BF16),
-            pltpu.VMEM((LEN, WIDE), F32),
-            pltpu.VMEM((LEN, WIDE), F32),
-            pltpu.VMEM((LEN, WIDE), F32),
-            pltpu.VMEM((LEN, WIDE), F32),
-            pltpu.VMEM((LEN, WIDE), BF16),
-            pltpu.VMEM((LEN, WIDE), BF16),
-            pltpu.VMEM((2, 2, 4, 96, LEN), BF16),
-            pltpu.VMEM((BLOCK + 8, WIDE), F32),
-            pltpu.VMEM((BLOCK + 8, 256), F32),
-            pltpu.VMEM((STATE, WIDE), F32),
-            pltpu.VMEM((8, BLOCK), F32),
-            pltpu.VMEM((4, 8, BLOCK), F32),
+            bf(LEN, D),
+            bf(2, 4, 2, 96, PROJ),
+            bf(2, 4, 2, 96, WIDE),
+            bf(2, 4, 2, 96, 256),
+            f32(GROUPS, 16, COLS),
+            bf(256, D),
+            bf(96, 128),
+            f32(128, 128),
+            f32(16, COLS),
+            bf(LEN, D),
+            f32(LEN, WIDE),
+            f32(LEN, WIDE),
+            f32(LEN, WIDE),
+            f32(LEN, WIDE),
+            bf(LEN, WIDE),
+            bf(LEN, WIDE),
+            bf(2, 2, 4, 96, LEN),
+            f32(BLOCK + 8, WIDE),
+            f32(BLOCK + 8, 256),
+            f32(STATE, WIDE),
+            f32(8, BLOCK),
+            f32(4, 8, BLOCK),
         ]
-        + sems(7)
-        + [pltpu.SemaphoreType.DMA((14,))],
+        + sems(96)
+        + [pltpu.SemaphoreType.DMA((26,))],
         compiler_params=pltpu.CompilerParams(collective_id=1, has_side_effects=True, vmem_limit_bytes=ROOM),
-        name="forward",
-    )(x, wx, wout, wbc, prm, conv_bc, bias_bc, cot)
+        name="front",
+    )(*args)
 
 
 def backward_kernel(
@@ -1115,13 +1137,13 @@
 
 
 def shards(tokens, norm_gain, w_gate, w_inner, w_bc, w_step, conv_inner, bias_inner, conv_bc, bias_bc, step_bias, decay_log, skip_gain, gate_gain, w_out, cotangent):
-    normed, wx, wout, wbc, prm = run_gather(
-        tokens, norm_gain, w_gate, w_inner, w_out, w_bc, w_step.T, conv_inner, bias_inner, gate_gain, step_bias, decay_log, skip_gain
+    (
+        inner, zin, y, hin, dt, r, u, bc, bc_in, zbc, normed_t, gains, mixed, gs, gg, cot_t, normed, wx, wout, wbc, prm,
+    ) = run_front(
+        tokens, norm_gain, w_gate, w_inner, w_out, w_bc, w_step.T, conv_inner, bias_inner, gate_gain, step_bias, decay_log,
+        skip_gain, conv_bc, bias_bc, cotangent,
     )
     wx, wout, wbc = wx.reshape(D, PROJ), wout.reshape(D, WIDE), wbc.reshape(D, 256)
-    inner, zin, y, hin, dt, r, u, bc, bc_in, zbc, normed_t, gains, mixed, gs, gg, cot_t = run_forward(
-        normed, wx, wout, wbc, prm, conv_bc, bias_bc.reshape(1, 256), cotangent
-    )
     cat, dbc, acc, output, wout_grad, gate_grad = run_backward(
         gs, inner, zin, y, hin, prm, bc, dt, r, u, gains, mixed, wout, cot_t, gg, normed_t, tokens
     )

time: 185 us -> 174 us (0.941)
  Pallas kernels: 180 us -> 168 us
    pallas_call x2 -> x1, Pallas kernels: 86.3 us -> 74.1 us  [run_front(): pl.pallas_call(front_kernel, grid=(2 * BLOCKS,), out_shape=[wide, wide, w...]
where the time goes in v5:
time: 174 us; the launch traced here: 173 us
  Pallas kernels  168 us (97%)
  other arithmetic  3.86 us (2%)
    pallas_call x1, Pallas kernels, run_front(): pl.pallas_call(front_kernel, grid=(2 * BLOCKS,), out_shape=[wide, wide, w...  74.1 us
    pallas_call x1, Pallas kernels, run_tail(): pl.pallas_call(tail_kernel, out_shape=[SHAPE((256, D), F32), SHAPE((96, C...  47 us
    pallas_call x1, Pallas kernels, run_backward(): pl.pallas_call(backward_kernel, grid=(BLOCKS,), out_shape=[SHAPE((LEN, MO...  42.4 us
    pallas_call x1, Pallas kernels, run_finish(): pl.pallas_call(finish_kernel, out_shape=[f32(256, D), SHAPE((256, D), BF1...  4.7 us
    pallas_call x3, other arithmetic, run_finish(): pl.pallas_call(finish_kernel, out_shape=[f32(256, D), SHAPE((256, D), BF1...  3.86 us

profile of v5, /device:TPU:0, one launch (start us, length us, event | category | flops | bytes accessed | tf_op | source)
XLA Modules:
  0.0 172.7 jit_solution(1590060065722737483)
XLA Ops:
  0.7 74.1 %front.1 = (f32[1024,768]{1,0:T(8,128)}, f32[1024,768]{1,0:T(8,128)}, f32[1024,768]{1,0:T(8,128)}, f32[4,2,128,384]{3,2,1,0:T(8,128)}, f32[2,1024,128]{2,1,0:T(8...) custom-call(bf16[256,1536]{1,0:T(8,128)(2,1)} %tokens.3, ...), custom_call_target="tpu_custom_call" | custom-call | tf_op jit(solution)/shard_map/front/pallas_call | solution.py:604
  74.8 42.4 %backward.1 = (bf16[1024,1024]{1,0:T(8,128)(2,1)}, bf16[1024,256]{1,0:T(8,128)(2,1)}, f32[2,16,384]{2,1,0:T(8,128)}, bf16[256,1536]{1,0:T(8,128)(2,1)}, f32[96,384]{1,0:T(8,128)}, /*index=5*/f32[96,384]{1,0:T(8,128)}) custom-call(f32[1024,768]{1,0:T(8,128)} %get-tuple-element.64.gs_in, f32[1024,768]{1,0:T(8,128)} %get-tuple-element.65.inner, ...), custom_call_target="tpu_custom_call" | custom-call | tf_op jit(solution)/shard_map/backward/pallas_call | solution.py:837
  117.1 47.0 %tail.1 = (f32[256,1536]{1,0:T(8,128)}, f32[96,512]{1,0:T(8,128)}, f32[96,256]{1,0:T(8,128)}, f32[48,384]{1,0:T(8,128)}) custom-call(bf16[1024,768]{1,0:T(8,128)(2,1)} %get-tuple-element.63.gg, bf16[1024,1024]{1,0:T(8,128)(2,1)} %get-tuple-element.79.cat, bf16[1536,1792]{1,0:T(8,128)(2,1)} %bitcast.9, ...), custom_call_target="tpu_custom_call" | custom-call | tf_op jit(solution)/shard_map/tail/pallas_call | solution.py:1018
  164.1 4.7 %finish.1 = (f32[256,1536]{1,0:T(8,128)}, bf16[256,1536]{1,0:T(8,128)(2,1)}, f32[96,384]{1,0:T(8,128)}, f32[96,256]{1,0:T(8,128)}, f32[96,384]{1,0:T(8,128)}, /*...) custom-call(f32[256,1536]{1,0:T(8,128)} %get-tuple-element.87.tokens, ...), custom_call_target="tpu_custom_call" | custom-call | tf_op jit(solution)/shard_map/finish/pallas_call | solution.py:1103
  168.8 1.3 reduce.1
  170.1 1.3 reduce.2
  171.4 1.3 reduce

commit v6 on v5

--- a/solution.py
+++ b/solution.py
@@ -264,20 +264,25 @@
         self.one = [
             net.plan(lambda p=p: self.far.at[pl.ds(128 * p, 128)], lambda p=p: self.half.at[p], "z", step) for p, step in HALVES
         ]
-        self.two = [net.plan(lambda p=p: self.fold.at[p], lambda p=p: self.whole.at[p], "z", step) for p, step in HALVES]
+        half = lambda ref, p, n: ref.at[p, pl.ds(128 * n, 128)]
+        self.ready = [net.plan(lambda p=p: half(self.fold, p, 1 - p), lambda p=p: half(self.whole, p, 1 - p), "z", step) for p, step in HALVES]
+        self.added = [net.plan(lambda p=p: half(self.fold, p, p), lambda p=p: half(self.whole, p, p), "z", step) for p, step in HALVES]
 
     def step1(self):
         for copy in self.one:
             copy.start()
+
+    def folded(self, p):
+        self.ready[p].start()
 
     def step2(self):
         arrive(self.one)
         for p, _ in HALVES:
             self.fold[p, 128 * p : 128 * p + 128, :] += self.half[p]
-            self.two[p].start()
+            self.added[p].start()
 
     def step3(self):
-        arrive(self.two)
+        arrive(self.ready + self.added)
         return self.whole[0].astype(F32) + self.whole[1].astype(F32)
 
 
@@ -675,9 +680,9 @@
 
 
 def backward_kernel(
-    gs_in, inner, zin, y, hin, prm, bc, dt, r, u, gains, mixed, wout, cot_t, gg, normed_t, tokens,
-    cat_out, dbc_out, acc, branch_out, wout_out, wgate_out,
-    ext, dstate, dst, dbc, held, got, away, mv, wv, cv, gv, nv, ownb, g0, g1, g2, g3, s1, s2, s3, t1, t2, t3, send, recv, local,
+    gs_in, inner, zin, y, hin, prm, bc, dt, r, u, gains, mixed, wout, cot_t, gg, normed_t, tokens, zbc, bc_in, conv_bc,
+    cat_out, acc, acc_bc, branch_out, wout_out, wgate_out,
+    ext, extbc, dstate, dst, dbc, held, got, away, mv, wv, cv, gv, nv, ownb, g0, g1, g2, g3, s1, s2, s3, t1, t2, t3, send, recv, local,
 ):
     k = pl.program_id(0)
     net = Net(send, recv)
@@ -705,12 +710,15 @@
         loads[4].wait()
         away[1] = grads(nv, gv, net.other)
         cross[1].start()
-        g2[0] = branch(net.near("z", 1)).astype(BF16)
-        g2[1] = branch(net.near("z", -1)).astype(BF16)
+        for p, step in HALVES:
+            g2[p] = branch(net.near("z", step)).astype(BF16)
+            token.folded(p)
         ownb[...] = branch(z)
         held[0] = grads(cv, mv, cc)
         held[1] = grads(nv, gv, cc)
         acc[...] = jnp.zeros_like(acc)
+        acc_bc[...] = jnp.zeros_like(acc_bc)
+        extbc[BLOCK : BLOCK + 8, :] = jnp.zeros((8, 256), F32)
         for g in range(GROUPS):
             acc[g, 5:6, :] = gains[0:1, g * COLS : (g + 1) * COLS]
         ext[BLOCK : BLOCK + 8, :] = jnp.zeros((8, WIDE), F32)
@@ -719,6 +727,7 @@
     @pl.when(k > 0)
     def _():
         ext[BLOCK : BLOCK + 8, :] = ext[0:8, :]
+        extbc[BLOCK : BLOCK + 8, :] = extbc[0:8, :]
 
     b, c = bc[:, :STATE], bc[:, STATE:]
     valid = iota((BLOCK, BLOCK), 1) >= iota((BLOCK, BLOCK), 0)
@@ -815,8 +824,20 @@
         acc[g, 7:8, 0:128] += jnp.sum(da * dt[g], axis=0, keepdims=True) * rate
         acc[g, 8:9, 0:128] += folded(jnp.sum(skipgrad, axis=0, keepdims=True) + jnp.zeros((8, COLS), F32), fold)[0:1, :]
     ds = jnp.where(valid, dst[...], 0.0).astype(BF16)
-    dbc_out[:, STATE:] = (dbc[:, STATE:] + dot_tn(ds, b)).astype(BF16)
-    dbc_out[:, :STATE] = (dbc[:, :STATE] + dot(ds, c)).astype(BF16)
+    dbc[:, STATE:] += dot_tn(ds, b)
+    dbc[:, :STATE] += dot(ds, c)
+    zb = zbc[...]
+    sig = sigmoid(zb)
+    dz = dbc[...] * (sig + zb * sig * (1.0 - sig))
+    extbc[0:BLOCK, :] = dz
+    bi = bc_in[...]
+    gi = jnp.zeros((BLOCK, 256), F32)
+    for j in range(4):
+        moved = extbc[3 - j : 3 - j + BLOCK, :]
+        gi = gi + conv_bc[j : j + 1, :] * moved
+        acc_bc[j : j + 1, :] += jnp.sum(bi * moved, axis=0, keepdims=True)
+    acc_bc[4:5, :] += jnp.sum(dz, axis=0, keepdims=True)
+    cat_out[:, MORE:] = gi.astype(BF16)
 
     @pl.when(k == BLOCKS - 1)
     def _():
@@ -838,9 +859,9 @@
         backward_kernel,
         grid=(BLOCKS,),
         out_shape=[
-            SHAPE((LEN, MORE), BF16),
-            SHAPE((LEN, 256), BF16),
+            SHAPE((LEN, MORE + 256), BF16),
             SHAPE((GROUPS, 16, COLS), F32),
+            SHAPE((8, 256), F32),
             SHAPE((256, D), BF16),
             SHAPE((96, COLS), F32),
             SHAPE((96, COLS), F32),
@@ -856,10 +877,11 @@
             keep(8, WIDE),
         ]
         + [ANY] * 5
-        + [keep(256, D)],
-        out_specs=[cols(MORE), cols(256), keep(GROUPS, 16, COLS), keep(256, D), keep(96, COLS), keep(96, COLS)],
+        + [keep(256, D), cols(256), cols(256), keep(4, 256)],
+        out_specs=[cols(MORE + 256), keep(GROUPS, 16, COLS), keep(8, 256), keep(256, D), keep(96, COLS), keep(96, COLS)],
         scratch_shapes=[
             f32(BLOCK + 8, WIDE),
+            f32(BLOCK + 8, 256),
             f32(STATE, WIDE),
             f32(BLOCK, BLOCK),
             f32(BLOCK, 256),
@@ -876,7 +898,7 @@
         + token_scratch()
         + grid_scratch("y", COLS)
         + grid_scratch("x", COLS)
-        + sems(24)
+        + sems(26)
         + [pltpu.SemaphoreType.DMA((5,))],
         compiler_params=pltpu.CompilerParams(collective_id=2, has_side_effects=True, vmem_limit_bytes=ROOM),
         name="backward",
@@ -884,27 +906,15 @@
 
 
 def tail_kernel(
-    gg, cat, wx, normed_t, normed, dbc, zbc, bc_in, acc, wbc, tokens, cot, gain, conv,
+    gg, cat, wx, normed_t, normed, acc, acc_bc, wbc, gain,
     tokens_out, inner_out, bc_out, small_out,
-    ggv, catv, wxv, ntv, nv, mine, slots, zv, xi, wv, xv, ov, ext, gnbc, ownb, held, got, away, dbw, heldb, gotb, small, sp0, sp1, sp2, sp3, bz, by,
+    ggv, catv, wxv, ntv, nv, wv, ownb, held, got, away, dbw, heldb, gotb, small, sp0, sp1, sp2, sp3, bz, by,
     g0, g1, g2, g3, a1, a2, a3, b1, b2, b3, c1, c2, c3, send, recv, local,
 ):
     net = Net(send, recv)
     at = net.at
     yh, cx, cc, z, y = at["yh"], at["x"], at["c"], at["z"], at["y"]
-    pairs = (
-        (gg, ggv),
-        (cat, catv),
-        (wx, wxv),
-        (normed, nv),
-        (normed_t, ntv),
-        (rows(zbc, z * 256, 256), zv.at[pl.ds(0, 256)]),
-        (rows(zbc, lax.rem(z * 256 + 256, LEN), 16), zv.at[pl.ds(256, 16)]),
-        (rows(bc_in, z * 256, 256), xi),
-        (wbc, wv),
-        (tokens, xv),
-        (cot, ov),
-    )
+    pairs = ((cat, catv), (gg, ggv), (wx, wxv), (wbc, wv), (normed, nv), (normed_t, ntv))
     loads = [pltpu.make_async_copy(src, dst, local.at[i]) for i, (src, dst) in enumerate(pairs)]
     for copy in loads:
         copy.start()
@@ -912,75 +922,60 @@
     spans = ((0, COLS), (WIDE, 128))
     rings = (GridSum(net, "x", held, spans, (a1, a2, a3), (0, 48)), GridSum(net, "y", held, spans, (b1, b2, b3), (48, 48)))
     ring_bc = GridSum(net, "x", heldb, ((0, 128),), (c1, c2, c3))
-    mine[0:LEN, :] = dbc[...]
-    mine[LEN : LEN + 16, :] = jnp.zeros((16, 256), BF16)
-    slots[z] = mine[pl.ds(pl.multiple_of(z * 256, 16), 272), :]
     net.barrier([(a, s) for a in ("z", "x", "y") for s in (1, -1, 2)] + [("c", 1)])
-    swap = [net.start(rows(mine, net.near("z", s) * 256, 272), slots.at[z], "z", s) for s in (1, -1, 2)]
-    gain_row = gain[...].reshape(1, D)
-    norm_part = jnp.zeros((1, D), F32)
 
     def block(place):
         cut = pl.ds(pl.multiple_of(place * 256, 256), 256)
-        got = dot_nt(ggv[cut, :], wxv[:, 0:WIDE]) + dot_nt(catv[cut, :], wxv[:, WIDE:])
-        return got, jnp.sum(got * nv[cut, :].astype(F32), axis=0, keepdims=True)
+        return dot_nt(ggv[cut, :], wxv[:, 0:WIDE]) + dot_nt(catv[cut, 0:MORE], wxv[:, WIDE:]) + dot_nt(catv[cut, MORE:], wv[...])
+
+    def of_norm(place, grad):
+        cut = pl.ds(pl.multiple_of(place * 256, 256), 256)
+        return jnp.sum(grad * nv[cut, :].astype(F32), axis=0, keepdims=True)
 
     for copy in loads[:4]:
         copy.wait()
-    out, part = block(net.near("z", 2))
-    norm_part = norm_part + part
-    g0[...] = out.astype(BF16)
+    far = block(net.near("z", 2))
+    g0[...] = far.astype(BF16)
     token.step1()
-    grads = lambda core: dot(ntv[core].reshape(8 * 96, LEN), catv[...]).astype(BF16).reshape(2, 4, 96, MORE)
     loads[4].wait()
-    away[...] = grads(net.other)
-    cross = net.start(away, got, "c")
-    for copy in loads[5:]:
-        copy.wait()
-    arrive(swap)
-    total = (slots[0].astype(F32) + slots[1].astype(F32)) + (slots[2].astype(F32) + slots[3].astype(F32))
-    sig = sigmoid(zv[...])
-    dz = total * (sig * (1.0 + zv[...] * (1.0 - sig)))
-    ext[...] = jnp.where(iota((272, 256), 0) + z * 256 < LEN, dz, 0.0)
-    gbc = jnp.zeros((256, 256), F32)
+    norm_part = of_norm(net.near("z", 2), far)
+    for p, step in HALVES:
+        out = block(net.near("z", step))
+        g2[p] = out.astype(BF16)
+        norm_part = norm_part + of_norm(net.near("z", step), out)
+    ownb[...] = block(z)
+    norm_part = (norm_part + of_norm(z, ownb[...])) / gain[...].reshape(1, D)
     small[0:16, :] = acc[0]
     small[16:32, :] = acc[1]
     small[32:48, :] = jnp.zeros((16, COLS), F32)
-    for j in range(4):
-        moved = ext[3 - j : 3 - j + 256, :]
-        gbc = gbc + conv[j : j + 1, :] * moved
-        small[36 + j : 37 + j, 0:256] = jnp.sum(xi[...] * moved, axis=0, keepdims=True)
-    small[40:41, 0:256] = jnp.sum(ext[0:256, :], axis=0, keepdims=True)
-    gbc = gbc.astype(BF16)
-    own = pl.ds(pl.multiple_of(z * 256, 256), 256)
+    for k in range(4):
+        small[32 + k : 33 + k, :] = norm_part[:, k * COLS : (k + 1) * COLS]
+    small[36:41, 0:256] = acc_bc[0:5, :]
+    sp0[z] = small[32:48, :]
+    q = net.around(sp0.at[z], sp0.at[z], "z")
+    for p, _ in HALVES:
+        token.folded(p)
+    loads[5].wait()
+    grads = lambda core, cut, n: dot(ntv[core].reshape(8 * 96, LEN), catv[:, cut]).astype(BF16).reshape(2, 4, 96, n)
     for core in range(2):
-        dbw[core] = dot(ntv[core, :, :, :, own].reshape(8 * 96, 256), gbc).astype(BF16).reshape(2, 4, 96, 256)
+        dbw[core] = grads(core, slice(MORE, MORE + 256), 256)
     crossb = net.start(dbw.at[net.other], gotb, "c")
-    gnbc[...] = dot_nt(gbc, wv[...])
-    norm_part = norm_part + jnp.sum(gnbc[...] * nv[own, :].astype(F32), axis=0, keepdims=True)
-    held[...] = grads(cc)
-    cross.arrived()
-    held[...] += got[...]
-    for ring in rings:
-        ring.step1()
+    away[...] = grads(net.other, slice(0, MORE), MORE)
+    cross = net.start(away, got, "c")
     crossb.arrived()
     heldb[...] = dbw[cc] + gotb[...]
     ring_bc.step1()
-    for p, step in HALVES:
-        out, part = block(net.near("z", step))
-        norm_part = norm_part + part
-        g2[p] = out.astype(BF16)
-    token.step2()
-    out, part = block(z)
-    norm_part = (norm_part + part) / gain_row
-    ownb[...] = out + gnbc[...]
-    for k in range(4):
-        small[32 + k : 33 + k, :] = norm_part[:, k * COLS : (k + 1) * COLS]
-    sp1[cx] = small[...]
+    held[...] = grads(cc, slice(0, MORE), MORE)
+    cross.arrived()
+    held[...] += got[...]
+    arrive(q)
+    sp1[cx, 0:32, :] = small[0:32, :]
+    sp1[cx, 32:48, :] = (sp0[0] + sp0[1]) + (sp0[2] + sp0[3])
     q = net.around(sp1.at[cx], sp1.at[cx], "x")
     ring_bc.step2()
-    v = xv[...].astype(F32)
-    root = lax.rsqrt(jnp.mean(v * v, axis=1, keepdims=True) + EPS)
+    for ring in rings:
+        ring.step1()
+    token.step2()
     arrive(q)
     sp2[y] = (sp1[0] + sp1[1]) + (sp1[2] + sp1[3])
     q = net.around(sp2.at[y], sp2.at[y], "y")
@@ -988,27 +983,20 @@
     qb = [net.start(by.at[yh], by.at[yh], "y", 2)]
     for ring in rings:
         ring.step2()
-    arrive(q)
-    sp3[cc] = (sp2[0] + sp2[1]) + (sp2[2] + sp2[3])
-    q = [net.start(sp3.at[cc], sp3.at[cc], "c")]
     arrive(qb)
     bz[z, :, 0:128] = by[0]
     bz[z, :, 128:256] = by[1]
     qb = net.around(bz.at[z], bz.at[z], "z")
     arrive(q)
-    small[...] = sp3[0] + sp3[1]
-    sp0[z] = small[32:48, :]
-    q = net.around(sp0.at[z], sp0.at[z], "z")
-    small_out[0:32, :] = small[0:32, :]
+    sp3[cc] = (sp2[0] + sp2[1]) + (sp2[2] + sp2[3])
+    q = [net.start(sp3.at[cc], sp3.at[cc], "c")]
     for ring in rings:
         ring.step3(inner_out)
-    g = token.step3() + ownb[...]
-    scaled = g * gain_row
-    tokens_out[...] = ov[...].astype(F32) + root * scaled - v * (root * root * root) * jnp.mean(scaled * v, axis=1, keepdims=True)
+    arrive(q)
+    small_out[...] = sp3[0] + sp3[1]
+    tokens_out[...] = token.step3() + ownb[...]
     arrive(qb)
     bc_out[...] = (bz[0] + bz[1]) + (bz[2] + bz[3])
-    arrive(q)
-    small_out[32:48, :] = (sp0[0] + sp0[1]) + (sp0[2] + sp0[3])
     net.finish()
 
 
@@ -1023,23 +1011,15 @@
             SHAPE((96, 256), F32),
             SHAPE((48, COLS), F32),
         ],
-        in_specs=[ANY] * 5 + [VMEM, ANY, ANY, VMEM, ANY, ANY, ANY, VMEM, VMEM],
+        in_specs=[ANY] * 5 + [VMEM, VMEM, ANY, VMEM],
         out_specs=[VMEM] * 4,
         scratch_shapes=[
             bf(LEN, WIDE),
-            bf(LEN, MORE),
+            bf(LEN, MORE + 256),
             bf(D, PROJ),
             bf(2, 2, 4, 96, LEN),
             bf(LEN, D),
-            bf(LEN + 16, 256),
-            bf(4, 272, 256),
-            f32(272, 256),
-            f32(256, 256),
             bf(D, 256),
-            bf(256, D),
-            bf(256, D),
-            f32(272, 256),
-            f32(256, D),
             f32(256, D),
             bf(2, 4, 96, MORE),
             bf(2, 4, 96, MORE),
@@ -1060,77 +1040,52 @@
         + grid_scratch("y", COLS + 128, 48)
         + grid_scratch("x", 128)
         + sems(64)
-        + [pltpu.SemaphoreType.DMA((11,))],
+        + [pltpu.SemaphoreType.DMA((6,))],
         compiler_params=pltpu.CompilerParams(collective_id=3, has_side_effects=True, vmem_limit_bytes=ROOM),
         name="tail",
     )(*args)
 
 
-def finish_kernel(tokens, branch, inner, bc, small, gate, wout, tokens_out, branch_out, inner_out, bc_out, gate_out, wout_out, step_out, norm, conv, bias, conv_bc, bias_bc, step_bias, decay, skip, gain, tv, rv, iv, cv, gv, wv, sem):
-    trips = (
-        (tokens, tv, tokens_out),
-        (branch, rv, branch_out),
-        (inner.at[:, pl.ds(0, COLS)], iv, inner_out),
-        (bc, cv, bc_out),
-        (gate, gv, gate_out),
-        (wout, wv, wout_out),
-    )
-    reads = [pltpu.make_async_copy(src, via, sem.at[i]) for i, (src, via, dst) in enumerate(trips)]
-    copies = [pltpu.make_async_copy(via, dst, sem.at[len(trips) + i]) for i, (src, via, dst) in enumerate(trips)]
-    for copy in reads:
-        copy.start()
-    for read, copy in zip(reads, copies):
-        read.wait()
-        copy.start()
-    step_out[...] = jnp.transpose(jnp.concatenate([inner[:, COLS:], jnp.zeros((32, 128), F32)], axis=0))[0:HEADS, 0:96]
-    for k in range(4):
-        norm[:, k * COLS : (k + 1) * COLS] = small[32 + k : 33 + k, :]
-    conv_bc[...] = small[36:40, 0:256]
-    bias_bc[...] = small[40:41, 0:256]
-    mine = small[pl.ds(pl.multiple_of(lax.axis_index("yh") * 16, 8), 16), :]
-    conv[...] = mine[0:4, :]
-    bias[...] = mine[4:5, :]
-    gain[...] = mine[5:6, :]
-    step_bias[...] = mine[6:7, 0:HEADS]
-    decay[...] = mine[7:8, 0:HEADS]
-    skip[...] = mine[8:9, 0:HEADS]
-    for copy in copies:
-        copy.wait()
+def finish_kernel(grad, tokens, cot, branch, norm_gain, inner, bc, small, gate, wout, tokens_out, branch_out, inner_out, bc_out, gate_out, wout_out, step_out, norm, conv, bias, conv_bc, bias_bc, step_bias, decay, skip, gain):
+    v = tokens[...].astype(F32)
+    root = lax.rsqrt(jnp.mean(v * v, axis=1, keepdims=True) + EPS)
+    scaled = grad[...] * norm_gain[...].reshape(1, D)
+    tokens_out[...] = cot[...].astype(F32) + root * scaled - v * (root * root * root) * jnp.mean(scaled * v, axis=1, keepdims=True)
+    branch_out[...] = branch[...]
+
+    @pl.when(pl.program_id(0) == 0)
+    def _():
+        inner_out[...] = inner[:, :COLS]
+        bc_out[...] = bc[...]
+        gate_out[...] = gate[...]
+        wout_out[...] = wout[...]
+        step_out[...] = jnp.transpose(jnp.concatenate([inner[:, COLS:], jnp.zeros((32, 128), F32)], axis=0))[0:HEADS, 0:96]
+        norm[...] = jnp.concatenate([small[32 + k : 33 + k, :] for k in range(4)], axis=1).reshape(D)
+        conv_bc[...] = small[36:40, 0:256]
+        bias_bc[...] = small[40:41, 0:256].reshape(256)
+        mine = small[pl.ds(pl.multiple_of(lax.axis_index("yh") * 16, 8), 16), :]
+        conv[...] = mine[0:4, :]
+        bias[...] = mine[4:5, :].reshape(COLS)
+        gain[...] = mine[5:6, :].reshape(COLS)
+        step_bias[...] = mine[6:7, 0:HEADS].reshape(HEADS)
+        decay[...] = mine[7:8, 0:HEADS].reshape(HEADS)
+        skip[...] = mine[8:9, 0:HEADS].reshape(HEADS)
 
 
 def run_finish(*args):
     f32 = lambda *s: SHAPE(s, F32)
+    strip = lambda: pl.BlockSpec((64, D), lambda k: (k, 0))
+    whole = lambda *s: pl.BlockSpec(s, lambda k: (0,) * len(s))
+    shapes = (
+        (96, COLS), (96, 256), (96, COLS), (96, COLS), (HEADS, 96), (D,), (4, COLS), (COLS,), (4, 256), (256,), (HEADS,), (HEADS,), (HEADS,), (COLS,),
+    )
     return pl.pallas_call(
         finish_kernel,
-        out_shape=[
-            f32(256, D),
-            SHAPE((256, D), BF16),
-            f32(96, COLS),
-            f32(96, 256),
-            f32(96, COLS),
-            f32(96, COLS),
-            f32(HEADS, 96),
-            f32(1, D),
-            f32(4, COLS),
-            f32(1, COLS),
-            f32(4, 256),
-            f32(1, 256),
-            f32(1, HEADS),
-            f32(1, HEADS),
-            f32(1, HEADS),
-            f32(1, COLS),
-        ],
-        in_specs=[ANY, ANY, VMEM, ANY, VMEM, ANY, ANY],
-        out_specs=[ANY] * 6 + [VMEM] * 10,
-        scratch_shapes=[
-            pltpu.VMEM((256, D), F32),
-            pltpu.VMEM((256, D), BF16),
-            pltpu.VMEM((96, COLS), F32),
-            pltpu.VMEM((96, 256), F32),
-            pltpu.VMEM((96, COLS), F32),
-            pltpu.VMEM((96, COLS), F32),
-            pltpu.SemaphoreType.DMA((12,)),
-        ],
+        grid=(4,),
+        out_shape=[f32(256, D), SHAPE((256, D), BF16)] + [f32(*s) for s in shapes],
+        in_specs=[strip(), strip(), strip(), strip()]
+        + [whole(*s) for s in ((D,), (96, COLS + 128), (96, 256), (48, COLS), (96, COLS), (96, COLS))],
+        out_specs=[strip(), strip()] + [whole(*s) for s in shapes],
         compiler_params=pltpu.CompilerParams(vmem_limit_bytes=ROOM),
         name="finish",
     )(*args)
@@ -1144,20 +1099,17 @@
         skip_gain, conv_bc, bias_bc, cotangent,
     )
     wx, wout, wbc = wx.reshape(D, PROJ), wout.reshape(D, WIDE), wbc.reshape(D, 256)
-    cat, dbc, acc, output, wout_grad, gate_grad = run_backward(
-        gs, inner, zin, y, hin, prm, bc, dt, r, u, gains, mixed, wout, cot_t, gg, normed_t, tokens
+    cat, acc, acc_bc, output, wout_grad, gate_grad = run_backward(
+        gs, inner, zin, y, hin, prm, bc, dt, r, u, gains, mixed, wout, cot_t, gg, normed_t, tokens, zbc, bc_in, conv_bc
     )
-    tokens_grad, inner_grad, bc_grad, small = run_tail(
-        gg, cat, wx, normed_t, normed, dbc, zbc, bc_in, acc, wbc, tokens, cotangent, norm_gain, conv_bc
-    )
+    grad, inner_grad, bc_grad, small = run_tail(gg, cat, wx, normed_t, normed, acc, acc_bc, wbc, norm_gain)
     (
         tokens_grad, output, inner_grad, bc_grad, gate_grad, wout_grad, step_grad,
         norm, conv, bias, conv_bc_grad, bias_bc_grad, step_bias_grad, decay, skip, gate_gain_grad,
-    ) = run_finish(tokens_grad, output, inner_grad, bc_grad, small, gate_grad, wout_grad)
-    flat = lambda v: v.reshape(-1)
+    ) = run_finish(grad, tokens, cotangent, output, norm_gain, inner_grad, bc_grad, small, gate_grad, wout_grad)
     return (
-        output, tokens_grad, flat(norm), gate_grad, inner_grad, bc_grad, step_grad.T, conv, flat(bias), conv_bc_grad,
-        flat(bias_bc_grad), flat(step_bias_grad), flat(decay), flat(skip), flat(gate_gain_grad), wout_grad,
+        output, tokens_grad, norm, gate_grad, inner_grad, bc_grad, step_grad.T, conv, bias, conv_bc_grad,
+        bias_bc_grad, step_bias_grad, decay, skip, gate_gain_grad, wout_grad,
     )
 
 

time: 174 us -> 171 us (0.983)
  other arithmetic: 3.86 us -> 0 us
  Pallas kernels: 168 us -> 170 us
    pallas_call x3 -> x0, other arithmetic: 3.86 us -> none  [run_finish(): pl.pallas_call(finish_kernel, out_shape=[f32(256, D), SHAPE((256, D), BF1...]
where the time goes in v6:
time: 171 us; the launch traced here: 170 us
  Pallas kernels  170 us (99%)
    pallas_call x1, Pallas kernels, run_front(): pl.pallas_call(front_kernel, grid=(2 * BLOCKS,), out_shape=[wide, wide, w...  74.1 us
    pallas_call x1, Pallas kernels, run_tail(): pl.pallas_call(tail_kernel, out_shape=[SHAPE((256, D), F32), SHAPE((96, C...  47.3 us
    pallas_call x1, Pallas kernels, run_backward(): pl.pallas_call(backward_kernel, grid=(BLOCKS,), out_shape=[SHAPE((LEN, MO...  43 us
    pallas_call x1, Pallas kernels, run_finish(): pl.pallas_call(finish_kernel, grid=(4,), out_shape=[f32(256, D), SHAPE((2...  5.12 us

profile of v6, /device:TPU:0, one launch (start us, length us, event | category | flops | bytes accessed | tf_op | source)
XLA Modules:
  0.0 170.4 jit_solution(17681005646152017446)
XLA Ops:
  0.7 74.1 %front.1 = (f32[1024,768]{1,0:T(8,128)}, f32[1024,768]{1,0:T(8,128)}, f32[1024,768]{1,0:T(8,128)}, f32[4,2,128,384]{3,2,1,0:T(8,128)}, f32[2,1024,128]{2,1,0:T(8...) custom-call(bf16[256,1536]{1,0:T(8,128)(2,1)} %tokens.3, ...), custom_call_target="tpu_custom_call" | custom-call | tf_op jit(solution)/shard_map/front/pallas_call | solution.py:609
  74.8 43.0 %backward.1 = (bf16[1024,1280]{1,0:T(8,128)(2,1)}, f32[2,16,384]{2,1,0:T(8,128)}, f32[8,256]{1,0:T(8,128)}, bf16[256,1536]{1,0:T(8,128)(2,1)}, f32[96,384]{1,0:T(8,128)}, /*index=5*/f32[96,384]{1,0:T(8,128)}) custom-call(f32[1024,768]{1,0:T(8,128)} %get-tuple-element.64.gs_in, f32[1024,768]{1,0:T(8,128)} %get-tuple-element.65.inner, ...), custom_call_target="tpu_custom_call" | custom-call | tf_op jit(solution)/shard_map/backward/pallas_call | solution.py:858
  117.7 47.3 %tail.1 = (f32[256,1536]{1,0:T(8,128)}, f32[96,512]{1,0:T(8,128)}, f32[96,256]{1,0:T(8,128)}, f32[48,384]{1,0:T(8,128)}) custom-call(bf16[1024,768]{1,0:T(8,128)(2,1)} %get-tuple-element.63.gg, bf16[1024,1280]{1,0:T(8,128)(2,1)} %get-tuple-element.81.cat, bf16[1536,1792]{1,0:T(8,128)(2,1)} %bitcast.5, ...), custom_call_target="tpu_custom_call" | custom-call | tf_op jit(solution)/shard_map/tail/pallas_call | solution.py:1006
  165.1 5.1 %finish.1 = (f32[256,1536]{1,0:T(8,128)}, bf16[256,1536]{1,0:T(8,128)(2,1)}, f32[96,384]{1,0:T(8,128)}, f32[96,256]{1,0:T(8,128)}, f32[96,384]{1,0:T(8,128)}, /*...) custom-call(f32[256,1536]{1,0:T(8,128)} %get-tuple-element.87.grad, ...), custom_call_target="tpu_custom_call" | custom-call | tf_op jit(solution)/shard_map/finish/pallas_call | solution.py:1082

commit v7 on v6

--- a/solution.py
+++ b/solution.py
@@ -130,11 +130,13 @@
     def around(self, src, dst, axis):
         return [self.start(src, dst, axis, step) for step in (1, -1, 2)]
 
-    def barrier(self, peers):
-        here = pltpu.get_barrier_semaphore()
+    def greet(self, peers):
+        here, self.peers = pltpu.get_barrier_semaphore(), len(peers)
         for peer in peers:
             pl.semaphore_signal(here, inc=1, device_id=self.targets[peer], device_id_type=MESH)
-        pl.semaphore_wait(here, len(peers))
+
+    def met(self):
+        pl.semaphore_wait(pltpu.get_barrier_semaphore(), self.peers)
 
     def finish(self):
         for copy in self.copies:
@@ -325,6 +327,7 @@
     def _():
         load = pltpu.make_async_copy(x, xv, local.at[7])
         load.start()
+        net.greet([("z", 1), ("z", -1), ("z", 2), ("x", 1), ("x", -1), ("y", 1), ("y", -1), ("y", 2), ("c", 1)])
         own().start()
         stept[...] = jnp.zeros_like(stept)
         stept[0:HEADS, 0:96] = w_step[...].astype(F32)
@@ -336,7 +339,6 @@
         pk[6:7, 0:HEADS] = step_bias[...].reshape(1, HEADS)
         pk[7:8, 0:HEADS] = decay_log[...].reshape(1, HEADS)
         pk[8:9, 0:HEADS] = skip_gain[...].reshape(1, HEADS)
-        net.barrier([("z", 1), ("z", -1), ("z", 2), ("x", 1), ("x", -1), ("y", 1), ("y", -1), ("y", 2), ("c", 1)])
         first = {
             "x": ((w_gate, wx, 0, COLS), (w_bc.at[:, lanes(yh * 128, 128)], wbc, 0, 128)),
             "y": ((w_inner, wx, WIDE, COLS), (stepv, wx, STEPS, 128)),
@@ -356,18 +358,19 @@
                 return ref.at[lax.rem(place, 2), :, cc, cut, lanes(base + (place // 2) * n, n)]
             return ref.at[:, place, cc, cut, lanes(base, 2 * n)]
 
+        load.wait()
+        v = xv[...].astype(F32)
+        root = lax.rsqrt(jnp.mean(v * v, axis=1, keepdims=True) + EPS)
+        normed[pl.ds(pl.multiple_of(z * 256, 256), 256), :] = (v * root * gain[...].reshape(1, D)).astype(BF16)
+        net.met()
+        zs = {}
+        for p, s in order:
+            here = rows(normed, z * 256 + 128 * p, 128)
+            zs[p, s] = go(here, here, "z", s)
         sent = {"x": [], "y": []}
         for axis in ("x", "y"):
             for src, ref, base, n in first[axis]:
                 sent[axis].append([go(src, spot(ref, base, n, y, cx), axis, step) for _, step in HALVES])
-        load.wait()
-        v = xv[...].astype(F32)
-        root = lax.rsqrt(jnp.mean(v * v, axis=1, keepdims=True) + EPS)
-        normed[pl.ds(pl.multiple_of(z * 256, 256), 256), :] = (v * root * gain[...].reshape(1, D)).astype(BF16)
-        zs = {}
-        for p, s in order:
-            here = rows(normed, z * 256 + 128 * p, 128)
-            zs[p, s] = go(here, here, "z", s)
         mine = [
             pltpu.make_async_copy(src, spot(ref, base, n, y, cx), local.at[8 + k])
             for k, (src, ref, base, n) in enumerate(first["x"] + first["y"])
@@ -679,6 +682,12 @@
     )(*args)
 
 
+def later(v, after, step):
+    turned = pltpu.roll(v, BLOCK - step, 0)
+    ends = jnp.where(iota(after.shape, 0) < 8 - step, turned[BLOCK - 8 :, :], pltpu.roll(after, 8 - step, 0))
+    return jnp.concatenate([turned[: BLOCK - 8, :], ends], axis=0)
+
+
 def backward_kernel(
     gs_in, inner, zin, y, hin, prm, bc, dt, r, u, gains, mixed, wout, cot_t, gg, normed_t, tokens, zbc, bc_in, conv_bc,
     cat_out, acc, acc_bc, branch_out, wout_out, wgate_out,
@@ -693,16 +702,21 @@
 
     @pl.when(k == 0)
     def _():
+        net.greet([("z", 1), ("z", -1)] + [(a, s) for a in ("x", "y") for s in (1, -1, 2)] + [("c", 1)])
         loads = [pltpu.make_async_copy(src, dst, local.at[n]) for n, (src, dst) in enumerate(((mixed, mv), (wout, wv), (cot_t, cv), (gg, gv), (normed_t, nv)))]
         for copy in loads:
             copy.start()
-        net.barrier([("z", 1), ("z", -1)] + [(a, s) for a in ("x", "y") for s in (1, -1, 2)] + [("c", 1)])
         loads[0].wait()
         loads[1].wait()
         branch = lambda place: dot_nt(mv[pl.ds(pl.multiple_of(place * 256, 256), 256), :], wv[...])
         grads = lambda left, right, core: dot(left[core].reshape(8 * 96, LEN), right[...]).astype(BF16).reshape(2, 4, 96, WIDE)
         g0[...] = branch(net.near("z", 2)).astype(BF16)
+        net.met()
         token.step1()
+        for p, step in HALVES:
+            g2[p] = branch(net.near("z", step)).astype(BF16)
+            token.folded(p)
+        ownb[...] = branch(z)
         loads[2].wait()
         away[0] = grads(cv, mv, net.other)
         cross[0].start()
@@ -710,10 +724,6 @@
         loads[4].wait()
         away[1] = grads(nv, gv, net.other)
         cross[1].start()
-        for p, step in HALVES:
-            g2[p] = branch(net.near("z", step)).astype(BF16)
-            token.folded(p)
-        ownb[...] = branch(z)
         held[0] = grads(cv, mv, cc)
         held[1] = grads(nv, gv, cc)
         acc[...] = jnp.zeros_like(acc)
@@ -800,11 +810,11 @@
         dw = dwi + dws
         skipgrad = gs * xv
         diff = folded(gl.astype(F32) * (yv - skip * xv) - wl.astype(F32) * dwi, fold)
-        zsum = folded(w * dws, fold)
+        zsum = dot((w * dws).astype(BF16), fold)
         const = folded(jnp.sum(h * dh, axis=0, keepdims=True) * grow[BLOCK - 1 : BLOCK, :] + jnp.zeros((8, COLS), F32), fold)
         da = dot_right(suffix, diff, 3) + dot_right(prefix, zsum, 3) + const[0:1, :]
         rate = -jnp.exp(prm[g, 7:8, 0:128])
-        dstep = (folded(xv * dw, fold) + rate * da) * sigmoid(u[g])
+        dstep = (dot((xv * dw).astype(BF16), fold) + rate * da) * sigmoid(u[g])
         cat_out[:, WIDE + 128 * g : WIDE + 128 * (g + 1)] = dstep.astype(BF16)
         gx = (grow * gs).astype(BF16)
         dbc[:, STATE:] += dot_nt(gx, h.astype(BF16))
@@ -812,10 +822,11 @@
         dstate[:, cut] = grow[BLOCK - 1 : BLOCK, :] * dh + dot_tn(c, gx)
         dx = dte * dw + skip * gs
         dz = dx * (zs * (1.0 + zv * (1.0 - zs)))
-        ext[0:BLOCK, cut] = dz
+        after = ext[BLOCK : BLOCK + 8, cut]
+        ext[0:8, cut] = dz[0:8, :]
         gi = jnp.zeros((BLOCK, COLS), F32)
         for j in range(4):
-            moved = ext[3 - j : 3 - j + BLOCK, cut]
+            moved = dz if j == 3 else later(dz, after, 3 - j)
             gi = gi + prm[g, j : j + 1, :] * moved
             acc[g, j : j + 1, :] += jnp.sum(xi * moved, axis=0, keepdims=True)
         cat_out[:, cut] = gi.astype(BF16)
@@ -908,13 +919,15 @@
 def tail_kernel(
     gg, cat, wx, normed_t, normed, acc, acc_bc, wbc, gain,
     tokens_out, inner_out, bc_out, small_out,
-    ggv, catv, wxv, ntv, nv, wv, ownb, held, got, away, dbw, heldb, gotb, small, sp0, sp1, sp2, sp3, bz, by,
+    far_gg, far_cat, ggv, catv, wxv, ntv, nv, wv, ownb, held, got, away, dbw, heldb, gotb, small, sp0, sp1, sp2, sp3, bz, by,
     g0, g1, g2, g3, a1, a2, a3, b1, b2, b3, c1, c2, c3, send, recv, local,
 ):
     net = Net(send, recv)
     at = net.at
     yh, cx, cc, z, y = at["yh"], at["x"], at["c"], at["z"], at["y"]
-    pairs = ((cat, catv), (gg, ggv), (wx, wxv), (wbc, wv), (normed, nv), (normed_t, ntv))
+    net.greet([(a, s) for a in ("z", "x", "y") for s in (1, -1, 2)] + [("c", 1)])
+    far_rows = lambda ref: rows(ref, net.near("z", 2) * 256, 256)
+    pairs = ((far_rows(cat), far_cat), (far_rows(gg), far_gg), (wx, wxv), (wbc, wv), (cat, catv), (gg, ggv), (normed_t, ntv), (normed, nv))
     loads = [pltpu.make_async_copy(src, dst, local.at[i]) for i, (src, dst) in enumerate(pairs)]
     for copy in loads:
         copy.start()
@@ -922,11 +935,13 @@
     spans = ((0, COLS), (WIDE, 128))
     rings = (GridSum(net, "x", held, spans, (a1, a2, a3), (0, 48)), GridSum(net, "y", held, spans, (b1, b2, b3), (48, 48)))
     ring_bc = GridSum(net, "x", heldb, ((0, 128),), (c1, c2, c3))
-    net.barrier([(a, s) for a in ("z", "x", "y") for s in (1, -1, 2)] + [("c", 1)])
+
+    def product(gates, others):
+        return dot_nt(gates, wxv[:, 0:WIDE]) + dot_nt(others[:, 0:MORE], wxv[:, WIDE:]) + dot_nt(others[:, MORE:], wv[...])
 
     def block(place):
         cut = pl.ds(pl.multiple_of(place * 256, 256), 256)
-        return dot_nt(ggv[cut, :], wxv[:, 0:WIDE]) + dot_nt(catv[cut, 0:MORE], wxv[:, WIDE:]) + dot_nt(catv[cut, MORE:], wv[...])
+        return product(ggv[cut, :], catv[cut, :])
 
     def of_norm(place, grad):
         cut = pl.ds(pl.multiple_of(place * 256, 256), 256)
@@ -934,15 +949,26 @@
 
     for copy in loads[:4]:
         copy.wait()
-    far = block(net.near("z", 2))
+    far = product(far_gg[...], far_cat[...])
     g0[...] = far.astype(BF16)
+    net.met()
     token.step1()
-    loads[4].wait()
+    for copy in loads[4:7]:
+        copy.wait()
+    grads = lambda core, cut, n: dot(ntv[core].reshape(8 * 96, LEN), catv[:, cut]).astype(BF16).reshape(2, 4, 96, n)
+    for core in range(2):
+        dbw[core] = grads(core, slice(MORE, MORE + 256), 256)
+    crossb = net.start(dbw.at[net.other], gotb, "c")
+    loads[7].wait()
     norm_part = of_norm(net.near("z", 2), far)
     for p, step in HALVES:
         out = block(net.near("z", step))
         g2[p] = out.astype(BF16)
         norm_part = norm_part + of_norm(net.near("z", step), out)
+        if p == 0:
+            crossb.arrived()
+            heldb[...] = dbw[cc] + gotb[...]
+            ring_bc.step1()
     ownb[...] = block(z)
     norm_part = (norm_part + of_norm(z, ownb[...])) / gain[...].reshape(1, D)
     small[0:16, :] = acc[0]
@@ -955,38 +981,30 @@
     q = net.around(sp0.at[z], sp0.at[z], "z")
     for p, _ in HALVES:
         token.folded(p)
-    loads[5].wait()
-    grads = lambda core, cut, n: dot(ntv[core].reshape(8 * 96, LEN), catv[:, cut]).astype(BF16).reshape(2, 4, 96, n)
-    for core in range(2):
-        dbw[core] = grads(core, slice(MORE, MORE + 256), 256)
-    crossb = net.start(dbw.at[net.other], gotb, "c")
+    ring_bc.step2()
     away[...] = grads(net.other, slice(0, MORE), MORE)
     cross = net.start(away, got, "c")
-    crossb.arrived()
-    heldb[...] = dbw[cc] + gotb[...]
-    ring_bc.step1()
     held[...] = grads(cc, slice(0, MORE), MORE)
     cross.arrived()
     held[...] += got[...]
+    ring_bc.step3(by.at[yh])
+    qb = [net.start(by.at[yh], by.at[yh], "y", 2)]
     arrive(q)
     sp1[cx, 0:32, :] = small[0:32, :]
     sp1[cx, 32:48, :] = (sp0[0] + sp0[1]) + (sp0[2] + sp0[3])
     q = net.around(sp1.at[cx], sp1.at[cx], "x")
-    ring_bc.step2()
     for ring in rings:
         ring.step1()
     token.step2()
+    arrive(qb)
+    bz[z, :, 0:128] = by[0].astype(BF16)
+    bz[z, :, 128:256] = by[1].astype(BF16)
+    qb = net.around(bz.at[z], bz.at[z], "z")
     arrive(q)
     sp2[y] = (sp1[0] + sp1[1]) + (sp1[2] + sp1[3])
     q = net.around(sp2.at[y], sp2.at[y], "y")
-    ring_bc.step3(by.at[yh])
-    qb = [net.start(by.at[yh], by.at[yh], "y", 2)]
     for ring in rings:
         ring.step2()
-    arrive(qb)
-    bz[z, :, 0:128] = by[0]
-    bz[z, :, 128:256] = by[1]
-    qb = net.around(bz.at[z], bz.at[z], "z")
     arrive(q)
     sp3[cc] = (sp2[0] + sp2[1]) + (sp2[2] + sp2[3])
     q = [net.start(sp3.at[cc], sp3.at[cc], "c")]
@@ -996,7 +1014,7 @@
     small_out[...] = sp3[0] + sp3[1]
     tokens_out[...] = token.step3() + ownb[...]
     arrive(qb)
-    bc_out[...] = (bz[0] + bz[1]) + (bz[2] + bz[3])
+    bc_out[...] = (bz[0].astype(F32) + bz[1].astype(F32)) + (bz[2].astype(F32) + bz[3].astype(F32))
     net.finish()
 
 
@@ -1014,6 +1032,8 @@
         in_specs=[ANY] * 5 + [VMEM, VMEM, ANY, VMEM],
         out_specs=[VMEM] * 4,
         scratch_shapes=[
+            bf(256, WIDE),
+            bf(256, MORE + 256),
             bf(LEN, WIDE),
             bf(LEN, MORE + 256),
             bf(D, PROJ),
@@ -1032,7 +1052,7 @@
             f32(4, 48, COLS),
             f32(4, 48, COLS),
             f32(2, 48, COLS),
-            f32(4, 96, 256),
+            bf(4, 96, 256),
             f32(2, 96, 128),
         ]
         + token_scratch()
@@ -1040,7 +1060,7 @@
         + grid_scratch("y", COLS + 128, 48)
         + grid_scratch("x", 128)
         + sems(64)
-        + [pltpu.SemaphoreType.DMA((6,))],
+        + [pltpu.SemaphoreType.DMA((8,))],
         compiler_params=pltpu.CompilerParams(collective_id=3, has_side_effects=True, vmem_limit_bytes=ROOM),
         name="tail",
     )(*args)

time: 171 us -> 165 us (0.965)
  Pallas kernels: 170 us -> 163 us
    pallas_call x1, Pallas kernels: 47.3 us -> 42.8 us  [run_tail(): pl.pallas_call(tail_kernel, out_shape=[SHAPE((256, D), F32), SHAPE((96, C...]
    pallas_call x1, Pallas kernels: 43 us -> 41 us  [run_backward(): pl.pallas_call(backward_kernel, grid=(BLOCKS,), out_shape=[SHAPE((LEN, MO...]
where the time goes in v7:
time: 165 us; the launch traced here: 164 us
  Pallas kernels  163 us (99%)
    pallas_call x1, Pallas kernels, run_front(): pl.pallas_call(front_kernel, grid=(2 * BLOCKS,), out_shape=[wide, wide, w...  73.7 us
    pallas_call x1, Pallas kernels, run_tail(): pl.pallas_call(tail_kernel, out_shape=[SHAPE((256, D), F32), SHAPE((96, C...  42.8 us
    pallas_call x1, Pallas kernels, run_backward(): pl.pallas_call(backward_kernel, grid=(BLOCKS,), out_shape=[SHAPE((LEN, MO...  41 us
    pallas_call x1, Pallas kernels, run_finish(): pl.pallas_call(finish_kernel, grid=(4,), out_shape=[f32(256, D), SHAPE((2...  5.12 us

profile of v7, /device:TPU:0, one launch (start us, length us, event | category | flops | bytes accessed | tf_op | source)
XLA Modules:
  0.0 163.5 jit_solution(3281324906875670753)
XLA Ops:
  0.7 73.7 %front.1 = (f32[1024,768]{1,0:T(8,128)}, f32[1024,768]{1,0:T(8,128)}, f32[1024,768]{1,0:T(8,128)}, f32[4,2,128,384]{3,2,1,0:T(8,128)}, f32[2,1024,128]{2,1,0:T(8...) custom-call(bf16[256,1536]{1,0:T(8,128)(2,1)} %tokens.3, ...), custom_call_target="tpu_custom_call" | custom-call | tf_op jit(solution)/shard_map/front/pallas_call | solution.py:612
  74.4 41.0 %backward.1 = (bf16[1024,1280]{1,0:T(8,128)(2,1)}, f32[2,16,384]{2,1,0:T(8,128)}, f32[8,256]{1,0:T(8,128)}, bf16[256,1536]{1,0:T(8,128)(2,1)}, f32[96,384]{1,0:T(8,128)}, /*index=5*/f32[96,384]{1,0:T(8,128)}) custom-call(f32[1024,768]{1,0:T(8,128)} %get-tuple-element.64.gs_in, f32[1024,768]{1,0:T(8,128)} %get-tuple-element.65.inner, ...), custom_call_target="tpu_custom_call" | custom-call | tf_op jit(solution)/shard_map/backward/pallas_call | solution.py:869
  115.4 42.8 %tail.1 = (f32[256,1536]{1,0:T(8,128)}, f32[96,512]{1,0:T(8,128)}, f32[96,256]{1,0:T(8,128)}, f32[48,384]{1,0:T(8,128)}) custom-call(bf16[1024,768]{1,0:T(8,128)(2,1)} %get-tuple-element.63.gg, bf16[1024,1280]{1,0:T(8,128)(2,1)} %get-tuple-element.81.cat, bf16[1536,1792]{1,0:T(8,128)(2,1)} %bitcast.5, ...), custom_call_target="tpu_custom_call" | custom-call | tf_op jit(solution)/shard_map/tail/pallas_call | solution.py:1024
  158.2 5.1 %finish.1 = (f32[256,1536]{1,0:T(8,128)}, bf16[256,1536]{1,0:T(8,128)(2,1)}, f32[96,384]{1,0:T(8,128)}, f32[96,256]{1,0:T(8,128)}, f32[96,384]{1,0:T(8,128)}, /*...) custom-call(f32[256,1536]{1,0:T(8,128)} %get-tuple-element.87.grad, ...), custom_call_target="tpu_custom_call" | custom-call | tf_op jit(solution)/shard_map/finish/pallas_call | solution.py:1102
